TPU v7x, 32 devices: a whole 2x2x4 slice. The times are simulated.
32 devices in a mesh: dp: 8 (over z, x), seq: 4 (over y, core).
Axes of the slice: x: 2, y: 2, z: 4, core: 2. Of those that a mesh axis runs over, the one named last changes fastest.
Arguments:
- points: bfloat16 [8, 1024, 20], P('dp', 'seq'), may hold values from -4 to 4
- counts: int32 [8], P('dp'), may hold values from 5 to 20
- cotangent: bfloat16 [8, 1024, 256], P('dp', 'seq'), may hold values from -6 to 6
- weights: float32 [1585152], P('dp'), may hold values from -2 to 2
- momenta: float32 [1585152], P('dp'), may hold values from -320 to 320
- averages: float32 [1585152], P('dp'), may hold values from -2 to 2
Outputs:
- states: bfloat16 [8, 1024, 256], P('dp', 'seq')
- point_grad: float32 [8, 1024, 20], P('dp', 'seq')
- gradients: float32 [1585152], P('dp')
- weights_new: float32 [1585152], P('dp')
- momenta_new: float32 [1585152], P('dp')
- averages_new: float32 [1585152], P('dp')
All inputs are finite; a program needn't handle non-finite values.
Results may differ from a plain program's by a relative error of at most 0.014.
Values may be sent and summed in bfloat16 or wider, within the bound.
A program may use at most 192 MiB of HBM per device.

v0:
```python
import math

import jax
import jax.numpy as jnp
from jax import lax
from jax.sharding import PartitionSpec as P

HEADS = 8
FF = 1024
LAYERS = 2
LOOPS = 2


EPSILON = 1e-05
RATE = 0.0003
MOMENTUM = 0.5
AVERAGE_DECAY = 0.9


def split_flat(vector, model_width, hidden_width, input_width, layer_count):
    layouts = [(input_width, model_width), (model_width,)]
    for layer_index in range(layer_count):
        layouts = layouts + [
            (4, model_width),
            (model_width, 3 * model_width),
            (model_width, model_width),
            (model_width, hidden_width),
            (hidden_width,),
            (hidden_width, model_width),
        ]
    pieces = []
    offset = 0
    for dimensions in layouts:
        amount = math.prod(dimensions)
        pieces.append(vector[offset : offset + amount].reshape(dimensions))
        offset = offset + amount
    return pieces


def layer_norm(values, gain, bias):
    centred = values - jnp.mean(values, axis=-1, keepdims=True)
    variance = jnp.mean(centred * centred, axis=-1, keepdims=True)
    return centred * lax.rsqrt(variance + EPSILON) * gain + bias


def head_scores(queries, key_rows, causal, head_width):
    row_count = queries.shape[0]
    key_count = key_rows.shape[0]
    scores = jnp.einsum(
        "qhd,khd->hqk",
        queries.reshape(row_count, HEADS, head_width),
        key_rows.reshape(key_count, HEADS, head_width),
        preferred_element_type=jnp.float32,
    ) * (1.0 / math.sqrt(head_width))
    return jnp.where(causal[None], scores, -jnp.inf)


def layer_forward(hidden_state, layer_params, masks):
    causal = masks[0]
    norm_params, w_qkv, w_out, w_up, b_up, w_down = layer_params
    norm_values = norm_params.astype(jnp.float32)
    row_count, model_width = hidden_state.shape
    head_width = model_width // HEADS
    normed_low = layer_norm(hidden_state, norm_values[0], norm_values[1]).astype(jnp.bfloat16)
    projected = jnp.dot(normed_low, w_qkv, preferred_element_type=jnp.float32).astype(jnp.bfloat16)
    queries = projected[:, :model_width]
    key_rows = projected[:, model_width : 2 * model_width]
    value_rows = projected[:, 2 * model_width :]
    all_keys, all_values = (
        lax.all_gather(key_rows, "seq", axis=0, tiled=True),
        lax.all_gather(value_rows, "seq", axis=0, tiled=True),
    )
    scores = head_scores(queries, all_keys, causal, head_width)
    peak = jnp.max(scores, axis=-1, keepdims=True)
    exponent = jnp.exp(scores - peak)
    denominator = jnp.sum(exponent, axis=-1, keepdims=True)
    probabilities_low = (exponent / denominator).astype(jnp.bfloat16)
    log_total = peak + jnp.log(denominator)
    key_count = all_values.shape[0]
    attended = (
        jnp.einsum(
            "hqk,khd->qhd",
            probabilities_low,
            all_values.reshape(key_count, HEADS, head_width),
            preferred_element_type=jnp.float32,
        )
        .reshape(row_count, model_width)
        .astype(jnp.bfloat16)
    )
    updated = hidden_state + jnp.dot(attended, w_out, preferred_element_type=jnp.float32)
    second_low = layer_norm(updated, norm_values[2], norm_values[3]).astype(jnp.bfloat16)
    before_act = jnp.dot(second_low, w_up, preferred_element_type=jnp.float32) + b_up.astype(
        jnp.float32
    )
    activated = jax.nn.gelu(before_act).astype(jnp.bfloat16)
    output = updated + jnp.dot(activated, w_down, preferred_element_type=jnp.float32)
    saved = (
        hidden_state,
        normed_low,
        queries,
        all_keys,
        all_values,
        log_total,
        attended,
        updated,
        second_low,
        before_act,
        activated,
    )
    return (output, saved)


def layer_backward(grad_out, saved, layer_params, masks):
    causal, causal_back, first_row = masks
    (
        hidden_state,
        normed_low,
        queries,
        all_keys,
        all_values,
        log_total,
        attended,
        updated,
        second_low,
        before_act,
        activated,
    ) = saved
    norm_params, w_qkv, w_out, w_up, b_up, w_down = layer_params
    norm_values = norm_params.astype(jnp.float32)
    row_count, model_width = hidden_state.shape
    head_width = model_width // HEADS
    key_count = all_keys.shape[0]
    out_low = grad_out.astype(jnp.bfloat16)
    grad_w_down = jnp.einsum("tf,td->fd", activated, out_low, preferred_element_type=jnp.float32)
    grad_activated = jnp.dot(out_low, w_down.T, preferred_element_type=jnp.float32)
    act_values, gelu_pull = jax.vjp(jax.nn.gelu, before_act)
    pre_low = gelu_pull(grad_activated)[0].astype(jnp.bfloat16)
    grad_w_up = jnp.einsum("td,tf->df", second_low, pre_low, preferred_element_type=jnp.float32)
    grad_b_up = jnp.sum(pre_low.astype(jnp.float32), axis=0)
    grad_second = jnp.dot(pre_low, w_up.T, preferred_element_type=jnp.float32)
    norm_result, norm_pull = jax.vjp(layer_norm, updated, norm_values[2], norm_values[3])
    grad_through, grad_gain_two, grad_bias_two = norm_pull(grad_second)
    grad_updated = grad_out + grad_through
    branch_low = grad_updated.astype(jnp.bfloat16)
    grad_w_out = jnp.einsum("td,te->de", attended, branch_low, preferred_element_type=jnp.float32)
    grad_attended = jnp.dot(branch_low, w_out.T, preferred_element_type=jnp.float32).astype(
        jnp.bfloat16
    )
    scores = head_scores(queries, all_keys, causal, head_width)
    probabilities = jnp.exp(scores - log_total)
    probabilities_low = probabilities.astype(jnp.bfloat16)
    grad_heads = grad_attended.reshape(row_count, HEADS, head_width)
    query_heads = queries.reshape(row_count, HEADS, head_width)
    key_heads = all_keys.reshape(key_count, HEADS, head_width)
    value_heads = all_values.reshape(key_count, HEADS, head_width)
    grad_probabilities = jnp.einsum(
        "qhd,khd->hqk", grad_heads, value_heads, preferred_element_type=jnp.float32
    )
    inner = jnp.sum(probabilities * grad_probabilities, axis=-1, keepdims=True)
    grad_scores = (probabilities * (grad_probabilities - inner)).astype(jnp.bfloat16)
    score_scale = 1.0 / math.sqrt(head_width)
    grad_queries = (
        jnp.einsum(
            "hqk,khd->qhd", grad_scores, key_heads, preferred_element_type=jnp.float32
        ).reshape(row_count, model_width)
        * score_scale
    )
    grad_keys_all = (
        jnp.einsum(
            "hqk,qhd->khd", grad_scores, query_heads, preferred_element_type=jnp.float32
        ).reshape(key_count, model_width)
        * score_scale
    )
    grad_values_all = jnp.einsum(
        "hqk,qhd->khd", probabilities_low, grad_heads, preferred_element_type=jnp.float32
    ).reshape(key_count, model_width)
    grad_keys, grad_values = (
        lax.psum_scatter(
            grad_keys_all.astype(jnp.bfloat16), "seq", scatter_dimension=0, tiled=True
        ).astype(jnp.float32),
        lax.psum_scatter(
            grad_values_all.astype(jnp.bfloat16), "seq", scatter_dimension=0, tiled=True
        ).astype(jnp.float32),
    )
    projected_low = jnp.concatenate([grad_queries, grad_keys, grad_values], axis=1).astype(
        jnp.bfloat16
    )
    grad_w_qkv = jnp.einsum(
        "td,te->de", normed_low, projected_low, preferred_element_type=jnp.float32
    )
    grad_normed = jnp.dot(projected_low, w_qkv.T, preferred_element_type=jnp.float32)
    norm_first, first_pull = jax.vjp(layer_norm, hidden_state, norm_values[0], norm_values[1])
    grad_hidden, grad_gain_one, grad_bias_one = first_pull(grad_normed)
    grad_norms = jnp.stack([grad_gain_one, grad_bias_one, grad_gain_two, grad_bias_two])
    return (
        grad_updated + grad_hidden,
        (grad_norms, grad_w_qkv, grad_w_out, grad_w_up, grad_b_up, grad_w_down),
    )


def shards(points, counts, cotangent, weights, momenta, averages):
    row_count = points.shape[1]
    input_width = points.shape[2]
    model_width = cotangent.shape[2]
    hidden_width = FF
    length_all = row_count * lax.axis_size("seq")
    first_row = lax.axis_index("seq") * row_count
    query_positions = first_row + jnp.arange(row_count, dtype=jnp.int32)
    key_positions = jnp.arange(length_all, dtype=jnp.int32)
    causal = key_positions[None, :] <= query_positions[:, None]
    causal_back = query_positions[None, :] <= key_positions[:, None]
    masks = (causal, causal_back, first_row)
    column_mask = (jnp.arange(input_width, dtype=jnp.int32) < counts[0]).astype(jnp.float32)
    masked_low = (points[0].astype(jnp.float32) * column_mask).astype(jnp.bfloat16)
    flat_low = weights.astype(jnp.bfloat16)
    gathered = lax.all_gather(flat_low, "dp", axis=0, tiled=True)
    held_pieces = split_flat(gathered, model_width, hidden_width, input_width, LAYERS)
    kept = []
    hidden_state = jnp.zeros((row_count, model_width), jnp.float32)
    for loop_index in range(LOOPS):
        pieces = held_pieces
        if loop_index == 0:
            embedding = jnp.dot(masked_low, pieces[0], preferred_element_type=jnp.float32) + pieces[
                1
            ].astype(jnp.float32)
        hidden_state = hidden_state + embedding
        for layer_index in range(LAYERS):
            hidden_state, saved = layer_forward(
                hidden_state, pieces[2 + 6 * layer_index : 8 + 6 * layer_index], masks
            )
            kept.append(saved)
    states = hidden_state.astype(jnp.bfloat16)[None]
    layer_sums = [
        tuple(
            (
                jnp.zeros(piece.shape, jnp.float32)
                for piece in pieces[2 + 6 * layer_index : 8 + 6 * layer_index]
            )
        )
        for layer_index in range(LAYERS)
    ]
    grad_state = cotangent[0].astype(jnp.float32)
    grad_embedding = jnp.zeros((row_count, model_width), jnp.float32)
    for loop_index in reversed(range(LOOPS)):
        pieces = held_pieces
        for layer_index in reversed(range(LAYERS)):
            grad_state, layer_grads = layer_backward(
                grad_state,
                kept[loop_index * LAYERS + layer_index],
                pieces[2 + 6 * layer_index : 8 + 6 * layer_index],
                masks,
            )
            layer_sums[layer_index] = jax.tree.map(jnp.add, layer_sums[layer_index], layer_grads)
        grad_embedding = grad_embedding + grad_state
    embed_low = grad_embedding.astype(jnp.bfloat16)
    grad_read_in = jnp.einsum(
        "ti,td->id", masked_low, embed_low, preferred_element_type=jnp.float32
    )
    grad_read_bias = jnp.sum(embed_low.astype(jnp.float32), axis=0)
    point_grad = (
        jnp.dot(embed_low, pieces[0].T, preferred_element_type=jnp.float32) * column_mask
    )[None]
    flat_parts = [grad_read_in.reshape(-1), grad_read_bias]
    for layer_index in range(LAYERS):
        flat_parts = flat_parts + [member.reshape(-1) for member in layer_sums[layer_index]]
    used_grads = jnp.concatenate(flat_parts)
    total_length = weights.shape[0] * lax.axis_size("dp")
    flat_grad = jnp.pad(used_grads, (0, total_length - used_grads.shape[0]))
    owner_share = lax.psum_scatter(flat_grad, "dp", scatter_dimension=0, tiled=True)
    gradients = lax.psum(owner_share.astype(jnp.bfloat16), "seq").astype(jnp.float32)
    momenta_new = MOMENTUM * momenta + gradients
    weights_new = weights - RATE * (gradients + MOMENTUM * momenta_new)
    averages_new = AVERAGE_DECAY * averages + (1.0 - AVERAGE_DECAY) * weights_new
    return (states, point_grad, gradients, weights_new, momenta_new, averages_new)


def solution(mesh):
    placed = (P("dp", "seq", None), P("dp"), P("dp", "seq", None), P("dp"), P("dp"), P("dp"))
    return jax.shard_map(
        shards,
        mesh=mesh,
        in_specs=placed,
        out_specs=(P("dp", "seq", None), P("dp", "seq", None), P("dp"), P("dp"), P("dp"), P("dp")),
        check_vma=False,
    )
```

profile of v0, /device:TPU:0, one launch (start us, length us, event | category | flops | bytes accessed | tf_op | source)
XLA Modules:
  0.0 897.1 jit_solution(5917076368743523003)
XLA Ops:
  18.4 97.7 %all-gather.3.cloned.1.call-done = bf16[8,1,198144]{2,1,0:T(2,128)(2,1)} async-done(((bf16[1,1,198144]{2,1,0:T(2,128)(2,1)}), bf16[8,1,198144]{2,1,0:T(2,128)(2,1)}) %all-gather.3.cloned.1.call-update) | async-done | bytes 3170320 | tf_op jit(solution)/shard_map/all_gather | solution.py:216
  116.2 18.6 %reduce = bf16[8,198144]{1,0:T(8,128)(2,1)S(1)} reduce(bf16[8,1,198144]{2,1,0:T(2,128)(2,1)} %all-gather.3.cloned.1.call-done, bf16[]{:T(256)} %constant.85), dimensions={1}, to_apply=%all-gather.reduce_sub_computation | reduce | bytes 6340610 | tf_op jit(solution)/shard_map/all_gather | solution.py:216
  152.4 7.2 all_gather.28
  159.9 7.5 all_gather.29
  181.9 7.7 all_gather.30
  192.7 8.2 all_gather.31
  216.0 7.3 all_gather.32
  225.3 8.6 all_gather.33
  244.5 7.9 all_gather.34
  255.5 7.7 all_gather.35
  287.6 6.5 multiply_reduce_fusion.3
  295.8 7.0 multiply_convert_fusion.3
  317.1 23.3 %reduce-scatter.9.cloned.1.call-done = bf16[256,256]{0,1:T(8,128)(2,1)} async-done(((bf16[1024,256]{0,1:T(8,128)(2,1)}), bf16[256,256]{0,1:T(8,128)(2,1)}) %reduce-scatter.9.cloned.1.call-update) | async-done | bytes 131088 | tf_op jit(solution)/shard_map/reduce_scatter | solution.py:178
  365.8 6.5 multiply_reduce_fusion.2
  372.3 6.9 multiply_convert_fusion.2
  396.5 22.3 %reduce-scatter.13.cloned.1.call-done = bf16[256,256]{0,1:T(8,128)(2,1)} async-done(((bf16[1024,256]{0,1:T(8,128)(2,1)}), bf16[256,256]{0,1:T(8,128)(2,1)}) %reduce-scatter.13.cloned.1.call-update) | async-done | bytes 131088 | tf_op jit(solution)/shard_map/reduce_scatter | solution.py:178
  438.0 6.7 multiply_reduce_fusion.1
  444.8 6.9 multiply_convert_fusion.1
  468.0 23.4 %reduce-scatter.17.cloned.1.call-done = bf16[256,256]{0,1:T(8,128)(2,1)} async-done(((bf16[1024,256]{0,1:T(8,128)(2,1)}), bf16[256,256]{0,1:T(8,128)(2,1)}) %reduce-scatter.17.cloned.1.call-update) | async-done | bytes 131088 | tf_op jit(solution)/shard_map/reduce_scatter | solution.py:178
  510.6 6.5 multiply_reduce_fusion
  519.7 7.1 multiply_convert_fusion
  545.7 17.6 %reduce-scatter.21.cloned.1.call-done = bf16[256,256]{0,1:T(8,128)(2,1)} async-done(((bf16[1024,256]{0,1:T(8,128)(2,1)}), bf16[256,256]{0,1:T(8,128)(2,1)}) %reduce-scatter.21.cloned.1.call-update) | async-done | bytes 131088 | tf_op jit(solution)/shard_map/reduce_scatter | solution.py:178
  606.1 249.6 %all-reduce.6 = bf16[1585152]{0:T(1024)(128)(2,1)} all-reduce(f32[1585152]{0:T(1024)} %pad.4), channel_id=10, replica_groups=mesh['dp'=8,'seq'=4] {'dp'}, use_global_device_ids=true, to_apply=%region_73.74.clone | all-reduce | flops 1585152 | bytes 9510912
  860.9 26.1 %all-reduce.5.cloned.1.call-done = bf16[198144]{0:T(1024)(128)(2,1)} async-done(((bf16[198144]{0:T(1024)(128)(2,1)}), bf16[198144]{0:T(1024)(128)(2,1)}) %all-reduce.5.cloned.1.call-update) | async-done | bytes 396304 | tf_op jit(solution)/shard_map/psum | solution.py:270
  (549 shorter events, 284.2 us)
Async XLA Ops:
  7.2 109.0 %all-gather.3.cloned.1.call-start = ((), (), s32[]{:S(2)}) async-start(), calls=%async_computation.17 | async-start | bytes 7133184 | tf_op jit(solution)/shard_map/all_gather | solution.py:216
  13.7 303.4 %reduce-scatter.11.cloned.1.call-start = ((), (), s32[]{:S(2)}) async-start(), calls=%async_computation.9 | async-start | bytes 655360 | tf_op jit(solution)/shard_map/reduce_scatter | solution.py:181
  18.2 132.2 %copy-start.149 = (f32[20]{0:T(128)}, f32[20]{0:T(128)S(1)}, u32[]{:S(2)}) copy-start(f32[20]{0:T(128)S(1)} %compare_convert_fusion) | copy-start | bytes 244
  151.9 62.9 %copy-start.89 = (f32[256]{0:T(256)}, f32[256]{0:T(256)S(1)}, u32[]{:S(2)}) copy-start(f32[256]{0:T(256)S(1)} %get-tuple-element.142) | copy-start | bytes 3076
  151.9 63.0 %copy-start.134 = (f32[256]{0:T(256)}, f32[256]{0:T(256)S(1)}, u32[]{:S(2)}) copy-start(f32[256]{0:T(256)S(1)} %get-tuple-element.143) | copy-start | bytes 3076
  151.9 89.4 %copy-start.96 = (f32[256]{0:T(256)}, f32[256]{0:T(256)S(1)}, u32[]{:S(2)}) copy-start(f32[256]{0:T(256)S(1)} %get-tuple-element.145) | copy-start | bytes 3076
  151.9 89.4 %copy-start.122 = (f32[256]{0:T(256)}, f32[256]{0:T(256)S(1)}, u32[]{:S(2)}) copy-start(f32[256]{0:T(256)S(1)} %get-tuple-element.144) | copy-start | bytes 3076
  151.9 90.8 %copy-start.92 = (f32[256]{0:T(256)}, f32[256]{0:T(256)S(1)}, u32[]{:S(2)}) copy-start(f32[256]{0:T(256)S(1)} %get-tuple-element.81) | copy-start | bytes 3076
  151.9 128.0 %copy-start.98 = (f32[256]{0:T(256)}, f32[256]{0:T(256)S(1)}, u32[]{:S(2)}) copy-start(f32[256]{0:T(256)S(1)} %get-tuple-element.78) | copy-start | bytes 3076
  295.7 44.7 %reduce-scatter.9.cloned.1.call-start = ((), (), s32[]{:S(2)}) async-start(), calls=%async_computation.8 | async-start | bytes 655360 | tf_op jit(solution)/shard_map/reduce_scatter | solution.py:178
  306.4 90.1 %reduce-scatter.15.cloned.1.call-start = ((), (), s32[]{:S(2)}) async-start(), calls=%async_computation.11 | async-start | bytes 655360 | tf_op jit(solution)/shard_map/reduce_scatter | solution.py:181
  372.2 46.5 %reduce-scatter.13.cloned.1.call-start = ((), (), s32[]{:S(2)}) async-start(), calls=%async_computation.10 | async-start | bytes 655360 | tf_op jit(solution)/shard_map/reduce_scatter | solution.py:178
  381.1 37.7 %copy-start.24 = (bf16[256,768]{1,0:T(8,128)(2,1)S(1)}, bf16[256,768]{1,0:T(8,128)(2,1)}, u32[]{:S(2)}) copy-start(bf16[256,768]{1,0:T(8,128)(2,1)} %copy-done.22) | copy-start | bytes 1179652
  382.8 85.2 %reduce-scatter.19.cloned.1.call-start = ((), (), s32[]{:S(2)}) async-start(), calls=%async_computation.13 | async-start | bytes 655360 | tf_op jit(solution)/shard_map/reduce_scatter | solution.py:181
  444.8 46.7 %reduce-scatter.17.cloned.1.call-start = ((), (), s32[]{:S(2)}) async-start(), calls=%async_computation.12 | async-start | bytes 655360 | tf_op jit(solution)/shard_map/reduce_scatter | solution.py:178
  455.3 90.3 %reduce-scatter.23.cloned.1.call-start = ((), (), s32[]{:S(2)}) async-start(), calls=%async_computation.15 | async-start | bytes 655360 | tf_op jit(solution)/shard_map/reduce_scatter | solution.py:181
  517.2 46.1 %reduce-scatter.21.cloned.1.call-start = ((), (), s32[]{:S(2)}) async-start(), calls=%async_computation.14 | async-start | bytes 655360 | tf_op jit(solution)/shard_map/reduce_scatter | solution.py:178
  530.4 356.6 %all-reduce.5.cloned.1.call-start = ((), (), s32[]{:S(2)}) async-start(), calls=%async_computation.16 | async-start | bytes 794624 | tf_op jit(solution)/shard_map/psum | solution.py:270
  545.6 44.1 %copy-start.135 = (f32[1,2,4,128]{3,1,2,0:T(2,128)S(1)}, f32[1,2,4,128]{3,1,2,0:T(2,128)}, u32[]{:S(2)}) copy-start(f32[1,2,4,128]{3,1,2,0:T(2,128)} %copy.125) | copy-start | bytes 12292
  606.0 251.6 %copy-start.68 = (f32[256,1024]{1,0:T(8,128)S(1)}, f32[256,1024]{1,0:T(8,128)}, u32[]{:S(2)}) copy-start(f32[256,1024]{1,0:T(8,128)} %copy-done.67) | copy-start | bytes 3145732
  606.0 254.1 %copy-start.95 = (bf16[20,256]{1,0:T(8,128)(2,1)S(1)}, bf16[20,256]{1,0:T(8,128)(2,1)}, u32[]{:S(2)}) copy-start(bf16[20,256]{1,0:T(8,128)(2,1)} %copy-done.94) | copy-start | bytes 30724
  606.0 254.1 %copy-start.150 = (f32[20]{0:T(128)S(1)}, f32[20]{0:T(128)}, u32[]{:S(2)}) copy-start(f32[20]{0:T(128)} %copy-done.149) | copy-start | bytes 244
  606.1 281.0 %copy-start.36 = (f32[198144]{0:T(1024)S(1)}, f32[198144]{0:T(1024)}, u32[]{:S(2)}) copy-start(f32[198144]{0:T(1024)} %param.9) | copy-start | bytes 2377732
  606.1 280.9 %copy-start.72 = (f32[198144]{0:T(1024)S(1)}, f32[198144]{0:T(1024)}, u32[]{:S(2)}) copy-start(f32[198144]{0:T(1024)} %param.11) | copy-start | bytes 2377732
  (137 other events, 1604.3 us)
Sparse Core Ops, SparseCore 0:
  13.8 102.3 all-gather.2
  295.9 19.5 reduce-scatter.10
  318.7 21.6 reduce-scatter.8
  372.4 21.6 reduce-scatter.14
  397.1 21.6 reduce-scatter.12
  444.9 21.6 reduce-scatter.18
  469.8 21.6 reduce-scatter.16
  517.3 21.6 reduce-scatter.22
  541.6 21.6 reduce-scatter.20
  857.8 29.1 all-reduce.4
where the time goes:
time: 903 us; the launch traced here: 897 us
  blocking collectives  312 us (35%)
  waiting for transfers between devices  211 us (23%)
  matrix products  155 us (17%)
  local copies, waits for them, and re-layouts  106 us (12%)
  other arithmetic  93.6 us (10%)
  between operations  18 us (2%)
    unnamed x1, blocking collectives  250 us
    all_gather x1, waiting for transfers between devices, shards(): gathered = lax.all_gather(flat_low, 'dp', axis=0, tiled=True)  97.7 us
    reduce_scatter x4, waiting for transfers between devices, layer_backward(): lax.psum_scatter(grad_keys_all.astype(jnp.bfloat16), 'seq', scatter_dimen...  86.7 us
    unnamed x328, local copies, waits for them, and re-layouts  60 us
    all_gather x4, blocking collectives, layer_forward(): lax.all_gather(key_rows, 'seq', axis=0, tiled=True)  32.1 us
    all_gather x4, blocking collectives, layer_forward(): lax.all_gather(value_rows, 'seq', axis=0, tiled=True)  30.1 us
    convert_element_type x4, other arithmetic, layer_backward(): (probabilities * (grad_probabilities - inner)).astype(jnp.bfloat16)  27.9 us
    dot_general x4, matrix products, layer_backward(): jnp.einsum('qhd,khd->hqk', grad_heads, value_heads, preferred_element_typ...  26.2 us
  transfers between devices with their start and end apart: 10, of which 6 were waited for; matrix products, arithmetic and copies ran while one was open for 10% of the time, Pallas kernels for 0%

commit v1 on v0

v1 whole, which is shorter than its diff:
```python
import functools
import math

import jax
import jax.numpy as jnp
from jax import lax
from jax.experimental import pallas as pl
from jax.experimental.pallas import tpu as pltpu
from jax.sharding import PartitionSpec as P

MESH = pl.DeviceIdType.MESH
HEADS = 8
FF = 1024
LAYERS = 2
LOOPS = 2
APPS = LAYERS * LOOPS

EPSILON = 1e-05
RATE = 0.0003
MOMENTUM = 0.5
AVERAGE_DECAY = 0.9

F32 = jnp.float32
BF16 = jnp.bfloat16
DEPTH_PAD = 32
GELU_A = math.sqrt(2.0 / math.pi)
GELU_B = 0.044715


def mm(left, right):
    return jnp.dot(left, right, preferred_element_type=F32)


def mm_nt(left, right):
    return lax.dot_general(left, right, (((1,), (1,)), ((), ())), preferred_element_type=F32)


def twice(column):
    return jnp.concatenate([column, column], axis=1)


def halves(values):
    return values[:, :128] + values[:, 128:]


def normalise(values):
    centred = values - jnp.mean(values, axis=0, keepdims=True)
    variance = jnp.mean(centred * centred, axis=0, keepdims=True)
    scale = lax.rsqrt(variance + EPSILON)
    return centred * scale, scale


def normalise_back(grad, unit, scale, gain):
    scaled = grad * gain
    first = jnp.mean(scaled, axis=0, keepdims=True)
    second = jnp.mean(scaled * unit, axis=0, keepdims=True)
    return (scaled - first - unit * second) * scale


def block_kernel(
    seq_count,
    masked_t, rit, rin, rbias, norms, bup, wqkv_t, wqkv, wo_t, wo, wup_t, wup, wd_t, wd, cot,
    states, pg_t, gri, grb, gnorm, gwqkv, gwo, gwup, gbup, gwd,
    hid, nrm, qsave, kv, kvt, att, osave, lse, upd, nrm2, gp, act, emb,
    qmask, qtok, domask, dotok, ps, ds, peak, total, mixed, dq, gbuf, gemb, gin, gsend, grecv,
    send_n, recv_n, send_g, recv_g,
):
    me = lax.axis_index("seq")
    width = hid.shape[1]
    rows = hid.shape[2]
    head_width = width // HEADS
    exp_scale = math.log2(math.e) / math.sqrt(head_width)
    score_scale = 1.0 / math.sqrt(head_width)

    barrier = pltpu.get_barrier_semaphore()
    for step in range(1, seq_count):
        pl.semaphore_signal(
            barrier, inc=1, device_id={"seq": lax.rem(me + step, seq_count)}, device_id_type=MESH
        )

    qmask[...] = jnp.zeros_like(qmask)
    domask[...] = jnp.zeros_like(domask)
    for ref in (gnorm, gwqkv, gwo, gwup, gbup, gwd):
        ref[...] = jnp.zeros_like(ref)
    ones = jnp.ones((16, rows), BF16)
    column_head = lax.broadcasted_iota(jnp.int32, (rows, width), 1) // head_width

    embedded = mm(rit[...], masked_t[...]) + twice(rbias[...])
    emb[...] = embedded
    hid[0] = embedded
    pl.semaphore_wait(barrier, seq_count - 1)

    def normed_copy(app, source, target):
        return pltpu.make_async_remote_copy(
            src_ref=nrm.at[app, source],
            dst_ref=nrm.at[app, source],
            send_sem=send_n.at[app, target],
            recv_sem=recv_n.at[app, source],
            device_id={"seq": target},
            device_id_type=MESH,
        )

    def grad_copy(app, source, target):
        return pltpu.make_async_remote_copy(
            src_ref=gsend.at[app, target],
            dst_ref=grecv.at[app, source],
            send_sem=send_g.at[app, target],
            recv_sem=recv_g.at[app, source],
            device_id={"seq": target},
            device_id_type=MESH,
        )

    causal = lax.broadcasted_iota(jnp.int32, (rows, rows), 0) <= lax.broadcasted_iota(
        jnp.int32, (rows, rows), 1
    )

    def project_block(app, layer, block):
        block_t = nrm[app, block]
        kvt[app, block] = mm(wqkv_t[layer, width:], block_t).astype(BF16)
        kv[app, block] = mm(
            jnp.transpose(block_t.astype(F32)).astype(BF16), wqkv[layer, :, width:]
        ).astype(BF16)

    def attend_block(app, block, diagonal):
        for head in range(HEADS):
            lanes = slice(head * head_width, (head + 1) * head_width)
            scores = mm(kv[app, block, :, :width], qmask[head]) * exp_scale
            if diagonal:
                scores = jnp.where(causal, scores, -jnp.inf)
                top = jnp.max(scores, axis=0, keepdims=True)
                weight = jnp.exp2(scores - top)
                total[head : head + 1] = jnp.sum(weight, axis=0, keepdims=True)
                mixed[lanes] = mm(
                    kvt[app, block, width + head * head_width : width + (head + 1) * head_width],
                    weight.astype(BF16),
                )
            else:
                old = peak[head : head + 1]
                top = jnp.maximum(old, jnp.max(scores, axis=0, keepdims=True))
                fade = jnp.exp2(old - top)
                weight = jnp.exp2(scores - top)
                total[head : head + 1] = total[head : head + 1] * fade + jnp.sum(
                    weight, axis=0, keepdims=True
                )
                mixed[lanes] = mixed[lanes] * fade + mm(
                    kvt[app, block, width + head * head_width : width + (head + 1) * head_width],
                    weight.astype(BF16),
                )
            peak[head : head + 1] = top

    def forward(app, carry):
        layer = lax.rem(app, LAYERS)
        unit, _ = normalise(hid[app])
        normed = (unit * twice(norms[layer, 0]) + twice(norms[layer, 1])).astype(BF16)
        nrm[app, me] = normed
        for step in range(1, seq_count):

            @pl.when(me + step < seq_count)
            def _():
                normed_copy(app, me, me + step).start()

        queries = mm(wqkv_t[layer, :width], normed).astype(BF16)
        qsave[app] = queries
        for head in range(HEADS):
            lanes = slice(head * head_width, (head + 1) * head_width)
            qmask[head, lanes] = queries[lanes]
        project_block(app, layer, me)
        attend_block(app, me, True)

        def earlier(step, inner):
            block = me - 1 - step
            normed_copy(app, block, me).wait_recv()
            project_block(app, layer, block)
            attend_block(app, block, False)
            return inner

        lax.fori_loop(0, me, earlier, 0)
        for head in range(HEADS):
            lanes = slice(head * head_width, (head + 1) * head_width)
            out = mixed[lanes] * (1.0 / total[head : head + 1])
            osave[app, lanes] = out
            att[app, lanes] = out.astype(BF16)
        lse[app] = peak[...] + jnp.log2(total[...])
        updated = hid[app] + mm(wo_t[layer], att[app])
        upd[app] = updated
        unit, _ = normalise(updated)
        second = (unit * twice(norms[layer, 2]) + twice(norms[layer, 3])).astype(BF16)
        nrm2[app] = second
        before = mm(wup_t[layer], second) + twice(bup[layer])
        squared = before * before
        inner = GELU_A * before * (1.0 + GELU_B * squared)
        turned = jnp.tanh(inner)
        half = 0.5 * (1.0 + turned)
        activated = (before * half).astype(BF16)
        act[app] = activated
        gp[app] = half + (0.5 * GELU_A) * before * (1.0 - turned * turned) * (
            1.0 + (3.0 * GELU_B) * squared
        )
        result = upd[app] + mm(wd_t[layer], act[app])
        again = jnp.where((layer == LAYERS - 1) & (app < APPS - 1), 1.0, 0.0)
        hid[app + 1] = result + again * emb[...]
        return carry

    lax.fori_loop(0, APPS, forward, 0)
    states[...] = jnp.transpose(hid[APPS]).astype(BF16)

    gbuf[...] = jnp.transpose(cot[...].astype(F32))
    gemb[...] = jnp.zeros_like(gemb)

    def attend_back(app, layer, block, diagonal):
        keys = kv[app, block, :, :width]
        values = kv[app, block, :, width:]
        for head in range(HEADS):
            lanes = slice(head * head_width, (head + 1) * head_width)
            wide = slice(head * rows, (head + 1) * rows)
            scores = mm(keys, qmask[head]) * exp_scale
            weight = jnp.exp2(scores - lse[app, head : head + 1])
            if diagonal:
                weight = jnp.where(causal, weight, 0.0)
            ps[:, wide] = weight.astype(BF16)
            grad = mm(values, domask[head])
            back = (weight * (grad - total[head : head + 1])).astype(BF16)
            ds[:, wide] = back
            part = mm(kvt[app, block, lanes], back)
            dq[lanes] = dq[lanes] + part
        grad_keys = (mm(ds[...], qtok[...]) * score_scale).astype(BF16)
        grad_values = mm(ps[...], dotok[...]).astype(BF16)
        block_t = nrm[app, block]
        gwqkv[layer, :, width : 2 * width] += mm(block_t, grad_keys)
        gwqkv[layer, :, 2 * width :] += mm(block_t, grad_values)
        return mm_nt(wqkv[layer, :, width : 2 * width], grad_keys) + mm_nt(
            wqkv[layer, :, 2 * width :], grad_values
        )

    def backward(order, carry):
        app = APPS - 1 - order
        layer = lax.rem(app, LAYERS)
        grad_out = gbuf[...]
        out_low = grad_out.astype(BF16)
        gwd[layer] += mm_nt(act[app], out_low)
        pre_low = (mm(wd[layer], out_low) * gp[app]).astype(BF16)
        act[app] = pre_low
        gwup[layer] += mm_nt(nrm2[app], act[app])
        gbup[layer] += mm_nt(ones, act[app])[:8]
        grad_second = mm(wup[layer], act[app])
        unit, scale = normalise(upd[app])
        gnorm[layer, 2] += halves(grad_second * unit)
        gnorm[layer, 3] += halves(grad_second)
        grad_updated = gbuf[...] + normalise_back(grad_second, unit, scale, twice(norms[layer, 2]))
        gbuf[...] = grad_updated
        branch_low = grad_updated.astype(BF16)
        gwo[layer] += mm_nt(att[app], branch_low)
        grad_att = mm(wo[layer], branch_low).astype(BF16)
        for head in range(HEADS):
            lanes = slice(head * head_width, (head + 1) * head_width)
            domask[head, lanes] = grad_att[lanes]
            qmask[head, lanes] = qsave[app, lanes]
            total[head : head + 1] = jnp.sum(
                osave[app, lanes] * grad_att[lanes].astype(F32), axis=0, keepdims=True
            )
        grad_tok = jnp.transpose(grad_att.astype(F32))
        query_tok = jnp.transpose(qsave[app].astype(F32))
        for head in range(HEADS):
            wide = slice(head * rows, (head + 1) * rows)
            dotok[wide] = jnp.where(column_head == head, grad_tok, 0.0).astype(BF16)
            qtok[wide] = jnp.where(column_head == head, query_tok, 0.0).astype(BF16)
        dq[...] = jnp.zeros_like(dq)

        def earlier(block, inner):
            gsend[app, block] = attend_back(app, layer, block, False).astype(BF16)
            grad_copy(app, me, block).start()
            return inner

        lax.fori_loop(0, me, earlier, 0)
        gin[...] = attend_back(app, layer, me, True)
        grad_queries = (dq[...] * score_scale).astype(BF16)
        gwqkv[layer, :, :width] += mm_nt(nrm[app, me], grad_queries)
        gin[...] += mm(wqkv[layer, :, :width], grad_queries)

        def later(source, inner):
            grad_copy(app, source, me).wait_recv()
            gin[...] += grecv[app, source].astype(F32)
            return inner

        lax.fori_loop(me + 1, seq_count, later, 0)
        grad_normed = gin[...]
        unit, scale = normalise(hid[app])
        gnorm[layer, 0] += halves(grad_normed * unit)
        gnorm[layer, 1] += halves(grad_normed)
        grad_in = gbuf[...] + normalise_back(grad_normed, unit, scale, twice(norms[layer, 0]))
        gbuf[...] = grad_in
        first = jnp.where(layer == 0, 1.0, 0.0)
        gemb[...] += first * grad_in
        return carry

    lax.fori_loop(0, APPS, backward, 0)
    embed_low = gemb[...].astype(BF16)
    gri[...] = mm_nt(masked_t[...], embed_low)
    grb[...] = mm_nt(ones, embed_low)[:8]
    pg_t[...] = mm(rin[...], embed_low)

    def finish(app, carry):
        def sent_normed(target, inner):
            normed_copy(app, me, target).wait_send()
            return inner

        def sent_grad(target, inner):
            grad_copy(app, me, target).wait_send()
            return inner

        lax.fori_loop(me + 1, seq_count, sent_normed, 0)
        lax.fori_loop(0, me, sent_grad, 0)
        return carry

    lax.fori_loop(0, APPS, finish, 0)


def run_block(seq_count, rows, width, hidden, operands):
    vmem = pl.BlockSpec(memory_space=pltpu.VMEM)
    shape = jax.ShapeDtypeStruct
    outs = (
        shape((rows, width), BF16),
        shape((DEPTH_PAD, rows), F32),
        shape((DEPTH_PAD, width), F32),
        shape((8, width), F32),
        shape((LAYERS, 4, width, 128), F32),
        shape((LAYERS, width, 3 * width), F32),
        shape((LAYERS, width, width), F32),
        shape((LAYERS, width, hidden), F32),
        shape((LAYERS, 8, hidden), F32),
        shape((LAYERS, hidden, width), F32),
    )
    scratch = [
        pltpu.VMEM((APPS + 1, width, rows), F32),
        pltpu.VMEM((APPS, seq_count, width, rows), BF16),
        pltpu.VMEM((APPS, width, rows), BF16),
        pltpu.VMEM((APPS, seq_count, rows, 2 * width), BF16),
        pltpu.VMEM((APPS, seq_count, 2 * width, rows), BF16),
        pltpu.VMEM((APPS, width, rows), BF16),
        pltpu.VMEM((APPS, width, rows), F32),
        pltpu.VMEM((APPS, HEADS, rows), F32),
        pltpu.VMEM((APPS, width, rows), F32),
        pltpu.VMEM((APPS, width, rows), BF16),
        pltpu.VMEM((APPS, hidden, rows), F32),
        pltpu.VMEM((APPS, hidden, rows), BF16),
        pltpu.VMEM((width, rows), F32),
        pltpu.VMEM((HEADS, width, rows), BF16),
        pltpu.VMEM((HEADS * rows, width), BF16),
        pltpu.VMEM((HEADS, width, rows), BF16),
        pltpu.VMEM((HEADS * rows, width), BF16),
        pltpu.VMEM((rows, HEADS * rows), BF16),
        pltpu.VMEM((rows, HEADS * rows), BF16),
        pltpu.VMEM((HEADS, rows), F32),
        pltpu.VMEM((HEADS, rows), F32),
        pltpu.VMEM((width, rows), F32),
        pltpu.VMEM((width, rows), F32),
        pltpu.VMEM((width, rows), F32),
        pltpu.VMEM((width, rows), F32),
        pltpu.VMEM((width, rows), F32),
        pltpu.VMEM((APPS, seq_count, width, rows), BF16),
        pltpu.VMEM((APPS, seq_count, width, rows), BF16),
        pltpu.SemaphoreType.DMA((APPS, seq_count)),
        pltpu.SemaphoreType.DMA((APPS, seq_count)),
        pltpu.SemaphoreType.DMA((APPS, seq_count)),
        pltpu.SemaphoreType.DMA((APPS, seq_count)),
    ]
    return pl.pallas_call(
        functools.partial(block_kernel, seq_count),
        out_shape=outs,
        in_specs=[vmem] * len(operands),
        out_specs=(vmem,) * len(outs),
        scratch_shapes=scratch,
        compiler_params=pltpu.CompilerParams(
            collective_id=0, has_side_effects=True, vmem_limit_bytes=62 * 1024 * 1024
        ),
    )(*operands)


def split_flat(vector, model_width, hidden_width, input_width, layer_count):
    layouts = [(input_width, model_width), (model_width,)]
    for _ in range(layer_count):
        layouts = layouts + [
            (4, model_width),
            (model_width, 3 * model_width),
            (model_width, model_width),
            (model_width, hidden_width),
            (hidden_width,),
            (hidden_width, model_width),
        ]
    pieces = []
    offset = 0
    for dimensions in layouts:
        amount = math.prod(dimensions)
        pieces.append(vector[offset : offset + amount].reshape(dimensions))
        offset = offset + amount
    return pieces


def shards(points, counts, cotangent, weights, momenta, averages):
    rows = points.shape[1]
    depth = points.shape[2]
    width = cotangent.shape[2]
    seq_count = lax.axis_size("seq")
    column_mask = jnp.arange(depth, dtype=jnp.int32) < counts[0]
    masked_low = jnp.where(column_mask, points[0], 0).astype(BF16)
    masked_t = jnp.pad(masked_low.T, ((0, DEPTH_PAD - depth), (0, 0)))
    gathered = lax.all_gather(weights.astype(BF16), "dp", axis=0, tiled=True)
    pieces = split_flat(gathered, width, FF, depth, LAYERS)

    def layered(place):
        return jnp.stack([pieces[2 + 6 * layer + place] for layer in range(LAYERS)])

    def spread(values):
        return jnp.broadcast_to(values.astype(F32)[..., None], values.shape + (128,))

    def turned(values):
        return jnp.swapaxes(values, 1, 2)

    rin = jnp.pad(pieces[0], ((0, DEPTH_PAD - depth), (0, 0)))
    norms, wqkv, wo, wup, bup, wd = (layered(place) for place in range(6))
    operands = (
        masked_t, rin.T, rin, spread(pieces[1]), spread(norms), spread(bup),
        turned(wqkv), wqkv, turned(wo), wo, turned(wup), wup, turned(wd), wd, cotangent[0],
    )
    states, pg_t, gri, grb, gnorm, gwqkv, gwo, gwup, gbup, gwd = run_block(
        seq_count, rows, width, FF, operands
    )
    point_grad = jnp.where(column_mask, pg_t[:depth].T, 0.0)[None]
    gnorm = jnp.sum(gnorm, axis=-1)
    flat_parts = [gri[:depth].reshape(-1), grb[0]]
    for layer in range(LAYERS):
        flat_parts += [
            member.reshape(-1)
            for member in (
                gnorm[layer], gwqkv[layer], gwo[layer], gwup[layer], gbup[layer, 0], gwd[layer],
            )
        ]
    used_grads = jnp.concatenate(flat_parts)
    total_length = weights.shape[0] * lax.axis_size("dp")
    flat_grad = jnp.pad(used_grads, (0, total_length - used_grads.shape[0]))
    owner_share = lax.psum_scatter(flat_grad, "dp", scatter_dimension=0, tiled=True)
    gradients = lax.psum(owner_share.astype(BF16), "seq").astype(F32)
    momenta_new = MOMENTUM * momenta + gradients
    weights_new = weights - RATE * (gradients + MOMENTUM * momenta_new)
    averages_new = AVERAGE_DECAY * averages + (1.0 - AVERAGE_DECAY) * weights_new
    return (states[None], point_grad, gradients, weights_new, momenta_new, averages_new)


def solution(mesh):
    placed = (P("dp", "seq", None), P("dp"), P("dp", "seq", None), P("dp"), P("dp"), P("dp"))
    return jax.shard_map(
        shards,
        mesh=mesh,
        in_specs=placed,
        out_specs=(P("dp", "seq", None), P("dp", "seq", None), P("dp"), P("dp"), P("dp"), P("dp")),
        check_vma=False,
    )
```

time: 903 us -> 583 us (0.65)
  matrix products: 155 us -> 0 us
  Pallas kernels: 0 us -> 104 us
  waiting for transfers between devices: 211 us -> 132 us
  other arithmetic: 93.6 us -> 26.6 us
  blocking collectives: 312 us -> 249 us
  local copies, waits for them, and re-layouts: 106 us -> 54.4 us
    dot_general x75 -> x0, matrix products: 155 us -> none  [the longest x4 26.2 us: layer_backward(): jnp.einsum('qhd,khd->hqk', grad_heads, value_heads, preferred_element_typ...]
    pallas_call x0 -> x1, Pallas kernels: none -> 104 us  [run_block(): pl.pallas_call(functools.partial(block_kernel, seq_count), out_shape=outs...]
    reduce_scatter x8 -> x0, waiting for transfers between devices: 86.8 us -> none  [the longest x4 86.7 us: layer_backward(): lax.psum_scatter(grad_keys_all.astype(jnp.bfloat16), 'seq', scatter_dimen...]
    all_gather x8 -> x0, blocking collectives: 62.1 us -> none  [the longest x4 32.1 us: layer_forward(): lax.all_gather(key_rows, 'seq', axis=0, tiled=True)]
    unnamed x328 -> x49, local copies, waits for them, and re-layouts: 60 us -> 22.4 us
    convert_element_type x12 -> x4, other arithmetic: 32.5 us -> 1.87 us  [the longest x1 1.18 us: shards(): gathered = lax.all_gather(weights.astype(BF16), 'dp', axis=0, tiled=True)]
    reduce_sum x29 -> x1, other arithmetic: 25.6 us -> 1.57 us  [shards(): gnorm = jnp.sum(gnorm, axis=-1)]
    all_gather x8 -> x0, local copies, waits for them, and re-layouts: 10.1 us -> none  [the longest x4 5.29 us: layer_forward(): lax.all_gather(value_rows, 'seq', axis=0, tiled=True)]
  transfers between devices with their start and end apart: 10 -> 2, of which waited for: 6 -> 2; matrix products, arithmetic and copies ran while one was open for 10% -> 1% of each run, Pallas kernels for 0% -> 0%
where the time goes in v1:
time: 583 us; the launch traced here: 582 us
  blocking collectives  249 us (43%)
  waiting for transfers between devices  132 us (23%)
  Pallas kernels  104 us (18%)
  local copies, waits for them, and re-layouts  54.4 us (9%)
  other arithmetic  26.6 us (5%)
  between operations  15.8 us (3%)
    unnamed x1, blocking collectives  249 us
    pallas_call x1, Pallas kernels, run_block(): pl.pallas_call(functools.partial(block_kernel, seq_count), out_shape=outs...  104 us
    all_gather x1, waiting for transfers between devices, shards(): gathered = lax.all_gather(weights.astype(BF16), 'dp', axis=0, tiled=True)  98.5 us
    psum x1, waiting for transfers between devices, shards(): gradients = lax.psum(owner_share.astype(BF16), 'seq').astype(F32)  33.2 us
    unnamed x49, local copies, waits for them, and re-layouts  22.4 us
    all_gather x1, other arithmetic, shards(): gathered = lax.all_gather(weights.astype(BF16), 'dp', axis=0, tiled=True)  18.8 us
  transfers between devices with their start and end apart: 2, of which 2 were waited for; matrix products, arithmetic and copies ran while one was open for 1% of the time, Pallas kernels for 0%

profile of v1, /device:TPU:0, one launch (start us, length us, event | category | flops | bytes accessed | tf_op | source)
XLA Modules:
  0.0 581.7 jit_solution(3532653209067803921)
XLA Ops:
  7.2 1.2 convert_element_type.33
  8.4 5.3 reshape.60
  14.4 1.2 dynamic-slice
  17.7 98.5 %all-gather.3.cloned.1.call-done = bf16[8,1,198144]{2,1,0:T(2,128)(2,1)} async-done(((bf16[1,1,198144]{2,1,0:T(2,128)(2,1)}), bf16[8,1,198144]{2,1,0:T(2,128)(2,1)}) %all-gather.3.cloned.1.call-update) | async-done | bytes 3170320 | tf_op jit(solution)/shard_map/all_gather | solution.py:407
  116.2 18.8 %reduce = bf16[8,198144]{1,0:T(8,128)(2,1)S(1)} reduce(bf16[8,1,198144]{2,1,0:T(2,128)(2,1)} %all-gather.3.cloned.1.call-done, bf16[]{:T(256)} %constant.27), dimensions={1}, to_apply=%all-gather.reduce_sub_computation | reduce | bytes 6340610 | tf_op jit(solution)/shard_map/all_gather | solution.py:407
  134.9 6.4 %reshape.61 = bf16[1585152]{0:T(1024)(128)(2,1)} reshape(bf16[8,198144]{1,0:T(8,128)(2,1)S(1)} %reduce) | data formatting | bytes 6340608
  143.7 1.3 fusion.3
  145.0 2.8 fusion.1
  151.2 1.1 stack_reshape.27
  152.9 2.1 stack_reshape.31
  158.1 1.2 copy.25.wqkv_t
  160.3 1.4 copy.27.wup_t
  161.7 1.1 constant_dynamic-update-slice_fusion.6.wd
  162.8 1.3 copy.28.wd_t
  164.9 1.3 broadcast_in_dim.44.bup
  166.2 1.3 broadcast_in_dim.43.norms
  167.5 103.8 %shard_map.109 = (bf16[256,256]{1,0:T(8,128)(2,1)}, f32[32,256]{1,0:T(8,128)}, f32[32,256]{1,0:T(8,128)}, f32[8,256]{1,0:T(8,128)}, f32[2,4,256,128]{3,2,1,0:T(8...) custom-call(bf16[32,256]{1,0:T(8,128)(2,1)} %pad.11.masked_t, ...), custom_call_target="tpu_custom_call" | custom-call | tf_op jit(solution)/shard_map/pallas_call | solution.py:367
  272.0 1.6 reduce_sum.9
  276.5 1.5 fusion.5
  278.1 1.8 slice_bitcast_fusion.1
  283.2 3.1 pad.13
  286.4 249.4 %all-reduce.8 = bf16[1585152]{0:T(1024)(128)(2,1)S(1)} all-reduce(f32[1585152]{0:T(1024)} %pad.13), channel_id=2, replica_groups=mesh['dp'=8,'seq'=4] {'dp'}, use_global_device_ids=true, to_apply=%region_1.2.clone | all-reduce | flops 1585152 | bytes 9510912
  537.5 33.2 %all-reduce.7.cloned.1.call-done = bf16[198144]{0:T(1024)(128)(2,1)} async-done(((bf16[198144]{0:T(1024)(128)(2,1)}), bf16[198144]{0:T(1024)(128)(2,1)}) %all-reduce.7.cloned.1.call-update) | async-done | bytes 396304 | tf_op jit(solution)/shard_map/psum | solution.py:442
  570.6 3.5 multiply_add_fusion
  (85 shorter events, 22.0 us)
Async XLA Ops:
  7.2 109.0 %all-gather.3.cloned.1.call-start = ((), (), s32[]{:S(2)}) async-start(), calls=%async_computation.1 | async-start | bytes 7133184 | tf_op jit(solution)/shard_map/all_gather | solution.py:407
  13.7 557.0 %all-reduce.7.cloned.1.call-start = ((), (), s32[]{:S(2)}) async-start(), calls=%async_computation | async-start | bytes 794624 | tf_op jit(solution)/shard_map/psum | solution.py:442
  141.3 6.6 %slice-start = ((bf16[1585152]{0:T(1024)(128)(2,1)}), bf16[5120]{0:T(1024)(128)(2,1)S(1)}, s32[]{:S(2)}) async-start(bf16[1585152]{0:T(1024)(128)(2,1)} %reshape.61), calls=%async_computation.2 | async-start | bytes 20480 | tf_op jit(solution)/shard_map/slice | solution.py:394
  149.4 3.3 copy-start.4
  158.1 9.4 %copy-start.2 = (bf16[2,256,768]{2,1,0:T(8,128)(2,1)}, bf16[2,256,768]{2,1,0:T(8,128)(2,1)S(1)}, u32[]{:S(2)}) copy-start(bf16[2,256,768]{2,1,0:T(8,128)(2,1)S(1)} %constant_dynamic-update-slice_fusion.wqkv) | copy-start | bytes 2359300
  160.3 2.4 copy-start.1
  162.8 4.7 copy-start
  278.1 2.3 copy-start.3
  286.4 250.4 %copy-start.6 = (f32[32,256]{1,0:T(8,128)S(1)}, f32[32,256]{1,0:T(8,128)}, u32[]{:S(2)}) copy-start(f32[32,256]{1,0:T(8,128)} %get-tuple-element.17) | copy-start | bytes 98308
  286.4 287.8 %copy-start.5 = (bf16[256,256]{1,0:T(8,128)(2,1)S(1)}, bf16[256,256]{1,0:T(8,128)(2,1)}, u32[]{:S(2)}) copy-start(bf16[256,256]{1,0:T(8,128)(2,1)} %get-tuple-element.16) | copy-start | bytes 393220
Sparse Core Ops, SparseCore 0:
  13.8 102.3 all-gather.2
  536.9 33.7 all-reduce.6

commit v2 on v1

v2 whole, which is shorter than its diff:
```python
import functools
import math

import jax
import jax.numpy as jnp
from jax import lax
from jax.experimental import pallas as pl
from jax.experimental.pallas import tpu as pltpu
from jax.sharding import PartitionSpec as P

MESH = pl.DeviceIdType.MESH
HEADS = 8
FF = 1024
LAYERS = 2
LOOPS = 2
APPS = LAYERS * LOOPS

EPSILON = 1e-05
RATE = 0.0003
MOMENTUM = 0.5
AVERAGE_DECAY = 0.9

F32 = jnp.float32
BF16 = jnp.bfloat16
GELU_A = math.sqrt(2.0 / math.pi)
GELU_B = 0.044715


def mm(left, right):
    return jnp.dot(left, right, preferred_element_type=F32)


def mm_nt(left, right):
    return lax.dot_general(left, right, (((1,), (1,)), ((), ())), preferred_element_type=F32)


def twice(column):
    return jnp.concatenate([column, column], axis=1)


def halves(values):
    return values[:, :128] + values[:, 128:]


def normalise(values):
    centred = values - jnp.mean(values, axis=0, keepdims=True)
    variance = jnp.mean(centred * centred, axis=0, keepdims=True)
    scale = lax.rsqrt(variance + EPSILON)
    return centred * scale, scale


def normalise_back(grad, unit, scale, gain):
    scaled = grad * gain
    first = jnp.mean(scaled, axis=0, keepdims=True)
    second = jnp.mean(scaled * unit, axis=0, keepdims=True)
    return (scaled - first - unit * second) * scale


class Plan:
    def __init__(self, rows, depth, width, share, dp_count, seq_count):
        self.rows = rows
        self.depth = depth
        self.width = width
        self.hidden = FF
        self.dp = dp_count
        self.zs = dp_count // 2
        self.seq = seq_count
        self.flat = share // width
        self.half = -(-self.flat // 32) * 16
        self.block = 4 + 3 * width + width + FF + FF // width + FF
        self.total = self.flat * dp_count
        self.space = self.total + 32 + width

    def base(self, layer):
        return self.depth + 1 + layer * self.block


def whole_kernel(plan, names, *refs):
    ref = dict(zip(names, refs, strict=True))
    (
        points, counts, cot, weights, momenta, averages,
        states, point_grad, gradients, weights_new, momenta_new, averages_new,
    ) = (ref[name] for name in names[:12])
    rows, width, hidden = plan.rows, plan.width, plan.hidden
    seq_count, dp_count, zs, half = plan.seq, plan.dp, plan.zs, plan.half
    head_width = width // HEADS
    exp_scale = math.log2(math.e) / math.sqrt(head_width)
    score_scale = 1.0 / math.sqrt(head_width)
    low_half, high_half = half, plan.flat - half

    me = lax.axis_index("seq")
    owner = lax.axis_index("dp")
    my_z, my_x = owner // 2, lax.rem(owner, 2)
    my_y, my_c = me // 2, lax.rem(me, 2)
    sibling = {"seq": my_y * 2 + (1 - my_c)}
    across = {"seq": (1 - my_y) * 2 + my_c}
    beside = {"dp": my_z * 2 + (1 - my_x)}

    barrier = pltpu.get_barrier_semaphore()

    def greet(device):
        pl.semaphore_signal(barrier, inc=1, device_id=device, device_id_type=MESH)

    for step in range(1, seq_count):
        greet({"seq": lax.rem(me + step, seq_count)})
    greet(beside)

    def greet_z(step, carry):
        greet({"dp": lax.rem(my_z + step, zs) * 2 + my_x})
        return carry

    lax.fori_loop(1, zs, greet_z, 0)

    def remote(source, target, send, receive, device):
        return pltpu.make_async_remote_copy(
            src_ref=source, dst_ref=target, send_sem=send, recv_sem=receive,
            device_id=device, device_id_type=MESH,
        )

    gathered = ref["gathered"]
    tail_rows = high_half // 16 * 16
    for h in range(2):
        for r, count in ((0, low_half), (1, tail_rows)):
            gathered[owner, h, r, :count] = weights[
                pl.ds(2 * r * half + h, count, stride=2), :
            ].astype(BF16)
        if high_half < half:
            gathered[owner, h, 1, tail_rows:] = jnp.concatenate(
                [
                    weights[pl.ds(2 * (half + tail_rows) + h, high_half - tail_rows, stride=2), :],
                    jnp.zeros((half - high_half, 128), F32),
                ],
                axis=0,
            ).astype(BF16)

    pl.semaphore_wait(barrier, seq_count - 1 + zs)

    def along_z(source_z, target_z):
        piece = gathered.at[2 * source_z + my_x, my_c, my_y]
        return remote(
            piece, piece, ref["send_wz"].at[target_z], ref["recv_wz"].at[source_z],
            {"dp": 2 * target_z + my_x},
        )

    def along_y(z, part):
        piece = gathered.at[2 * z + my_x, my_c, part]
        return remote(piece, piece, ref["send_wy"].at[z], ref["recv_wy"].at[z], across)

    def along_x(z, x, part):
        piece = gathered.at[2 * z + x, my_c, part]
        return remote(
            piece, piece, ref["send_wx"].at[z, part], ref["recv_wx"].at[z, part], beside
        )

    def along_c(share, column):
        piece = gathered.at[share, column]
        return remote(piece, piece, ref["send_wc"].at[share], ref["recv_wc"].at[share], sibling)

    def each_z(body):
        def step(z, carry):
            body(z)
            return carry

        lax.fori_loop(0, zs, step, 0)

    def each_other_z(body):
        def step(z, carry):
            @pl.when(z != my_z)
            def _():
                body(z)

            return carry

        lax.fori_loop(0, zs, step, 0)

    each_other_z(lambda z: along_z(my_z, z).start())
    along_x(my_z, my_x, 0).start()
    along_x(my_z, my_x, 1).start()

    def second(z):
        along_z(z, my_z).wait_recv()
        along_y(z, my_y).start()
        along_x(z, my_x, my_y).start()

    def third(z):
        along_y(z, 1 - my_y).wait_recv()
        along_x(z, my_x, 1 - my_y).start()
        along_c(2 * z + my_x, my_c).start()

    def fourth(z):
        along_x(z, 1 - my_x, 0).wait_recv()
        along_x(z, 1 - my_x, 1).wait_recv()
        along_c(2 * z + 1 - my_x, my_c).start()

    def fifth(z):
        @pl.when(z != my_z)
        def _():
            along_c(2 * z + my_x, 1 - my_c).wait_recv()

        along_c(2 * z + 1 - my_x, 1 - my_c).wait_recv()

    each_other_z(second)
    each_other_z(third)
    each_z(fourth)
    each_z(fifth)

    flat = ref["flat"]
    for share in range(dp_count):
        for h in range(2):
            for r in range(2):
                flat[h, pl.ds(share * plan.flat + r * half, half), :] = gathered[
                    share, h, r
                ].astype(F32)

    rin, rit, rbias, norms, bup = (ref[n] for n in ("rin", "rit", "rbias", "norms", "bup"))
    wqkv, wqkv_t, wo, wo_t = (ref[n] for n in ("wqkv", "wqkv_t", "wo", "wo_t"))
    wup, wup_t, wd, wd_t = (ref[n] for n in ("wup", "wup_t", "wd", "wd_t"))
    depth_row = lax.broadcasted_iota(jnp.int32, (128, 128), 0)
    for h in range(2):
        lanes = slice(128 * h, 128 * (h + 1))
        block = flat[h, :128]
        turned = jnp.transpose(block)
        rbias[lanes] = jnp.broadcast_to(turned[:, plan.depth : plan.depth + 1], (128, 128))
        block = jnp.where(depth_row < plan.depth, block, 0.0)
        rin[:, lanes] = block.astype(BF16)
        rit[lanes] = jnp.transpose(block).astype(BF16)
        for layer in range(LAYERS):
            base = plan.base(layer)
            turned = jnp.transpose(flat[h, pl.ds(base, 128), :])
            for j in range(4):
                norms[layer, j, lanes] = jnp.broadcast_to(turned[:, j : j + 1], (128, 128))
            base += 4
            for j in range(3):
                value = flat[h, pl.ds(base + j, width, stride=3), :]
                place = slice(width * j + 128 * h, width * j + 128 * (h + 1))
                wqkv[layer, :, place] = value.astype(BF16)
                wqkv_t[layer, place] = jnp.transpose(value).astype(BF16)
            base += 3 * width
            value = flat[h, pl.ds(base, width), :]
            wo[layer, :, lanes] = value.astype(BF16)
            wo_t[layer, lanes] = jnp.transpose(value).astype(BF16)
            base += width
            parts = hidden // width
            for j in range(parts):
                value = flat[h, pl.ds(base + j, width, stride=parts), :]
                place = slice(width * j + 128 * h, width * j + 128 * (h + 1))
                wup[layer, :, place] = value.astype(BF16)
                wup_t[layer, place] = jnp.transpose(value).astype(BF16)
            base += hidden
            turned = jnp.transpose(flat[h, pl.ds(base, 128), :])
            for j in range(parts):
                bup[layer, width * j + 128 * h : width * j + 128 * (h + 1)] = jnp.broadcast_to(
                    turned[:, j : j + 1], (128, 128)
                )
            base += parts
            value = flat[h, pl.ds(base, hidden), :]
            wd[layer, :, lanes] = value.astype(BF16)
            wd_t[layer, lanes] = jnp.transpose(value).astype(BF16)

    column_mask = lax.broadcasted_iota(jnp.int32, (rows, 128), 1) < counts[0]
    wide_points = ref["wide_points"]
    wide_points[...] = jnp.zeros_like(wide_points)
    wide_points[:, : plan.depth] = points[...].astype(F32)
    masked_t = jnp.transpose(jnp.where(column_mask, wide_points[...], 0.0)).astype(BF16)
    ref["masked_t"][...] = masked_t

    (gnorm, hid, nrm, qsave, kv, kt, vt, att, osave, lse, upd, nrm2, gp, act, emb, qmask, qtok, domask, dotok, ps, ds, peak, total, mixed, dq, gbuf, gemb, gin, send_n, recv_n, send_g, recv_g) = (
        ref[n] for n in ("gnorm", "hid", "nrm", "qsave", "kv", "kt", "vt", "att", "osave", "lse", "upd", "nrm2", "gp", "act", "emb", "qmask", "qtok", "domask", "dotok", "ps", "ds", "peak", "total", "mixed", "dq", "gbuf", "gemb", "gin", "send_n", "recv_n", "send_g", "recv_g")
    )
    qmask[...] = jnp.zeros_like(qmask)
    domask[...] = jnp.zeros_like(domask)
    for sums in (gnorm, flat):
        sums[...] = jnp.zeros_like(sums)
    parts = hidden // width

    def accumulate(layer, offset, stride, value):
        start = plan.base(0) + layer * plan.block + offset
        count = value.shape[0]
        for h in range(2):
            lanes = slice(128 * h, 128 * (h + 1))
            flat[h, pl.ds(start, count, stride=stride), :] += value[:, lanes]

    ones = jnp.ones((16, rows), BF16)
    column_head = lax.broadcasted_iota(jnp.int32, (rows, width), 1) // head_width

    embedded = mm(rit[...], ref["masked_t"][...]) + twice(rbias[...])
    emb[...] = embedded
    hid[0] = embedded

    def normed_copy(app, source, target):
        return pltpu.make_async_remote_copy(
            src_ref=nrm.at[app, source],
            dst_ref=nrm.at[app, source],
            send_sem=send_n.at[app, target],
            recv_sem=recv_n.at[app, source],
            device_id={"seq": target},
            device_id_type=MESH,
        )

    def grad_copy(app, source, target):
        return pltpu.make_async_remote_copy(
            src_ref=nrm.at[app, target],
            dst_ref=nrm.at[app, source],
            send_sem=send_g.at[app, target],
            recv_sem=recv_g.at[app, source],
            device_id={"seq": target},
            device_id_type=MESH,
        )

    causal = lax.broadcasted_iota(jnp.int32, (rows, rows), 0) <= lax.broadcasted_iota(
        jnp.int32, (rows, rows), 1
    )

    def project_block(app, layer, block):
        block_t = nrm[app, block]
        kt[app, block] = mm(wqkv_t[layer, width : 2 * width], block_t).astype(BF16)
        vt[...] = mm(wqkv_t[layer, 2 * width :], block_t).astype(BF16)
        kv[app, block] = mm(
            jnp.transpose(block_t.astype(F32)).astype(BF16), wqkv[layer, :, width:]
        ).astype(BF16)

    def attend_block(app, block, diagonal):
        for head in range(HEADS):
            lanes = slice(head * head_width, (head + 1) * head_width)
            scores = mm(kv[app, block, :, :width], qmask[head]) * exp_scale
            if diagonal:
                scores = jnp.where(causal, scores, -jnp.inf)
                top = jnp.max(scores, axis=0, keepdims=True)
                weight = jnp.exp2(scores - top)
                total[head : head + 1] = jnp.sum(weight, axis=0, keepdims=True)
                mixed[lanes] = mm(
                    vt[lanes],
                    weight.astype(BF16),
                )
            else:
                old = peak[head : head + 1]
                top = jnp.maximum(old, jnp.max(scores, axis=0, keepdims=True))
                fade = jnp.exp2(old - top)
                weight = jnp.exp2(scores - top)
                total[head : head + 1] = total[head : head + 1] * fade + jnp.sum(
                    weight, axis=0, keepdims=True
                )
                mixed[lanes] = mixed[lanes] * fade + mm(
                    vt[lanes],
                    weight.astype(BF16),
                )
            peak[head : head + 1] = top

    def forward(app, carry):
        layer = lax.rem(app, LAYERS)
        unit, _ = normalise(hid[app])
        normed = (unit * twice(norms[layer, 0]) + twice(norms[layer, 1])).astype(BF16)
        nrm[app, me] = normed
        for step in range(1, seq_count):

            @pl.when(me + step < seq_count)
            def _():
                normed_copy(app, me, me + step).start()

        queries = mm(wqkv_t[layer, :width], normed).astype(BF16)
        qsave[app] = queries
        for head in range(HEADS):
            lanes = slice(head * head_width, (head + 1) * head_width)
            qmask[head, lanes] = queries[lanes]
        project_block(app, layer, me)
        attend_block(app, me, True)

        def earlier(step, inner):
            block = me - 1 - step
            normed_copy(app, block, me).wait_recv()
            project_block(app, layer, block)
            attend_block(app, block, False)
            return inner

        lax.fori_loop(0, me, earlier, 0)
        for head in range(HEADS):
            lanes = slice(head * head_width, (head + 1) * head_width)
            out = mixed[lanes] * (1.0 / total[head : head + 1])
            osave[app, lanes] = out
            att[app, lanes] = out.astype(BF16)
        lse[app] = peak[...] + jnp.log2(total[...])
        updated = hid[app] + mm(wo_t[layer], att[app])
        upd[app] = updated
        unit, _ = normalise(updated)
        second = (unit * twice(norms[layer, 2]) + twice(norms[layer, 3])).astype(BF16)
        nrm2[app] = second
        before = mm(wup_t[layer], second) + twice(bup[layer])
        squared = before * before
        inner = GELU_A * before * (1.0 + GELU_B * squared)
        turned = jnp.tanh(inner)
        half = 0.5 * (1.0 + turned)
        activated = (before * half).astype(BF16)
        act[app] = activated
        gp[app] = half + (0.5 * GELU_A) * before * (1.0 - turned * turned) * (
            1.0 + (3.0 * GELU_B) * squared
        )
        result = upd[app] + mm(wd_t[layer], act[app])
        again = jnp.where((layer == LAYERS - 1) & (app < APPS - 1), 1.0, 0.0)
        hid[app + 1] = result + again * emb[...]
        return carry

    lax.fori_loop(0, APPS, forward, 0)
    states[...] = jnp.transpose(hid[APPS]).astype(BF16)

    gbuf[...] = jnp.transpose(cot[...].astype(F32))
    gemb[...] = jnp.zeros_like(gemb)

    def attend_back(app, layer, block, diagonal):
        keys = kv[app, block, :, :width]
        values = kv[app, block, :, width:]
        for head in range(HEADS):
            lanes = slice(head * head_width, (head + 1) * head_width)
            wide = slice(head * rows, (head + 1) * rows)
            scores = mm(keys, qmask[head]) * exp_scale
            weight = jnp.exp2(scores - lse[app, head : head + 1])
            if diagonal:
                weight = jnp.where(causal, weight, 0.0)
            ps[:, wide] = weight.astype(BF16)
            grad = mm(values, domask[head])
            back = (weight * (grad - total[head : head + 1])).astype(BF16)
            ds[:, wide] = back
            part = mm(kt[app, block, lanes], back)
            dq[lanes] = dq[lanes] + part
        grad_keys = (mm(ds[...], qtok[...]) * score_scale).astype(BF16)
        grad_values = mm(ps[...], dotok[...]).astype(BF16)
        block_t = nrm[app, block]
        accumulate(layer, 5, 3, mm(block_t, grad_keys))
        accumulate(layer, 6, 3, mm(block_t, grad_values))
        return mm_nt(wqkv[layer, :, width : 2 * width], grad_keys) + mm_nt(
            wqkv[layer, :, 2 * width :], grad_values
        )

    def backward(order, carry):
        app = APPS - 1 - order
        layer = lax.rem(app, LAYERS)
        grad_out = gbuf[...]
        out_low = grad_out.astype(BF16)
        accumulate(layer, 4 + 4 * width + hidden + parts, 1, mm_nt(act[app], out_low))
        pre_low = (mm(wd[layer], out_low) * gp[app]).astype(BF16)
        act[app] = pre_low
        for j in range(parts):
            part = act[app, width * j : width * (j + 1)]
            accumulate(layer, 4 + 4 * width + j, parts, mm_nt(nrm2[app], part))
            accumulate(layer, 4 + 4 * width + hidden + j, 1, mm_nt(ones, part)[:1])
        grad_second = mm(wup[layer], act[app])
        unit, scale = normalise(upd[app])
        gnorm[layer, 2] += halves(grad_second * unit)
        gnorm[layer, 3] += halves(grad_second)
        grad_updated = gbuf[...] + normalise_back(grad_second, unit, scale, twice(norms[layer, 2]))
        gbuf[...] = grad_updated
        branch_low = grad_updated.astype(BF16)
        accumulate(layer, 4 + 3 * width, 1, mm_nt(att[app], branch_low))
        grad_att = mm(wo[layer], branch_low).astype(BF16)
        for head in range(HEADS):
            lanes = slice(head * head_width, (head + 1) * head_width)
            domask[head, lanes] = grad_att[lanes]
            qmask[head, lanes] = qsave[app, lanes]
            total[head : head + 1] = jnp.sum(
                osave[app, lanes] * grad_att[lanes].astype(F32), axis=0, keepdims=True
            )
        grad_tok = jnp.transpose(grad_att.astype(F32))
        query_tok = jnp.transpose(qsave[app].astype(F32))
        for head in range(HEADS):
            wide = slice(head * rows, (head + 1) * rows)
            dotok[wide] = jnp.where(column_head == head, grad_tok, 0.0).astype(BF16)
            qtok[wide] = jnp.where(column_head == head, query_tok, 0.0).astype(BF16)
        dq[...] = jnp.zeros_like(dq)

        def earlier(block, inner):
            nrm[app, block] = attend_back(app, layer, block, False).astype(BF16)
            grad_copy(app, me, block).start()
            return inner

        lax.fori_loop(0, me, earlier, 0)
        gin[...] = attend_back(app, layer, me, True)
        grad_queries = (dq[...] * score_scale).astype(BF16)
        accumulate(layer, 4, 3, mm_nt(nrm[app, me], grad_queries))
        gin[...] += mm(wqkv[layer, :, :width], grad_queries)

        def later(source, inner):
            grad_copy(app, source, me).wait_recv()
            gin[...] += nrm[app, source].astype(F32)
            return inner

        lax.fori_loop(me + 1, seq_count, later, 0)
        grad_normed = gin[...]
        unit, scale = normalise(hid[app])
        gnorm[layer, 0] += halves(grad_normed * unit)
        gnorm[layer, 1] += halves(grad_normed)
        grad_in = gbuf[...] + normalise_back(grad_normed, unit, scale, twice(norms[layer, 0]))
        gbuf[...] = grad_in
        first = jnp.where(layer == 0, 1.0, 0.0)
        gemb[...] += first * grad_in
        return carry

    lax.fori_loop(0, APPS, backward, 0)

    embed_low = gemb[...].astype(BF16)
    grad_in_rows = mm_nt(ref["masked_t"][...], embed_low)
    grad_bias_rows = mm_nt(ones, embed_low)
    point_rows = jnp.where(column_mask, jnp.transpose(mm(rin[...], embed_low)), 0.0)
    point_grad[...] = point_rows[:, : plan.depth]
    for h in range(2):
        lanes = slice(128 * h, 128 * (h + 1))
        flat[h, : plan.depth] = grad_in_rows[: plan.depth, lanes]
        flat[h, plan.depth : plan.depth + 1] = grad_bias_rows[:1, lanes]
        for layer in range(LAYERS):
            base = plan.base(layer)
            for j in range(4):
                flat[h, base + j : base + j + 1] = jnp.sum(
                    jnp.transpose(gnorm[layer, j, lanes]), axis=0, keepdims=True
                )

    each_other_z(lambda z: along_z(my_z, z).wait_send())
    each_other_z(lambda z: along_y(z, my_y).wait_send())
    for r in range(2):
        each_z(lambda z, r=r: along_x(z, my_x, r).wait_send())
    each_other_z(lambda z: along_c(2 * z + my_x, my_c).wait_send())
    each_z(lambda z: along_c(2 * z + 1 - my_x, my_c).wait_send())
    parts_low = ref["gathered"]
    for share in range(dp_count):
        for h in range(2):
            for r in range(2):
                parts_low[share, h, r] = flat[
                    h, pl.ds(share * plan.flat + r * half, half), :
                ].astype(BF16)

    from_core, from_x, from_y, from_z = (
        ref[n] for n in ("from_core", "from_x", "from_y", "from_z")
    )
    copy = remote(
        parts_low.at[:, 1 - my_c], from_core, ref["send_gc"].at[0], ref["recv_gc"].at[0], sibling
    )
    copy.start()
    copy.wait()

    def add(target, source):
        target[...] = (target[...].astype(F32) + source[...].astype(F32)).astype(BF16)

    def add_core(share, carry):
        for r in range(2):
            add(parts_low.at[share, my_c, r], from_core.at[share, r])
        return carry

    lax.fori_loop(0, dp_count, add_core, 0)

    def grad_x(z):
        return remote(
            parts_low.at[2 * z + 1 - my_x, my_c], from_x.at[z],
            ref["send_gx"].at[z], ref["recv_gx"].at[z], beside,
        )

    def grad_y(z):
        return remote(
            parts_low.at[2 * z + my_x, my_c, 1 - my_y], from_y.at[z],
            ref["send_gy"].at[z], ref["recv_gy"].at[z], across,
        )

    def grad_z(source_z, target_z):
        return remote(
            parts_low.at[2 * target_z + my_x, my_c, my_y], from_z.at[source_z],
            ref["send_gz"].at[target_z], ref["recv_gz"].at[source_z], {"dp": 2 * target_z + my_x},
        )

    each_z(lambda z: grad_x(z).start())

    def after_x(z):
        grad_x(z).wait()
        for r in range(2):
            add(parts_low.at[2 * z + my_x, my_c, r], from_x.at[z, r])
        grad_y(z).start()

    each_z(after_x)

    def after_y(z):
        grad_y(z).wait()
        add(parts_low.at[2 * z + my_x, my_c, my_y], from_y.at[z])

        @pl.when(z != my_z)
        def _():
            grad_z(my_z, z).start()

    each_z(after_y)
    last = ref["last"]
    last[...] = parts_low[owner, my_c, my_y].astype(F32)

    def after_z(z):
        grad_z(z, my_z).wait_recv()
        last[...] += from_z[z].astype(F32)

    each_other_z(after_z)
    summed = ref["summed"]
    summed[my_c, my_y] = last[...].astype(BF16)

    def share_seq(source, target):
        piece = summed.at[lax.rem(source, 2), source // 2]
        return remote(
            piece, piece, ref["send_gs"].at[target], ref["recv_gs"].at[source], {"seq": target}
        )

    for step in range(1, seq_count):
        share_seq(me, lax.rem(me + step, seq_count)).start()
    for step in range(1, seq_count):
        share_seq(lax.rem(me + step, seq_count), me).wait_recv()
    for h in range(2):
        for r, count in ((0, low_half), (1, high_half)):
            gradients[pl.ds(2 * r * half + h, count, stride=2), :] = summed[h, r].astype(F32)[
                :count
            ]
    grad = gradients[...]
    momentum = MOMENTUM * momenta[...] + grad
    momenta_new[...] = momentum
    fresh = weights[...] - RATE * (grad + MOMENTUM * momentum)
    weights_new[...] = fresh
    averages_new[...] = AVERAGE_DECAY * averages[...] + (1.0 - AVERAGE_DECAY) * fresh

    each_other_z(lambda z: grad_z(my_z, z).wait_send())
    for step in range(1, seq_count):
        share_seq(me, lax.rem(me + step, seq_count)).wait_send()

    def finish(app, carry):
        def sent_normed(target, inner):
            normed_copy(app, me, target).wait_send()
            return inner

        def sent_grad(target, inner):
            grad_copy(app, me, target).wait_send()
            return inner

        lax.fori_loop(me + 1, seq_count, sent_normed, 0)
        lax.fori_loop(0, me, sent_grad, 0)
        return carry

    lax.fori_loop(0, APPS, finish, 0)


def shards(points, counts, cotangent, weights, momenta, averages):
    rows, depth = points.shape[1:]
    width = cotangent.shape[2]
    share = weights.shape[0]
    plan = Plan(rows, depth, width, share, lax.axis_size("dp"), lax.axis_size("seq"))
    hidden, seq_count, dp_count, zs, half = plan.hidden, plan.seq, plan.dp, plan.zs, plan.half
    vmem = pl.BlockSpec(memory_space=pltpu.VMEM)
    smem = pl.BlockSpec(memory_space=pltpu.SMEM)
    shape = jax.ShapeDtypeStruct
    lines = (share // 128, 128)
    outs = (
        shape((rows, width), BF16),
        shape((rows, depth), F32),
        shape(lines, F32),
        shape(lines, F32),
        shape(lines, F32),
        shape(lines, F32),
    )
    low = lambda *dims: pltpu.VMEM(dims, BF16)
    full = lambda *dims: pltpu.VMEM(dims, F32)
    flags = lambda *dims: pltpu.SemaphoreType.DMA(dims)
    scratch = {
        "gathered": low(dp_count, 2, 2, half, 128),
        "flat": full(2, plan.space, 128),
        "rin": low(128, width),
        "rit": low(width, 128),
        "rbias": full(width, 128),
        "norms": full(LAYERS, 4, width, 128),
        "bup": full(LAYERS, hidden, 128),
        "wqkv": low(LAYERS, width, 3 * width),
        "wqkv_t": low(LAYERS, 3 * width, width),
        "wo": low(LAYERS, width, width),
        "wo_t": low(LAYERS, width, width),
        "wup": low(LAYERS, width, hidden),
        "wup_t": low(LAYERS, hidden, width),
        "wd": low(LAYERS, hidden, width),
        "wd_t": low(LAYERS, width, hidden),
        "wide_points": full(rows, 128),
        "masked_t": low(128, rows),
        "gnorm": full(LAYERS, 4, width, 128),
        "from_core": low(dp_count, 2, half, 128),
        "from_x": low(zs, 2, half, 128),
        "from_y": low(zs, half, 128),
        "from_z": low(zs, half, 128),
        "last": full(half, 128),
        "summed": low(2, 2, half, 128),
        "hid": full(APPS + 1, width, rows),
        "nrm": low(APPS, seq_count, width, rows),
        "qsave": low(APPS, width, rows),
        "kv": low(APPS, seq_count, rows, 2 * width),
        "kt": low(APPS, seq_count, width, rows),
        "vt": low(width, rows),
        "att": low(APPS, width, rows),
        "osave": full(APPS, width, rows),
        "lse": full(APPS, HEADS, rows),
        "upd": full(APPS, width, rows),
        "nrm2": low(APPS, width, rows),
        "gp": full(APPS, hidden, rows),
        "act": low(APPS, hidden, rows),
        "emb": full(width, rows),
        "qmask": low(HEADS, width, rows),
        "qtok": low(HEADS * rows, width),
        "domask": low(HEADS, width, rows),
        "dotok": low(HEADS * rows, width),
        "ps": low(rows, HEADS * rows),
        "ds": low(rows, HEADS * rows),
        "peak": full(HEADS, rows),
        "total": full(HEADS, rows),
        "mixed": full(width, rows),
        "dq": full(width, rows),
        "gbuf": full(width, rows),
        "gemb": full(width, rows),
        "gin": full(width, rows),
        "send_n": flags(APPS, seq_count),
        "recv_n": flags(APPS, seq_count),
        "send_g": flags(APPS, seq_count),
        "recv_g": flags(APPS, seq_count),
        "send_wz": flags(zs),
        "recv_wz": flags(zs),
        "send_wy": flags(zs),
        "recv_wy": flags(zs),
        "send_wx": flags(zs, 2),
        "recv_wx": flags(zs, 2),
        "send_wc": flags(dp_count),
        "recv_wc": flags(dp_count),
        "send_gc": flags(1),
        "recv_gc": flags(1),
        "send_gx": flags(zs),
        "recv_gx": flags(zs),
        "send_gy": flags(zs),
        "recv_gy": flags(zs),
        "send_gz": flags(zs),
        "recv_gz": flags(zs),
        "send_gs": flags(seq_count),
        "recv_gs": flags(seq_count),
    }
    names = (
        "points", "counts", "cot", "weights", "momenta", "averages",
        "states", "point_grad", "gradients", "weights_new", "momenta_new", "averages_new",
        *scratch,
    )
    states, point_grad, *vectors = pl.pallas_call(
        functools.partial(whole_kernel, plan, names),
        out_shape=outs,
        in_specs=[vmem, smem, vmem, vmem, vmem, vmem],
        out_specs=(vmem,) * len(outs),
        scratch_shapes=list(scratch.values()),
        compiler_params=pltpu.CompilerParams(
            collective_id=0, has_side_effects=True, vmem_limit_bytes=63 * 1024 * 1024
        ),
    )(
        points[0], counts, cotangent[0],
        weights.reshape(lines), momenta.reshape(lines), averages.reshape(lines),
    )
    return (states[None], point_grad[None], *(v.reshape(-1) for v in vectors))


def solution(mesh):
    placed = (P("dp", "seq", None), P("dp"), P("dp", "seq", None), P("dp"), P("dp"), P("dp"))
    return jax.shard_map(
        shards,
        mesh=mesh,
        in_specs=placed,
        out_specs=(P("dp", "seq", None), P("dp", "seq", None), P("dp"), P("dp"), P("dp"), P("dp")),
        check_vma=False,
    )
```

time: 583 us -> 187 us (0.32)
  blocking collectives: 249 us -> 0 us
  waiting for transfers between devices: 132 us -> 0 us
  Pallas kernels: 104 us -> 173 us
  local copies, waits for them, and re-layouts: 54.4 us -> 9.67 us
  other arithmetic: 26.6 us -> 0 us
  between operations: 15.8 us -> 1.3 us
    unnamed x1 -> x0, blocking collectives: 249 us -> none
    all_gather x1 -> x0, waiting for transfers between devices: 98.5 us -> none  [shards(): gathered = lax.all_gather(weights.astype(BF16), 'dp', axis=0, tiled=True)]
    pallas_call x1, Pallas kernels: 104 us -> 173 us  [shards(): pl.pallas_call(functools.partial(whole_kernel, plan, names), out_shape=ou...]
    psum x1 -> x0, waiting for transfers between devices: 33.2 us -> none  [shards(): gradients = lax.psum(owner_share.astype(BF16), 'seq').astype(F32)]
    all_gather x1 -> x0, other arithmetic: 18.8 us -> none  [shards(): gathered = lax.all_gather(weights.astype(BF16), 'dp', axis=0, tiled=True)]
    unnamed x49 -> x15, local copies, waits for them, and re-layouts: 22.4 us -> 9.67 us
    slice x11 -> x0, local copies, waits for them, and re-layouts: 9.55 us -> none  [the longest x7 5.85 us: split_flat(): pieces.append(vector[offset:offset + amount].reshape(dimensions))]
    another operation x18 -> x0, local copies, waits for them, and re-layouts: 9.08 us -> none  [the longest x16 8.97 us: layered(): return jnp.stack([pieces[2 + 6 * layer + place] for layer in range(LAYERS)])]
  transfers between devices with their start and end apart: 2 -> 0, of which waited for: 2 -> 0; matrix products, arithmetic and copies ran while one was open for 1% -> 0% of each run, Pallas kernels for 0% -> 0%
where the time goes in v2:
time: 187 us; the launch traced here: 184 us
  Pallas kernels  173 us (93%)
  local copies, waits for them, and re-layouts  9.67 us (5%)
    pallas_call x1, Pallas kernels, shards(): pl.pallas_call(functools.partial(whole_kernel, plan, names), out_shape=ou...  173 us
    unnamed x15, local copies, waits for them, and re-layouts  9.67 us

profile of v2, /device:TPU:0, one launch (start us, length us, event | category | flops | bytes accessed | tf_op | source)
XLA Modules:
  0.0 184.3 jit_solution(16334113593520486728)
XLA Ops:
  1.3 1.5 copy.12
  2.7 173.4 %shard_map.109 = (bf16[256,256]{1,0:T(8,128)(2,1)}, f32[256,20]{1,0:T(8,128)}, f32[1548,128]{1,0:T(8,128)}, f32[1548,128]{1,0:T(8,128)}, f32[1548,128]{1,0:T(8,128)}, /*index=5*/f32[1548,128]{1,0:T(8,128)}) custom-call(bf16[256,20]{1,0:T(8,128)(2,1)} %bitcast.18, s32[1]{0:T(128)S(6)} %copy.19.refs_1_, bf16[256,256]{1,0:T(8,128)(2,1)} %bitcast.19, ...), custom_call_target="tpu_custom_call" | custom-call | tf_op jit(solution)/shard_map/pallas_call | solution.py:738
  176.1 0.0 copy-start.3
  176.1 1.6 copy.13
  177.7 0.0 copy-done.3
  177.7 0.7 copy.20
  178.4 0.0 copy-start.2
  178.4 2.1 %copy.21 = f32[198144]{0:T(1024)} copy(f32[198144]{0:T(1024)} %bitcast.17) | data formatting | bytes 1585152
  180.5 0.0 copy-done.2
  180.5 0.0 copy-start.1
  180.5 0.9 copy.22
  181.5 0.5 copy-done.1
  182.0 0.0 copy-start
  182.0 0.9 copy.23
  182.9 0.5 copy-done
  183.4 0.9 copy.24
Async XLA Ops:
  176.1 1.6 copy-start.3
  178.4 2.1 %copy-start.2 = (f32[1548,128]{1,0:T(8,128)S(1)}, f32[1548,128]{1,0:T(8,128)}, u32[]{:S(2)}) copy-start(f32[1548,128]{1,0:T(8,128)} %get-tuple-element.15) | copy-start | bytes 2377732
  180.5 1.4 copy-start.1
  182.0 1.4 copy-start

commit v3 on v2

--- a/solution.py
+++ b/solution.py
@@ -24,6 +24,9 @@
 BF16 = jnp.bfloat16
 GELU_A = math.sqrt(2.0 / math.pi)
 GELU_B = 0.044715
+LOCAL = (
+    "gnorm", "hid", "nrm", "qsave", "kv", "kt", "vt", "att", "osave", "lse", "upd", "nrm2", "gp", "act", "emb", "qmask", "domask", "ps", "ds", "dqkv", "grad_low", "peak", "total", "gbuf", "gemb", "gin", "send_n", "recv_n", "send_g", "recv_g",
+)
 
 
 def mm(left, right):
@@ -35,6 +38,7 @@
 
 
 def twice(column):
+    column = column.astype(F32)
     return jnp.concatenate([column, column], axis=1)
 
 
@@ -78,9 +82,8 @@
 def whole_kernel(plan, names, *refs):
     ref = dict(zip(names, refs, strict=True))
     (
-        points, counts, cot, weights, momenta, averages,
-        states, point_grad, gradients, weights_new, momenta_new, averages_new,
-    ) = (ref[name] for name in names[:12])
+        points, counts, cot, weights, states, point_grad, gradients,
+    ) = (ref[name] for name in names[:7])
     rows, width, hidden = plan.rows, plan.width, plan.hidden
     seq_count, dp_count, zs, half = plan.seq, plan.dp, plan.zs, plan.half
     head_width = width // HEADS
@@ -228,7 +231,9 @@
             base = plan.base(layer)
             turned = jnp.transpose(flat[h, pl.ds(base, 128), :])
             for j in range(4):
-                norms[layer, j, lanes] = jnp.broadcast_to(turned[:, j : j + 1], (128, 128))
+                norms[layer, j, lanes] = jnp.broadcast_to(
+                    turned[:, j : j + 1], (128, 128)
+                ).astype(BF16)
             base += 4
             for j in range(3):
                 value = flat[h, pl.ds(base + j, width, stride=3), :]
@@ -251,22 +256,22 @@
             for j in range(parts):
                 bup[layer, width * j + 128 * h : width * j + 128 * (h + 1)] = jnp.broadcast_to(
                     turned[:, j : j + 1], (128, 128)
-                )
+                ).astype(BF16)
             base += parts
             value = flat[h, pl.ds(base, hidden), :]
             wd[layer, :, lanes] = value.astype(BF16)
             wd_t[layer, lanes] = jnp.transpose(value).astype(BF16)
 
-    column_mask = lax.broadcasted_iota(jnp.int32, (rows, 128), 1) < counts[0]
+    depth_mask = lax.broadcasted_iota(jnp.int32, (plan.depth, rows), 0) < counts[0]
     wide_points = ref["wide_points"]
     wide_points[...] = jnp.zeros_like(wide_points)
-    wide_points[:, : plan.depth] = points[...].astype(F32)
-    masked_t = jnp.transpose(jnp.where(column_mask, wide_points[...], 0.0)).astype(BF16)
+    wide_points[: plan.depth] = jnp.where(depth_mask, points[...].astype(F32), 0.0)
+    masked_t = wide_points[...].astype(BF16)
     ref["masked_t"][...] = masked_t
 
-    (gnorm, hid, nrm, qsave, kv, kt, vt, att, osave, lse, upd, nrm2, gp, act, emb, qmask, qtok, domask, dotok, ps, ds, peak, total, mixed, dq, gbuf, gemb, gin, send_n, recv_n, send_g, recv_g) = (
-        ref[n] for n in ("gnorm", "hid", "nrm", "qsave", "kv", "kt", "vt", "att", "osave", "lse", "upd", "nrm2", "gp", "act", "emb", "qmask", "qtok", "domask", "dotok", "ps", "ds", "peak", "total", "mixed", "dq", "gbuf", "gemb", "gin", "send_n", "recv_n", "send_g", "recv_g")
-    )
+    (
+        gnorm, hid, nrm, qsave, kv, kt, vt, att, osave, lse, upd, nrm2, gp, act, emb, qmask, domask, ps, ds, dqkv, grad_low, peak, total, gbuf, gemb, gin, send_n, recv_n, send_g, recv_g,
+    ) = (ref[n] for n in LOCAL)
     qmask[...] = jnp.zeros_like(qmask)
     domask[...] = jnp.zeros_like(domask)
     for sums in (gnorm, flat):
@@ -281,7 +286,6 @@
             flat[h, pl.ds(start, count, stride=stride), :] += value[:, lanes]
 
     ones = jnp.ones((16, rows), BF16)
-    column_head = lax.broadcasted_iota(jnp.int32, (rows, width), 1) // head_width
 
     embedded = mm(rit[...], ref["masked_t"][...]) + twice(rbias[...])
     emb[...] = embedded
@@ -311,40 +315,38 @@
         jnp.int32, (rows, rows), 1
     )
 
+    def mask_last(values, fill):
+        before = values.shape[0] - rows
+        last_block = jnp.where(causal, values[before:], fill)
+        return jnp.concatenate([values[:before], last_block], axis=0) if before else last_block
+
     def project_block(app, layer, block):
         block_t = nrm[app, block]
-        kt[app, block] = mm(wqkv_t[layer, width : 2 * width], block_t).astype(BF16)
-        vt[...] = mm(wqkv_t[layer, 2 * width :], block_t).astype(BF16)
-        kv[app, block] = mm(
+        places = slice(block * rows, (block + 1) * rows)
+        both = mm(wqkv_t[layer, width:], block_t).astype(BF16)
+        kt[app, :, places] = both[:width]
+        vt[:, places] = both[width:]
+        kv[app, places] = mm(
             jnp.transpose(block_t.astype(F32)).astype(BF16), wqkv[layer, :, width:]
         ).astype(BF16)
 
-    def attend_block(app, block, diagonal):
+    def attend(app, blocks):
+        keys = blocks * rows
         for head in range(HEADS):
             lanes = slice(head * head_width, (head + 1) * head_width)
-            scores = mm(kv[app, block, :, :width], qmask[head]) * exp_scale
-            if diagonal:
-                scores = jnp.where(causal, scores, -jnp.inf)
-                top = jnp.max(scores, axis=0, keepdims=True)
-                weight = jnp.exp2(scores - top)
-                total[head : head + 1] = jnp.sum(weight, axis=0, keepdims=True)
-                mixed[lanes] = mm(
-                    vt[lanes],
-                    weight.astype(BF16),
-                )
-            else:
-                old = peak[head : head + 1]
-                top = jnp.maximum(old, jnp.max(scores, axis=0, keepdims=True))
-                fade = jnp.exp2(old - top)
-                weight = jnp.exp2(scores - top)
-                total[head : head + 1] = total[head : head + 1] * fade + jnp.sum(
-                    weight, axis=0, keepdims=True
-                )
-                mixed[lanes] = mixed[lanes] * fade + mm(
-                    vt[lanes],
-                    weight.astype(BF16),
-                )
+            scores = mm(kv[app, :keys, :width], qmask[head]) * exp_scale
+            scores = mask_last(scores, -jnp.inf)
+            top = jnp.max(scores, axis=0, keepdims=True)
+            weight = jnp.exp2(scores - top)
             peak[head : head + 1] = top
+            total[head : head + 1] = jnp.sum(weight, axis=0, keepdims=True)
+            ps[head, :keys] = weight.astype(BF16)
+        for head in range(HEADS):
+            lanes = slice(head * head_width, (head + 1) * head_width)
+            out = mm(vt[lanes, :keys], ps[head, :keys]) * (1.0 / total[head : head + 1])
+            osave[app, lanes] = out
+            att[app, lanes] = out.astype(BF16)
+        lse[app] = peak[...] + jnp.log2(total[...])
 
     def forward(app, carry):
         layer = lax.rem(app, LAYERS)
@@ -362,23 +364,16 @@
         for head in range(HEADS):
             lanes = slice(head * head_width, (head + 1) * head_width)
             qmask[head, lanes] = queries[lanes]
-        project_block(app, layer, me)
-        attend_block(app, me, True)
-
-        def earlier(step, inner):
-            block = me - 1 - step
-            normed_copy(app, block, me).wait_recv()
-            project_block(app, layer, block)
-            attend_block(app, block, False)
-            return inner
-
-        lax.fori_loop(0, me, earlier, 0)
-        for head in range(HEADS):
-            lanes = slice(head * head_width, (head + 1) * head_width)
-            out = mixed[lanes] * (1.0 / total[head : head + 1])
-            osave[app, lanes] = out
-            att[app, lanes] = out.astype(BF16)
-        lse[app] = peak[...] + jnp.log2(total[...])
+        for place in range(seq_count):
+
+            @pl.when(me == place)
+            def _(place=place):
+                project_block(app, layer, place)
+                for block in range(place):
+                    normed_copy(app, block, me).wait_recv()
+                    project_block(app, layer, block)
+                attend(app, place + 1)
+
         updated = hid[app] + mm(wo_t[layer], att[app])
         upd[app] = updated
         unit, _ = normalise(updated)
@@ -405,30 +400,37 @@
     gbuf[...] = jnp.transpose(cot[...].astype(F32))
     gemb[...] = jnp.zeros_like(gemb)
 
-    def attend_back(app, layer, block, diagonal):
-        keys = kv[app, block, :, :width]
-        values = kv[app, block, :, width:]
+    def attend_back(app, layer, blocks):
+        keys = blocks * rows
+        own = slice(keys - rows, keys)
+        for head in range(HEADS):
+            scores = mm(kv[app, :keys, :width], qmask[head]) * exp_scale
+            weight = jnp.exp2(scores - lse[app, head : head + 1])
+            weight = mask_last(weight, 0.0)
+            ps[head, :keys] = weight.astype(BF16)
+            grad = mm(kv[app, :keys, width:], domask[head])
+            ds[head, :keys] = (weight * (grad - total[head : head + 1])).astype(BF16)
         for head in range(HEADS):
             lanes = slice(head * head_width, (head + 1) * head_width)
-            wide = slice(head * rows, (head + 1) * rows)
-            scores = mm(keys, qmask[head]) * exp_scale
-            weight = jnp.exp2(scores - lse[app, head : head + 1])
-            if diagonal:
-                weight = jnp.where(causal, weight, 0.0)
-            ps[:, wide] = weight.astype(BF16)
-            grad = mm(values, domask[head])
-            back = (weight * (grad - total[head : head + 1])).astype(BF16)
-            ds[:, wide] = back
-            part = mm(kt[app, block, lanes], back)
-            dq[lanes] = dq[lanes] + part
-        grad_keys = (mm(ds[...], qtok[...]) * score_scale).astype(BF16)
-        grad_values = mm(ps[...], dotok[...]).astype(BF16)
-        block_t = nrm[app, block]
-        accumulate(layer, 5, 3, mm(block_t, grad_keys))
-        accumulate(layer, 6, 3, mm(block_t, grad_values))
-        return mm_nt(wqkv[layer, :, width : 2 * width], grad_keys) + mm_nt(
-            wqkv[layer, :, 2 * width :], grad_values
-        )
+            below = slice(width + head * head_width, width + (head + 1) * head_width)
+            last_rows = slice(2 * width + head * head_width, 2 * width + (head + 1) * head_width)
+            dqkv[lanes, own] = (mm(kt[app, lanes, :keys], ds[head, :keys]) * score_scale).astype(BF16)
+            dqkv[below, :keys] = (
+                mm_nt(qsave[app, lanes], ds[head, :keys]) * score_scale
+            ).astype(BF16)
+            dqkv[last_rows, :keys] = mm_nt(grad_low[lanes], ps[head, :keys]).astype(BF16)
+        for block in range(blocks):
+            places = slice(block * rows, (block + 1) * rows)
+            first = 0 if block == blocks - 1 else width
+            grads = mm_nt(nrm[app, block], dqkv[first:, places])
+            for j in range(first // width, 3):
+                accumulate(layer, 4 + j, 3, grads[:, width * j - first : width * (j + 1) - first])
+            back = mm(wqkv[layer, :, first:], dqkv[first:, places])
+            if block == blocks - 1:
+                gin[...] = back
+            else:
+                nrm[app, block] = back.astype(BF16)
+                grad_copy(app, me, block).start()
 
     def backward(order, carry):
         app = APPS - 1 - order
@@ -451,6 +453,7 @@
         branch_low = grad_updated.astype(BF16)
         accumulate(layer, 4 + 3 * width, 1, mm_nt(att[app], branch_low))
         grad_att = mm(wo[layer], branch_low).astype(BF16)
+        grad_low[...] = grad_att
         for head in range(HEADS):
             lanes = slice(head * head_width, (head + 1) * head_width)
             domask[head, lanes] = grad_att[lanes]
@@ -458,24 +461,11 @@
             total[head : head + 1] = jnp.sum(
                 osave[app, lanes] * grad_att[lanes].astype(F32), axis=0, keepdims=True
             )
-        grad_tok = jnp.transpose(grad_att.astype(F32))
-        query_tok = jnp.transpose(qsave[app].astype(F32))
-        for head in range(HEADS):
-            wide = slice(head * rows, (head + 1) * rows)
-            dotok[wide] = jnp.where(column_head == head, grad_tok, 0.0).astype(BF16)
-            qtok[wide] = jnp.where(column_head == head, query_tok, 0.0).astype(BF16)
-        dq[...] = jnp.zeros_like(dq)
-
-        def earlier(block, inner):
-            nrm[app, block] = attend_back(app, layer, block, False).astype(BF16)
-            grad_copy(app, me, block).start()
-            return inner
-
-        lax.fori_loop(0, me, earlier, 0)
-        gin[...] = attend_back(app, layer, me, True)
-        grad_queries = (dq[...] * score_scale).astype(BF16)
-        accumulate(layer, 4, 3, mm_nt(nrm[app, me], grad_queries))
-        gin[...] += mm(wqkv[layer, :, :width], grad_queries)
+        for place in range(seq_count):
+
+            @pl.when(me == place)
+            def _(place=place):
+                attend_back(app, layer, place + 1)
 
         def later(source, inner):
             grad_copy(app, source, me).wait_recv()
@@ -498,8 +488,7 @@
     embed_low = gemb[...].astype(BF16)
     grad_in_rows = mm_nt(ref["masked_t"][...], embed_low)
     grad_bias_rows = mm_nt(ones, embed_low)
-    point_rows = jnp.where(column_mask, jnp.transpose(mm(rin[...], embed_low)), 0.0)
-    point_grad[...] = point_rows[:, : plan.depth]
+    point_grad[...] = jnp.where(depth_mask, mm(rin[...], embed_low)[: plan.depth], 0.0)
     for h in range(2):
         lanes = slice(128 * h, 128 * (h + 1))
         flat[h, : plan.depth] = grad_in_rows[: plan.depth, lanes]
@@ -604,15 +593,10 @@
         share_seq(lax.rem(me + step, seq_count), me).wait_recv()
     for h in range(2):
         for r, count in ((0, low_half), (1, high_half)):
-            gradients[pl.ds(2 * r * half + h, count, stride=2), :] = summed[h, r].astype(F32)[
+            ref["shared"][pl.ds(2 * r * half + h, count, stride=2), :] = summed[h, r].astype(F32)[
                 :count
             ]
-    grad = gradients[...]
-    momentum = MOMENTUM * momenta[...] + grad
-    momenta_new[...] = momentum
-    fresh = weights[...] - RATE * (grad + MOMENTUM * momentum)
-    weights_new[...] = fresh
-    averages_new[...] = AVERAGE_DECAY * averages[...] + (1.0 - AVERAGE_DECAY) * fresh
+    gradients[...] = ref["shared"][...].astype(BF16)
 
     each_other_z(lambda z: grad_z(my_z, z).wait_send())
     for step in range(1, seq_count):
@@ -644,14 +628,7 @@
     smem = pl.BlockSpec(memory_space=pltpu.SMEM)
     shape = jax.ShapeDtypeStruct
     lines = (share // 128, 128)
-    outs = (
-        shape((rows, width), BF16),
-        shape((rows, depth), F32),
-        shape(lines, F32),
-        shape(lines, F32),
-        shape(lines, F32),
-        shape(lines, F32),
-    )
+    outs = (shape((rows, width), BF16), shape((depth, rows), F32), shape(lines, BF16))
     low = lambda *dims: pltpu.VMEM(dims, BF16)
     full = lambda *dims: pltpu.VMEM(dims, F32)
     flags = lambda *dims: pltpu.SemaphoreType.DMA(dims)
@@ -661,8 +638,8 @@
         "rin": low(128, width),
         "rit": low(width, 128),
         "rbias": full(width, 128),
-        "norms": full(LAYERS, 4, width, 128),
-        "bup": full(LAYERS, hidden, 128),
+        "norms": low(LAYERS, 4, width, 128),
+        "bup": low(LAYERS, hidden, 128),
         "wqkv": low(LAYERS, width, 3 * width),
         "wqkv_t": low(LAYERS, 3 * width, width),
         "wo": low(LAYERS, width, width),
@@ -671,7 +648,7 @@
         "wup_t": low(LAYERS, hidden, width),
         "wd": low(LAYERS, hidden, width),
         "wd_t": low(LAYERS, width, hidden),
-        "wide_points": full(rows, 128),
+        "wide_points": full(128, rows),
         "masked_t": low(128, rows),
         "gnorm": full(LAYERS, 4, width, 128),
         "from_core": low(dp_count, 2, half, 128),
@@ -680,12 +657,13 @@
         "from_z": low(zs, half, 128),
         "last": full(half, 128),
         "summed": low(2, 2, half, 128),
+        "shared": full(share // 128, 128),
         "hid": full(APPS + 1, width, rows),
         "nrm": low(APPS, seq_count, width, rows),
         "qsave": low(APPS, width, rows),
-        "kv": low(APPS, seq_count, rows, 2 * width),
-        "kt": low(APPS, seq_count, width, rows),
-        "vt": low(width, rows),
+        "kv": low(APPS, seq_count * rows, 2 * width),
+        "kt": low(APPS, width, seq_count * rows),
+        "vt": low(width, seq_count * rows),
         "att": low(APPS, width, rows),
         "osave": full(APPS, width, rows),
         "lse": full(APPS, HEADS, rows),
@@ -695,15 +673,13 @@
         "act": low(APPS, hidden, rows),
         "emb": full(width, rows),
         "qmask": low(HEADS, width, rows),
-        "qtok": low(HEADS * rows, width),
         "domask": low(HEADS, width, rows),
-        "dotok": low(HEADS * rows, width),
-        "ps": low(rows, HEADS * rows),
-        "ds": low(rows, HEADS * rows),
+        "ps": low(HEADS, seq_count * rows, rows),
+        "ds": low(HEADS, seq_count * rows, rows),
+        "dqkv": low(3 * width, seq_count * rows),
+        "grad_low": low(width, rows),
         "peak": full(HEADS, rows),
         "total": full(HEADS, rows),
-        "mixed": full(width, rows),
-        "dq": full(width, rows),
         "gbuf": full(width, rows),
         "gemb": full(width, rows),
         "gin": full(width, rows),
@@ -731,24 +707,24 @@
         "recv_gs": flags(seq_count),
     }
     names = (
-        "points", "counts", "cot", "weights", "momenta", "averages",
-        "states", "point_grad", "gradients", "weights_new", "momenta_new", "averages_new",
+        "points", "counts", "cot", "weights", "states", "point_grad", "gradients",
         *scratch,
     )
-    states, point_grad, *vectors = pl.pallas_call(
+    states, point_grad, summed = pl.pallas_call(
         functools.partial(whole_kernel, plan, names),
         out_shape=outs,
-        in_specs=[vmem, smem, vmem, vmem, vmem, vmem],
+        in_specs=[vmem, smem, vmem, vmem],
         out_specs=(vmem,) * len(outs),
         scratch_shapes=list(scratch.values()),
         compiler_params=pltpu.CompilerParams(
             collective_id=0, has_side_effects=True, vmem_limit_bytes=63 * 1024 * 1024
         ),
-    )(
-        points[0], counts, cotangent[0],
-        weights.reshape(lines), momenta.reshape(lines), averages.reshape(lines),
-    )
-    return (states[None], point_grad[None], *(v.reshape(-1) for v in vectors))
+    )(points[0].T, counts, cotangent[0], weights.reshape(lines))
+    grad = summed.astype(F32)
+    momentum = MOMENTUM * momenta.reshape(lines) + grad
+    fresh = weights.reshape(lines) - RATE * (grad + MOMENTUM * momentum)
+    mean = AVERAGE_DECAY * averages.reshape(lines) + (1.0 - AVERAGE_DECAY) * fresh
+    return (states[None], point_grad.T[None], *(v.reshape(-1) for v in (grad, fresh, momentum, mean)))
 
 
 def solution(mesh):

time: 187 us -> 150 us (0.80)
  Pallas kernels: 173 us -> 140 us
  local copies, waits for them, and re-layouts: 9.67 us -> 2.11 us
  other arithmetic: 0 us -> 4.78 us
    pallas_call x1, Pallas kernels: 173 us -> 140 us  [shards(): pl.pallas_call(functools.partial(whole_kernel, plan, names), out_shape=ou...]
    unnamed x15 -> x10, local copies, waits for them, and re-layouts: 9.67 us -> 2.11 us
    reshape x0 -> x2, other arithmetic: none -> 4.78 us  [shards(): v.reshape(-1)]
where the time goes in v3:
time: 150 us; the launch traced here: 148 us
  Pallas kernels  140 us (93%)
  other arithmetic  4.78 us (3%)
  local copies, waits for them, and re-layouts  2.11 us (1%)
    pallas_call x1, Pallas kernels, shards(): pl.pallas_call(functools.partial(whole_kernel, plan, names), out_shape=ou...  140 us
    reshape x2, other arithmetic, shards(): v.reshape(-1)  4.78 us

profile of v3, /device:TPU:0, one launch (start us, length us, event | category | flops | bytes accessed | tf_op | source)
XLA Modules:
  0.0 147.7 jit_solution(15759603055743317470)
XLA Ops:
  1.3 0.0 copy-start.2
  1.3 139.5 %shard_map.109 = (bf16[256,256]{1,0:T(8,128)(2,1)}, f32[20,256]{1,0:T(8,128)}, bf16[1548,128]{1,0:T(8,128)(2,1)}) custom-call(bf16[20,256]{1,0:T(8,128)(2,1)} %bitcast.40, s32[1]{0:T(128)S(6)} %copy.14.refs_1_, bf16[256,256]{1,0:T(8,128)(2,1)} %bitcast.37, f32[1548,128]{1,0:T(8,128)} %bitcast.36), custom_call_target="tpu_custom_call" | custom-call | tf_op jit(solution)/shard_map/pallas_call | solution.py:713
  140.8 0.0 copy-start
  140.8 1.4 copy.12
  142.3 0.0 copy-start.1
  142.3 2.0 %convert_bitcast_fusion = f32[198144]{0:T(1024)} fusion(bf16[1548,128]{1,0:T(8,128)(2,1)} %get-tuple-element.11), kind=kLoop, calls=%fused_computation.2 | loop fusion | flops 198144 | bytes 1188864 | tf_op jit(solution)/shard_map/reshape | solution.py:727
  144.3 0.0 copy-done.2
  144.3 0.0 copy-done
  144.3 0.0 copy-done.1
  144.3 0.0 copy-start.3
  144.3 2.8 %fusion.2 = (f32[198144]{0:T(1024)}, f32[198144]{0:T(1024)}, f32[198144]{0:T(1024)}) fusion(f32[198144]{0:T(1024)S(1)} %copy-done.2, f32[198144]{0:T(1024)} %param.10, bf16[1548,128]{1,0:T(8,128)(2,1)S(1)} %copy-done.1, f32[198144]{0:T(1024)S(1)} %copy-done), kind=kLoop, calls=%fused_computation.6 | loop fusion | flops 1981440 | bytes 5151744 | tf_op jit(solution)/shard_map/reshape | solution.py:727
  147.1 0.0 copy-done.3
  147.1 0.7 copy.15
Async XLA Ops:
  1.3 143.0 %copy-start.2 = (f32[198144]{0:T(1024)S(1)}, f32[198144]{0:T(1024)}, u32[]{:S(2)}) copy-start(f32[198144]{0:T(1024)} %param.11) | copy-start | bytes 2377732
  140.8 3.5 %copy-start = (f32[198144]{0:T(1024)S(1)}, f32[198144]{0:T(1024)}, u32[]{:S(2)}) copy-start(f32[198144]{0:T(1024)} %param.9) | copy-start | bytes 2377732
  142.3 2.0 %copy-start.1 = (bf16[1548,128]{1,0:T(8,128)(2,1)S(1)}, bf16[1548,128]{1,0:T(8,128)(2,1)}, u32[]{:S(2)}) copy-start(bf16[1548,128]{1,0:T(8,128)(2,1)} %get-tuple-element.11) | copy-start | bytes 1188868
  144.3 2.8 %copy-start.3 = (bf16[256,256]{1,0:T(8,128)(2,1)S(1)}, bf16[256,256]{1,0:T(8,128)(2,1)}, u32[]{:S(2)}) copy-start(bf16[256,256]{1,0:T(8,128)(2,1)} %get-tuple-element.9) | copy-start | bytes 393220

commit v4 on v3

v4 whole, which is shorter than its diff:
```python
import functools
import math

import jax
import jax.numpy as jnp
from jax import lax
from jax.experimental import pallas as pl
from jax.experimental.pallas import tpu as pltpu
from jax.sharding import PartitionSpec as P

MESH = pl.DeviceIdType.MESH
HEADS = 8
FF = 1024
LAYERS = 2
LOOPS = 2
APPS = LAYERS * LOOPS

EPSILON = 1e-05
RATE = 0.0003
MOMENTUM = 0.5
AVERAGE_DECAY = 0.9

F32 = jnp.float32
BF16 = jnp.bfloat16
GELU_A = math.sqrt(2.0 / math.pi)
GELU_B = 0.044715
SEQ = 4
LOCAL = (
    "gnorm", "hid", "nrm", "qsave", "kv", "kt", "vt", "att", "osave", "lse", "upd", "nrm2", "gp",
    "act", "emb", "qmask", "domask", "ps", "ds", "dqkv", "grad_low", "peak", "total", "gbuf",
    "gemb", "gin", "held", "merge", "send_n", "recv_n", "send_g", "recv_g", "recv_m", "gathered",
    "flat",
)


def mm(left, right):
    return jnp.dot(left, right, preferred_element_type=F32)


def mm_nt(left, right):
    return lax.dot_general(left, right, (((1,), (1,)), ((), ())), preferred_element_type=F32)


def twice(column):
    column = column.astype(F32)
    return jnp.concatenate([column, column], axis=1)


def halves(values):
    return values[:, :128] + values[:, 128:]


def normalise(values):
    centred = values - jnp.mean(values, axis=0, keepdims=True)
    variance = jnp.mean(centred * centred, axis=0, keepdims=True)
    scale = lax.rsqrt(variance + EPSILON)
    return centred * scale, scale


def normalise_back(grad, unit, scale, gain):
    scaled = grad * gain
    first = jnp.mean(scaled, axis=0, keepdims=True)
    second = jnp.mean(scaled * unit, axis=0, keepdims=True)
    return (scaled - first - unit * second) * scale


class Plan:
    def __init__(self, rows, depth, width, share, dp_count, seq_count):
        self.rows = rows
        self.depth = depth
        self.width = width
        self.hidden = FF
        self.dp = dp_count
        self.zs = dp_count // 2
        self.seq = seq_count
        self.flat = share // width
        self.half = -(-self.flat // 32) * 16
        self.mixer = 4 + 3 * width + width
        self.block = self.mixer + FF + FF // width + FF
        self.total = self.flat * dp_count
        self.space = self.total + 32 + width
        self.used = self.base(LAYERS)
        self.reach = {
            (layer, part): min(self.zs, -(-(self.base(layer) + rows_here) // (2 * self.flat)))
            for layer in range(LAYERS)
            for part, rows_here in (("mixer", self.mixer), ("hidden", self.block))
        }
        self.reach[LAYERS - 1, "hidden"] = self.zs

    def base(self, layer):
        return self.depth + 1 + layer * self.block


def whole_kernel(plan, names, *refs):
    ref = dict(zip(names, refs, strict=True))
    (
        points, counts, cot, weights, states, point_grad, gradients,
    ) = (ref[name] for name in names[:7])
    rows, width, hidden = plan.rows, plan.width, plan.hidden
    dp_count, zs, half = plan.dp, plan.zs, plan.half
    head_width = width // HEADS
    exp_scale = math.log2(math.e) / math.sqrt(head_width)
    score_scale = 1.0 / math.sqrt(head_width)
    low_half, high_half = half, plan.flat - half
    (
        gnorm, hid, nrm, qsave, kv, kt, vt, att, osave, lse, upd, nrm2, gp, act, emb, qmask,
        domask, ps, ds, dqkv, grad_low, peak, total, gbuf, gemb, gin, held, merge,
        send_n, recv_n, send_g, recv_g, recv_m, gathered, flat,
    ) = (ref[n] for n in LOCAL)
    rin, rit, rbias, norms, bup = (ref[n] for n in ("rin", "rit", "rbias", "norms", "bup"))
    wqkv, wqkv_t, wo, wo_t = (ref[n] for n in ("wqkv", "wqkv_t", "wo", "wo_t"))
    wup, wup_t, wd, wd_t = (ref[n] for n in ("wup", "wup_t", "wd", "wd_t"))

    me = lax.axis_index("seq")
    owner = lax.axis_index("dp")
    my_z, my_x = owner // 2, lax.rem(owner, 2)
    my_y, my_c = me // 2, lax.rem(me, 2)
    sibling = {"seq": my_y * 2 + (1 - my_c)}
    across = {"seq": (1 - my_y) * 2 + my_c}
    here = my_x * 2 + my_y

    def in_plane(step):
        x = lax.rem(my_x + step // 2, 2)
        y = lax.rem(my_y + step % 2, 2)
        return x, y, {"dp": my_z * 2 + x, "seq": y * 2 + my_c}

    barrier = pltpu.get_barrier_semaphore()

    def greet(device):
        pl.semaphore_signal(barrier, inc=1, device_id=device, device_id_type=MESH)

    def greet_z(step, carry):
        greet({"dp": lax.rem(my_z + step, zs) * 2 + my_x})
        return carry

    for step in range(1, plan.seq):
        greet({"seq": lax.rem(me + step, plan.seq)})
    for step in (2, 3):
        greet(in_plane(step)[2])
    lax.fori_loop(1, zs, greet_z, 0)

    def remote(source, target, send, receive, device):
        return pltpu.make_async_remote_copy(
            src_ref=source, dst_ref=target, send_sem=send, recv_sem=receive,
            device_id=device, device_id_type=MESH,
        )

    def each(low, high, body):
        def step(z, carry):
            body(z)
            return carry

        lax.fori_loop(low, high, step, 0)

    def each_other_z(low, high, body):
        def step(z):
            @pl.when(z != my_z)
            def _():
                body(z)

        each(low, high, step)

    tail_rows = high_half // 16 * 16
    for h in range(2):
        for r, count in ((0, low_half), (1, tail_rows)):
            gathered[owner, h, r, :count] = weights[
                pl.ds(2 * r * half + h, count, stride=2), :
            ].astype(BF16)
        if high_half < half:
            gathered[owner, h, 1, tail_rows:] = jnp.concatenate(
                [
                    weights[pl.ds(2 * (half + tail_rows) + h, high_half - tail_rows, stride=2), :],
                    jnp.zeros((half - high_half, 128), F32),
                ],
                axis=0,
            ).astype(BF16)

    pl.semaphore_wait(barrier, plan.seq + zs)

    def weights_z(source_z, target_z):
        piece = gathered.at[2 * source_z + my_x, my_c, my_y]
        return remote(
            piece, piece, ref["send_wz"].at[target_z], ref["recv_wz"].at[source_z],
            {"dp": 2 * target_z + my_x},
        )

    def weights_plane_out(group, step):
        piece = gathered.at[2 * group + my_x, my_c, my_y]
        _, _, device = in_plane(step)
        return remote(
            piece, piece, ref["send_wp"].at[group, step], ref["recv_wp"].at[group, here], device
        )

    def weights_plane_in(group, step):
        x, y, device = in_plane(step)
        piece = gathered.at[2 * group + x, my_c, y]
        return remote(
            piece, piece, ref["send_wp"].at[group, step], ref["recv_wp"].at[group, x * 2 + y],
            device,
        )

    def weights_core(share, column):
        piece = gathered.at[share, column]
        return remote(piece, piece, ref["send_wc"].at[share], ref["recv_wc"].at[share], sibling)

    def own_group(group):
        @pl.when(group == my_z)
        def _():
            each_other_z(0, zs, lambda z: weights_z(group, z).start())
            for step in (2, 3):
                weights_plane_out(group, step).start()

    def forward_group(group):
        weights_z(group, my_z).wait_recv()
        for step in (1, 2, 3):
            weights_plane_out(group, step).start()

    def spread_group(group):
        own_group(group)

        @pl.when(group != my_z)
        def _():
            forward_group(group)

    def pass_group(group):
        @pl.when(group != my_z)
        def _():
            weights_plane_in(group, 1).wait_recv()
            weights_core(2 * group + my_x, my_c).start()

        for step in (2, 3):
            weights_plane_in(group, step).wait_recv()
        weights_core(2 * group + 1 - my_x, my_c).start()

    def take_group(group):
        @pl.when(group != my_z)
        def _():
            weights_core(2 * group + my_x, 1 - my_c).wait_recv()

        weights_core(2 * group + 1 - my_x, 1 - my_c).wait_recv()

    def unpack(low, high):
        for share in range(2 * low, 2 * high):
            for h in range(2):
                for r in range(2):
                    flat[h, pl.ds(share * plan.flat + r * half, half), :] = gathered[
                        share, h, r
                    ].astype(F32)

    def column_of(turned, j):
        return jnp.broadcast_to(turned[:, j : j + 1], (128, 128)).astype(BF16)

    def mixer_weights(layer):
        for h in range(2):
            lanes = slice(128 * h, 128 * (h + 1))
            base = plan.base(layer)
            turned = jnp.transpose(flat[h, pl.ds(base, 128), :])
            for j in range(4):
                norms[layer, j, lanes] = column_of(turned, j)
            base += 4
            for j in range(3):
                value = flat[h, pl.ds(base + j, width, stride=3), :]
                place = slice(width * j + 128 * h, width * j + 128 * (h + 1))
                wqkv[layer, :, place] = value.astype(BF16)
                wqkv_t[layer, place] = jnp.transpose(value).astype(BF16)
            base += 3 * width
            value = flat[h, pl.ds(base, width), :]
            wo[layer, :, lanes] = value.astype(BF16)
            wo_t[layer, lanes] = jnp.transpose(value).astype(BF16)

    parts = hidden // width

    def hidden_weights(layer):
        for h in range(2):
            lanes = slice(128 * h, 128 * (h + 1))
            base = plan.base(layer) + plan.mixer
            for j in range(parts):
                value = flat[h, pl.ds(base + j, width, stride=parts), :]
                place = slice(width * j + 128 * h, width * j + 128 * (h + 1))
                wup[layer, :, place] = value.astype(BF16)
                wup_t[layer, place] = jnp.transpose(value).astype(BF16)
            base += hidden
            turned = jnp.transpose(flat[h, pl.ds(base, 128), :])
            for j in range(parts):
                place = slice(width * j + 128 * h, width * j + 128 * (h + 1))
                bup[layer, place] = column_of(turned, j)
            base += parts
            value = flat[h, pl.ds(base, hidden), :]
            wd[layer, :, lanes] = value.astype(BF16)
            wd_t[layer, lanes] = jnp.transpose(value).astype(BF16)

    reach_a, reach_b = plan.reach[0, "mixer"], plan.reach[0, "hidden"]
    reach_c, reach_d = plan.reach[1, "mixer"], plan.reach[1, "hidden"]

    each(0, reach_a, spread_group)
    each(reach_a, reach_b, own_group)
    qmask[...] = jnp.zeros_like(qmask)
    domask[...] = jnp.zeros_like(domask)
    gnorm[...] = jnp.zeros_like(gnorm)
    gemb[...] = jnp.zeros_like(gemb)
    ones = jnp.ones((16, rows), BF16)
    depth_mask = lax.broadcasted_iota(jnp.int32, (plan.depth, rows), 0) < counts[0]
    wide_points = ref["wide_points"]
    wide_points[...] = jnp.zeros_like(wide_points)
    wide_points[: plan.depth] = jnp.where(depth_mask, points[...].astype(F32), 0.0)
    ref["masked_t"][...] = wide_points[...].astype(BF16)
    gbuf[...] = jnp.transpose(cot[...].astype(F32))
    each(0, reach_a, pass_group)
    each(0, reach_a, take_group)
    unpack(0, reach_a)

    depth_row = lax.broadcasted_iota(jnp.int32, (128, 128), 0)
    for h in range(2):
        lanes = slice(128 * h, 128 * (h + 1))
        block = flat[h, :128]
        turned = jnp.transpose(block)
        rbias[lanes] = jnp.broadcast_to(turned[:, plan.depth : plan.depth + 1], (128, 128))
        block = jnp.where(depth_row < plan.depth, block, 0.0)
        rin[:, lanes] = block.astype(BF16)
        rit[lanes] = jnp.transpose(block).astype(BF16)
    mixer_weights(0)

    embedded = mm(rit[...], ref["masked_t"][...]) + twice(rbias[...])
    emb[...] = embedded
    hid[0] = embedded

    def normed_copy(app, block, target, slot):
        return remote(
            nrm.at[app, block], nrm.at[app, block], send_n.at[app, slot], recv_n.at[app, block],
            {"seq": target},
        )

    def grad_copy(app, block, target, slot):
        return remote(
            nrm.at[app, block], nrm.at[app, me], send_g.at[app, slot], recv_g.at[app, me],
            {"seq": target},
        )

    def grad_arrival(app, source):
        return remote(
            nrm.at[app, source], nrm.at[app, source], send_g.at[app, 0], recv_g.at[app, source],
            {"seq": source},
        )

    def merge_copy(app, block):
        return remote(nrm.at[app, block], merge.at[app], send_g.at[app, 1], recv_m.at[app], sibling)

    causal = lax.broadcasted_iota(jnp.int32, (rows, rows), 0) <= lax.broadcasted_iota(
        jnp.int32, (rows, rows), 1
    )

    def mask_last(values, fill):
        before = values.shape[0] - rows
        last_block = jnp.where(causal, values[before:], fill)
        return jnp.concatenate([values[:before], last_block], axis=0) if before else last_block

    def project_block(app, layer, block):
        block_t = nrm[app, block]
        places = slice(block * rows, (block + 1) * rows)
        both = mm(wqkv_t[layer, width:], block_t).astype(BF16)
        kt[app, :, places] = both[:width]
        vt[:, places] = both[width:]
        kv[app, places] = mm(
            jnp.transpose(block_t.astype(F32)).astype(BF16), wqkv[layer, :, width:]
        ).astype(BF16)

    def attend(app, blocks):
        keys = blocks * rows
        for head in range(HEADS):
            scores = mm(kv[app, :keys, :width], qmask[head]) * exp_scale
            scores = mask_last(scores, -jnp.inf)
            top = jnp.max(scores, axis=0, keepdims=True)
            weight = jnp.exp2(scores - top)
            peak[head : head + 1] = top
            total[head : head + 1] = jnp.sum(weight, axis=0, keepdims=True)
            ps[head, :keys] = weight.astype(BF16)
        for head in range(HEADS):
            lanes = slice(head * head_width, (head + 1) * head_width)
            out = mm(vt[lanes, :keys], ps[head, :keys]) * (1.0 / total[head : head + 1])
            osave[app, lanes] = out
            att[app, lanes] = out.astype(BF16)
        lse[app] = peak[...] + jnp.log2(total[...])

    def gather_blocks(app, layer, place):
        project_block(app, layer, place)
        if place % 2 == 1:
            normed_copy(app, place - 1, me, 0).wait_recv()
            project_block(app, layer, place - 1)
        if place >= 2:
            near = place - 2
            far = 1 - near
            normed_copy(app, near, me, 0).wait_recv()
            normed_copy(app, near, place + 1 - 2 * (place % 2), 2).start()
            project_block(app, layer, near)
            normed_copy(app, far, me, 0).wait_recv()
            project_block(app, layer, far)

    def forward(app, carry):
        layer = lax.rem(app, LAYERS)

        @pl.when(app == 1)
        def _():
            each(reach_c, reach_d, pass_group)
            each(reach_b, reach_c, take_group)
            unpack(reach_b, reach_c)
            mixer_weights(1)

        unit, _ = normalise(hid[app])
        normed = (unit * twice(norms[layer, 0]) + twice(norms[layer, 1])).astype(BF16)
        nrm[app, me] = normed

        @pl.when(my_y == 0)
        def _():
            normed_copy(app, me, me + 2, 1).start()

        @pl.when(my_c == 0)
        def _():
            normed_copy(app, me, me + 1, 0).start()

        queries = mm(wqkv_t[layer, :width], normed).astype(BF16)
        qsave[app] = queries
        for head in range(HEADS):
            lanes = slice(head * head_width, (head + 1) * head_width)
            qmask[head, lanes] = queries[lanes]

        @pl.when(app == 0)
        def _():
            each_other_z(reach_a, reach_b, forward_group)
            each(reach_b, reach_d, own_group)

        for place in range(SEQ):

            @pl.when(me == place)
            def _(place=place):
                gather_blocks(app, layer, place)
                attend(app, place + 1)

        updated = hid[app] + mm(wo_t[layer], att[app])
        upd[app] = updated
        unit, _ = normalise(updated)
        second = (unit * twice(norms[layer, 2]) + twice(norms[layer, 3])).astype(BF16)
        nrm2[app] = second

        @pl.when(app == 0)
        def _():
            each(reach_a, reach_c, pass_group)
            each_other_z(reach_b, reach_d, forward_group)
            each(reach_a, reach_b, take_group)
            unpack(reach_a, reach_b)
            hidden_weights(0)

        @pl.when(app == 1)
        def _():
            each(reach_c, reach_d, take_group)
            unpack(reach_c, reach_d)
            hidden_weights(1)

        before = mm(wup_t[layer], nrm2[app]) + twice(bup[layer])
        squared = before * before
        inner = GELU_A * before * (1.0 + GELU_B * squared)
        turned = jnp.tanh(inner)
        risen = 0.5 * (1.0 + turned)
        act[app] = (before * risen).astype(BF16)
        gp[app] = risen + (0.5 * GELU_A) * before * (1.0 - turned * turned) * (
            1.0 + (3.0 * GELU_B) * squared
        )
        result = upd[app] + mm(wd_t[layer], act[app])
        again = jnp.where((layer == LAYERS - 1) & (app < APPS - 1), 1.0, 0.0)
        hid[app + 1] = result + again * emb[...]
        return carry

    lax.fori_loop(0, APPS, forward, 0)
    states[...] = jnp.transpose(hid[APPS]).astype(BF16)

    each_other_z(0, zs, lambda z: weights_z(my_z, z).wait_send())
    each_other_z(0, zs, lambda z: weights_plane_out(z, 1).wait_send())
    for step in (2, 3):
        each(0, zs, lambda z, step=step: weights_plane_out(z, step).wait_send())
    each_other_z(0, zs, lambda z: weights_core(2 * z + my_x, my_c).wait_send())
    each(0, zs, lambda z: weights_core(2 * z + 1 - my_x, my_c).wait_send())

    def normed_sent(app):
        @pl.when(my_c == 0)
        def _():
            normed_copy(app, me, me + 1, 0).wait_send()

        @pl.when(my_y == 0)
        def _():
            normed_copy(app, me, me + 2, 1).wait_send()

        @pl.when(my_y == 1)
        def _():
            normed_copy(app, my_c, my_y * 2 + 1 - my_c, 2).wait_send()

    each(0, APPS, normed_sent)
    flat[:, pl.ds(plan.used, plan.total - plan.used), :] = jnp.zeros(
        (2, plan.total - plan.used, 128), F32
    )

    from_core, from_plane, from_z = (ref[n] for n in ("from_core", "from_plane", "from_z"))
    last, summed = ref["last"], ref["summed"]

    def grads_core(group):
        pair = pl.ds(2 * group, 2)
        return remote(
            gathered.at[pair, 1 - my_c], from_core.at[pair],
            ref["send_gc"].at[group], ref["recv_gc"].at[group], sibling,
        )

    def grads_plane(group, step):
        x, y, device = in_plane(step)
        return remote(
            gathered.at[2 * group + x, my_c, y], from_plane.at[group, here],
            ref["send_gp"].at[group, step], ref["recv_gp"].at[group, here], device,
        )

    def grads_plane_in(group, step):
        x, y, device = in_plane(step)
        place = x * 2 + y
        return place, remote(
            gathered.at[2 * group + my_x, my_c, my_y], from_plane.at[group, place],
            ref["send_gp"].at[group, step], ref["recv_gp"].at[group, place], device,
        )

    def grads_z(source_z, target_z):
        return remote(
            gathered.at[2 * target_z + my_x, my_c, my_y], from_z.at[source_z],
            ref["send_gz"].at[target_z], ref["recv_gz"].at[source_z], {"dp": 2 * target_z + my_x},
        )

    def round_group(low, high):
        def body(group):
            for x in range(2):
                for h in range(2):
                    for r in range(2):
                        start = (2 * group + x) * plan.flat + r * half
                        gathered[2 * group + x, h, r] = flat[h, pl.ds(start, half), :].astype(BF16)
            grads_core(group).start()

        each(low, high, body)

    def plane_group(low, high):
        def body(group):
            grads_core(group).wait()
            for step in (3, 2, 1, 0):
                x, y, _ = in_plane(step)
                share = 2 * group + x
                gathered[share, my_c, y] = (
                    gathered[share, my_c, y].astype(F32) + from_core[share, y].astype(F32)
                ).astype(BF16)
                if step:
                    grads_plane(group, step).start()

        each(low, high, body)

    def rise_group(low, high):
        def body(group):
            value = gathered[2 * group + my_x, my_c, my_y].astype(F32)
            for step in (1, 2, 3):
                place, arrival = grads_plane_in(group, step)
                arrival.wait_recv()
                value = value + from_plane[group, place].astype(F32)
            gathered[2 * group + my_x, my_c, my_y] = value.astype(BF16)

            @pl.when(group != my_z)
            def _():
                grads_z(my_z, group).start()

            @pl.when(group == my_z)
            def _():
                last[...] = value

        each(low, high, body)

    def share_seq(source, target):
        piece = summed.at[lax.rem(source, 2), source // 2]
        return remote(
            piece, piece, ref["send_gs"].at[target], ref["recv_gs"].at[source], {"seq": target}
        )

    def collect(low, high):
        def body(z):
            grads_z(z, my_z).wait_recv()
            last[...] += from_z[z].astype(F32)

        def when_mine(group):
            @pl.when(group == my_z)
            def _():
                each_other_z(0, zs, body)
                summed[my_c, my_y] = last[...].astype(BF16)
                for step in range(1, SEQ):
                    share_seq(me, lax.rem(me + step, SEQ)).start()

        each(low, high, when_mine)

    def first_group(row):
        return min(zs, -(-row // (2 * plan.flat)))

    group_a = first_group(plan.base(1) + plan.mixer)
    group_b = first_group(plan.base(0) + plan.mixer)

    def accumulate(app, layer, offset, stride, value, again=False):
        start = plan.base(0) + layer * plan.block + offset
        count = value.shape[0]
        for h in range(2):
            place = (h, pl.ds(start, count, stride=stride), slice(None))
            part = value[:, 128 * h : 128 * (h + 1)]
            kept = flat[place]
            flat[place] = part + (kept if again else jnp.where(app < LAYERS, kept, 0.0))

    def attend_back(app, layer, blocks):
        keys = blocks * rows
        own = slice(keys - rows, keys)
        for head in range(HEADS):
            scores = mm(kv[app, :keys, :width], qmask[head]) * exp_scale
            weight = jnp.exp2(scores - lse[app, head : head + 1])
            weight = mask_last(weight, 0.0)
            ps[head, :keys] = weight.astype(BF16)
            grad = mm(kv[app, :keys, width:], domask[head])
            ds[head, :keys] = (weight * (grad - total[head : head + 1])).astype(BF16)
        for head in range(HEADS):
            lanes = slice(head * head_width, (head + 1) * head_width)
            key_lanes = slice(width + head * head_width, width + (head + 1) * head_width)
            value_lanes = slice(2 * width + head * head_width, 2 * width + (head + 1) * head_width)
            dqkv[lanes, own] = (mm(kt[app, lanes, :keys], ds[head, :keys]) * score_scale).astype(BF16)
            dqkv[key_lanes, :keys] = (
                mm_nt(qsave[app, lanes], ds[head, :keys]) * score_scale
            ).astype(BF16)
            dqkv[value_lanes, :keys] = mm_nt(grad_low[lanes], ps[head, :keys]).astype(BF16)
        place = blocks - 1
        order = [b for b in (1 - place % 2, place - 2, place - 1) if 0 <= b < place]
        order = [*dict.fromkeys(order), place]
        for block in order:
            places = slice(block * rows, (block + 1) * rows)
            first = 0 if block == place else width
            grads = mm_nt(nrm[app, block], dqkv[first:, places])
            for j in range(first // width, 3):
                accumulate(
                    app, layer, 4 + j, 3, grads[:, width * j - first : width * (j + 1) - first],
                    again=j > 0 and block != order[0],
                )
            back = mm(wqkv[layer, :, first:], dqkv[first:, places])
            if block == place:
                gin[...] = back
            elif block == place - 2:
                held[...] = back
            else:
                nrm[app, block] = back.astype(BF16)
                if place >= 2 and block == 1 - place % 2:
                    merge_copy(app, block).start()
                else:
                    grad_copy(app, block, block, 0).start()

    def flush_norms(layer):
        start = plan.base(0) + layer * plan.block
        for h in range(2):
            for j in range(4):
                flat[h, pl.ds(start + j, 1), :] = jnp.sum(
                    jnp.transpose(gnorm[layer, j, 128 * h : 128 * (h + 1)]), axis=0, keepdims=True
                )

    def backward(order, carry):
        app = APPS - 1 - order
        layer = lax.rem(app, LAYERS)
        out_low = gbuf[...].astype(BF16)
        accumulate(app, layer, plan.mixer + hidden + parts, 1, mm_nt(act[app], out_low))
        pre_low = (mm(wd[layer], out_low) * gp[app]).astype(BF16)
        act[app] = pre_low
        for j in range(parts):
            part = act[app, width * j : width * (j + 1)]
            accumulate(app, layer, plan.mixer + j, parts, mm_nt(nrm2[app], part))
            accumulate(app, layer, plan.mixer + hidden + j, 1, mm_nt(ones, part)[:1])

        @pl.when(app == 1)
        def _():
            round_group(group_a, zs)

        @pl.when(app == 0)
        def _():
            rise_group(group_a, zs)
            round_group(group_b, group_a)

        grad_second = mm(wup[layer], act[app])
        unit, scale = normalise(upd[app])
        gnorm[layer, 2] += halves(grad_second * unit)
        gnorm[layer, 3] += halves(grad_second)
        grad_updated = gbuf[...] + normalise_back(grad_second, unit, scale, twice(norms[layer, 2]))
        gbuf[...] = grad_updated
        branch_low = grad_updated.astype(BF16)
        accumulate(app, layer, 4 + 3 * width, 1, mm_nt(att[app], branch_low))
        grad_att = mm(wo[layer], branch_low).astype(BF16)
        grad_low[...] = grad_att
        for head in range(HEADS):
            lanes = slice(head * head_width, (head + 1) * head_width)
            domask[head, lanes] = grad_att[lanes]
            qmask[head, lanes] = qsave[app, lanes]
            total[head : head + 1] = jnp.sum(
                osave[app, lanes] * grad_att[lanes].astype(F32), axis=0, keepdims=True
            )

        @pl.when(app == 1)
        def _():
            plane_group(group_a, zs)

        @pl.when(app == 0)
        def _():
            plane_group(group_b, group_a)

        for place in range(SEQ):

            @pl.when(me == place)
            def _(place=place):
                attend_back(app, layer, place + 1)

        def arrive(source):
            grad_arrival(app, source).wait_recv()
            gin[...] += nrm[app, source].astype(F32)

        @pl.when(my_c == 0)
        def _():
            arrive(me + 1)

        @pl.when(my_y == 0)
        def _():
            arrive(me + 2)

        grad_normed = gin[...]
        unit, scale = normalise(hid[app])
        gnorm[layer, 0] += halves(grad_normed * unit)
        gnorm[layer, 1] += halves(grad_normed)
        grad_in = gbuf[...] + normalise_back(grad_normed, unit, scale, twice(norms[layer, 0]))
        gbuf[...] = grad_in
        first = jnp.where(layer == 0, 1.0, 0.0)
        gemb[...] += first * grad_in

        @pl.when(my_y == 1)
        def _():
            merge_copy(app, my_c).wait_recv()
            nrm[app, my_c] = (held[...] + merge[app].astype(F32)).astype(BF16)
            grad_copy(app, my_c, my_c, 2).start()

        @pl.when(app < LAYERS)
        def _():
            flush_norms(layer)

        return carry

    lax.fori_loop(0, APPS, backward, 0)
    embed_low = gemb[...].astype(BF16)
    grad_in_rows = mm_nt(ref["masked_t"][...], embed_low)
    grad_bias_rows = mm_nt(ones, embed_low)
    for h in range(2):
        lanes = slice(128 * h, 128 * (h + 1))
        flat[h, : plan.depth] = grad_in_rows[: plan.depth, lanes]
        flat[h, plan.depth : plan.depth + 1] = grad_bias_rows[:1, lanes]
    round_group(0, group_b)
    point_grad[...] = jnp.where(depth_mask, mm(rin[...], embed_low)[: plan.depth], 0.0)
    rise_group(group_b, group_a)
    plane_group(0, group_b)
    collect(group_b, zs)
    rise_group(0, group_b)
    collect(0, group_b)
    for step in range(1, SEQ):
        share_seq(lax.rem(me + step, SEQ), me).wait_recv()
    for h in range(2):
        for r, count in ((0, low_half), (1, high_half)):
            ref["shared"][pl.ds(2 * r * half + h, count, stride=2), :] = summed[h, r].astype(F32)[
                :count
            ]
    gradients[...] = ref["shared"][...].astype(BF16)

    for step in (1, 2, 3):
        each(0, zs, lambda z, step=step: grads_plane(z, step).wait_send())
    each_other_z(0, zs, lambda z: grads_z(my_z, z).wait_send())
    for step in range(1, SEQ):
        share_seq(me, lax.rem(me + step, SEQ)).wait_send()

    def finish(app):
        @pl.when(my_c == 1)
        def _():
            grad_copy(app, me - 1, me - 1, 0).wait_send()

        @pl.when(my_y == 1)
        def _():
            merge_copy(app, 1 - my_c).wait_send()
            grad_copy(app, my_c, my_c, 2).wait_send()

    each(0, APPS, finish)


def update_kernel(
    summed, weights, momenta, averages, states, point_grad,
    grad_out, fresh_out, momentum_out, mean_out, states_out, point_out,
):
    grad = summed[...].astype(F32)
    momentum = MOMENTUM * momenta[...] + grad
    fresh = weights[...] - RATE * (grad + MOMENTUM * momentum)
    grad_out[...] = grad
    momentum_out[...] = momentum
    fresh_out[...] = fresh
    mean_out[...] = AVERAGE_DECAY * averages[...] + (1.0 - AVERAGE_DECAY) * fresh

    @pl.when(pl.program_id(0) == 0)
    def _():
        states_out[...] = states[...]
        for row in range(point_grad.shape[0]):
            point_out[row] = point_grad[row : row + 1]


def shards(points, counts, cotangent, weights, momenta, averages):
    rows, depth = points.shape[1:]
    width = cotangent.shape[2]
    share = weights.shape[0]
    plan = Plan(rows, depth, width, share, lax.axis_size("dp"), lax.axis_size("seq"))
    hidden, dp_count, zs, half = plan.hidden, plan.dp, plan.zs, plan.half
    vmem = pl.BlockSpec(memory_space=pltpu.VMEM)
    smem = pl.BlockSpec(memory_space=pltpu.SMEM)
    shape = jax.ShapeDtypeStruct
    lines = (share // 128, 128)
    outs = (shape((rows, width), BF16), shape((depth, rows), F32), shape(lines, BF16))
    low = lambda *dims: pltpu.VMEM(dims, BF16)
    full = lambda *dims: pltpu.VMEM(dims, F32)
    flags = lambda *dims: pltpu.SemaphoreType.DMA(dims)
    scratch = {
        "gathered": low(dp_count, 2, 2, half, 128),
        "flat": full(2, plan.space, 128),
        "rin": low(128, width),
        "rit": low(width, 128),
        "rbias": full(width, 128),
        "norms": low(LAYERS, 4, width, 128),
        "bup": low(LAYERS, hidden, 128),
        "wqkv": low(LAYERS, width, 3 * width),
        "wqkv_t": low(LAYERS, 3 * width, width),
        "wo": low(LAYERS, width, width),
        "wo_t": low(LAYERS, width, width),
        "wup": low(LAYERS, width, hidden),
        "wup_t": low(LAYERS, hidden, width),
        "wd": low(LAYERS, hidden, width),
        "wd_t": low(LAYERS, width, hidden),
        "wide_points": full(128, rows),
        "masked_t": low(128, rows),
        "gnorm": full(LAYERS, 4, width, 128),
        "from_core": low(dp_count, 2, half, 128),
        "from_plane": low(zs, 4, half, 128),
        "from_z": low(zs, half, 128),
        "last": full(half, 128),
        "summed": low(2, 2, half, 128),
        "shared": full(share // 128, 128),
        "hid": full(APPS + 1, width, rows),
        "nrm": low(APPS, SEQ, width, rows),
        "qsave": low(APPS, width, rows),
        "kv": low(APPS, SEQ * rows, 2 * width),
        "kt": low(APPS, width, SEQ * rows),
        "vt": low(width, SEQ * rows),
        "att": low(APPS, width, rows),
        "osave": full(APPS, width, rows),
        "lse": full(APPS, HEADS, rows),
        "upd": full(APPS, width, rows),
        "nrm2": low(APPS, width, rows),
        "gp": full(APPS, hidden, rows),
        "act": low(APPS, hidden, rows),
        "emb": full(width, rows),
        "qmask": low(HEADS, width, rows),
        "domask": low(HEADS, width, rows),
        "ps": low(HEADS, SEQ * rows, rows),
        "ds": low(HEADS, SEQ * rows, rows),
        "dqkv": low(3 * width, SEQ * rows),
        "grad_low": low(width, rows),
        "peak": full(HEADS, rows),
        "total": full(HEADS, rows),
        "gbuf": full(width, rows),
        "gemb": full(width, rows),
        "gin": full(width, rows),
        "held": full(width, rows),
        "merge": low(APPS, width, rows),
        "send_n": flags(APPS, 3),
        "recv_n": flags(APPS, SEQ),
        "send_g": flags(APPS, 3),
        "recv_g": flags(APPS, SEQ),
        "recv_m": flags(APPS),
        "send_wz": flags(zs),
        "recv_wz": flags(zs),
        "send_wp": flags(zs, 4),
        "recv_wp": flags(zs, 4),
        "send_wc": flags(dp_count),
        "recv_wc": flags(dp_count),
        "send_gc": flags(zs),
        "recv_gc": flags(zs),
        "send_gp": flags(zs, 4),
        "recv_gp": flags(zs, 4),
        "send_gz": flags(zs),
        "recv_gz": flags(zs),
        "send_gs": flags(SEQ),
        "recv_gs": flags(SEQ),
    }
    names = (
        "points", "counts", "cot", "weights", "states", "point_grad", "gradients", *scratch,
    )
    mine = weights.reshape(lines)
    states, point_grad, summed = pl.pallas_call(
        functools.partial(whole_kernel, plan, names),
        out_shape=outs,
        in_specs=[vmem, smem, vmem, vmem],
        out_specs=(vmem,) * len(outs),
        scratch_shapes=list(scratch.values()),
        compiler_params=pltpu.CompilerParams(
            collective_id=0, has_side_effects=True, vmem_limit_bytes=63 * 1024 * 1024
        ),
    )(points[0].T, counts, cotangent[0], mine)
    vector = shape(lines, F32)
    step_rows = min(512, lines[0])
    line_block = pl.BlockSpec((step_rows, 128), lambda i: (i, 0))
    states_block = pl.BlockSpec((rows, width), lambda i: (0, 0))
    point_block = pl.BlockSpec((depth, rows), lambda i: (0, 0))
    grad, fresh, momentum, mean, states, point_grad = pl.pallas_call(
        update_kernel,
        grid=(-(-lines[0] // step_rows),),
        out_shape=(
            vector, vector, vector, vector, shape((rows, width), BF16), shape((depth, 1, rows), F32),
        ),
        in_specs=[line_block] * 4 + [states_block, point_block],
        out_specs=(
            line_block, line_block, line_block, line_block, states_block,
            pl.BlockSpec((depth, 1, rows), lambda i: (0, 0, 0)),
        ),
        compiler_params=pltpu.CompilerParams(vmem_limit_bytes=63 * 1024 * 1024),
    )(summed, mine, momenta.reshape(lines), averages.reshape(lines), states, point_grad)
    return (
        states[None], jnp.transpose(point_grad, (1, 2, 0)),
        *(v.reshape(-1) for v in (grad, fresh, momentum, mean)),
    )


def solution(mesh):
    placed = (P("dp", "seq", None), P("dp"), P("dp", "seq", None), P("dp"), P("dp"), P("dp"))
    return jax.shard_map(
        shards,
        mesh=mesh,
        in_specs=placed,
        out_specs=(P("dp", "seq", None), P("dp", "seq", None), P("dp"), P("dp"), P("dp"), P("dp")),
        check_vma=False,
    )
```

time: 150 us -> 139 us (0.927); the launches traced: 148 us -> 138 us
  other arithmetic: 4.78 us -> 0 us
  Pallas kernels: 140 us -> 137 us
  local copies, waits for them, and re-layouts: 2.11 us -> 0 us
    pallas_call x1, Pallas kernels: 140 us -> 133 us  [shards(): pl.pallas_call(functools.partial(whole_kernel, plan, names), out_shape=ou...]
    reshape x2 -> x0, other arithmetic: 4.78 us -> none  [shards(): v.reshape(-1)]
    pallas_call x0 -> x1, Pallas kernels: none -> 4.44 us  [shards(): pl.pallas_call(update_kernel, grid=(-(-lines[0] // step_rows),), out_shap...]
    unnamed x10 -> x0, local copies, waits for them, and re-layouts: 2.11 us -> none
where the time goes in v4:
time: 139 us; the launch traced here: 138 us
  Pallas kernels  137 us (99%)
  between operations  1.45 us (1%)
    pallas_call x1, Pallas kernels, shards(): pl.pallas_call(functools.partial(whole_kernel, plan, names), out_shape=ou...  133 us
    pallas_call x1, Pallas kernels, shards(): pl.pallas_call(update_kernel, grid=(-(-lines[0] // step_rows),), out_shap...  4.44 us

profile of v4, /device:TPU:0, one launch (start us, length us, event | category | flops | bytes accessed | tf_op | source)
XLA Modules:
  0.0 138.4 jit_solution(11913377381137099707)
XLA Ops:
  1.3 132.6 %shard_map.109 = (bf16[256,256]{1,0:T(8,128)(2,1)}, f32[20,256]{1,0:T(8,128)}, bf16[1548,128]{1,0:T(8,128)(2,1)}) custom-call(bf16[20,256]{1,0:T(8,128)(2,1)} %bitcast.18, s32[1]{0:T(128)S(6)} %copy.12.refs_1_, bf16[256,256]{1,0:T(8,128)(2,1)} %bitcast.17, f32[1548,128]{1,0:T(8,128)} %bitcast.13), custom_call_target="tpu_custom_call" | custom-call | tf_op jit(solution)/shard_map/pallas_call | solution.py:900
  133.8 4.4 %shard_map.110 = (f32[1548,128]{1,0:T(8,128)}, f32[1548,128]{1,0:T(8,128)}, f32[1548,128]{1,0:T(8,128)}, f32[1548,128]{1,0:T(8,128)}, bf16[256,256]{1,0:T(8,128)(2,1)}, /*index=5*/f32[20,1,256]{2,1,0:T(1,128)}) custom-call(bf16[1548,128]{1,0:T(8,128)(2,1)} %get-tuple-element.15.summed, f32[1548,128]{1,0:T(8,128)} %bitcast.14, f32[1548,128]{1,0:T(8,128)} %bitcast.15, ...), custom_call_target="tpu_custom_call" | custom-call | tf_op jit(solution)/shard_map/pallas_call | solution.py:915

commit v5 on v4

--- a/solution.py
+++ b/solution.py
@@ -28,7 +28,7 @@
 LOCAL = (
     "gnorm", "hid", "nrm", "qsave", "kv", "kt", "vt", "att", "osave", "lse", "upd", "nrm2", "gp",
     "act", "emb", "qmask", "domask", "ps", "ds", "dqkv", "grad_low", "peak", "total", "gbuf",
-    "gemb", "gin", "held", "merge", "send_n", "recv_n", "send_g", "recv_g", "recv_m", "gathered",
+    "gemb", "gin", "merge", "send_n", "recv_n", "send_g", "recv_g", "recv_m", "gathered",
     "flat",
 )
 
@@ -74,11 +74,11 @@
         self.zs = dp_count // 2
         self.seq = seq_count
         self.flat = share // width
-        self.half = -(-self.flat // 32) * 16
+        self.quarter = -(-self.flat // 64) * 16
         self.mixer = 4 + 3 * width + width
         self.block = self.mixer + FF + FF // width + FF
         self.total = self.flat * dp_count
-        self.space = self.total + 32 + width
+        self.space = self.total + 64 + width
         self.used = self.base(LAYERS)
         self.reach = {
             (layer, part): min(self.zs, -(-(self.base(layer) + rows_here) // (2 * self.flat)))
@@ -97,14 +97,15 @@
         points, counts, cot, weights, states, point_grad, gradients,
     ) = (ref[name] for name in names[:7])
     rows, width, hidden = plan.rows, plan.width, plan.hidden
-    dp_count, zs, half = plan.dp, plan.zs, plan.half
+    dp_count, zs, quarter = plan.dp, plan.zs, plan.quarter
     head_width = width // HEADS
     exp_scale = math.log2(math.e) / math.sqrt(head_width)
     score_scale = 1.0 / math.sqrt(head_width)
-    low_half, high_half = half, plan.flat - half
+    quarters = [(r, w, (2 * r + w) * quarter) for r in range(2) for w in range(2)]
+    waves = range(2)
     (
         gnorm, hid, nrm, qsave, kv, kt, vt, att, osave, lse, upd, nrm2, gp, act, emb, qmask,
-        domask, ps, ds, dqkv, grad_low, peak, total, gbuf, gemb, gin, held, merge,
+        domask, ps, ds, dqkv, grad_low, peak, total, gbuf, gemb, gin, merge,
         send_n, recv_n, send_g, recv_g, recv_m, gathered, flat,
     ) = (ref[n] for n in LOCAL)
     rin, rit, rbias, norms, bup = (ref[n] for n in ("rin", "rit", "rbias", "norms", "bup"))
@@ -160,91 +161,114 @@
 
         each(low, high, step)
 
-    tail_rows = high_half // 16 * 16
     for h in range(2):
-        for r, count in ((0, low_half), (1, tail_rows)):
-            gathered[owner, h, r, :count] = weights[
-                pl.ds(2 * r * half + h, count, stride=2), :
-            ].astype(BF16)
-        if high_half < half:
-            gathered[owner, h, 1, tail_rows:] = jnp.concatenate(
-                [
-                    weights[pl.ds(2 * (half + tail_rows) + h, high_half - tail_rows, stride=2), :],
-                    jnp.zeros((half - high_half, 128), F32),
-                ],
-                axis=0,
-            ).astype(BF16)
+        for r, w, start in quarters:
+            count = min(quarter, plan.flat - start)
+            whole_rows = count // 16 * 16
+            if whole_rows:
+                gathered[owner, h, r, w, :whole_rows] = weights[
+                    pl.ds(2 * start + h, whole_rows, stride=2), :
+                ].astype(BF16)
+            if whole_rows < quarter:
+                rest = [jnp.zeros((quarter - count, 128), F32)]
+                if whole_rows < count:
+                    begin = 2 * (start + whole_rows) + h
+                    rest = [weights[pl.ds(begin, count - whole_rows, stride=2), :], *rest]
+                gathered[owner, h, r, w, whole_rows:] = jnp.concatenate(rest, axis=0).astype(BF16)
+
+    depth_mask = lax.broadcasted_iota(jnp.int32, (plan.depth, rows), 0) < counts[0]
+    gin[...] = jnp.zeros_like(gin)
+    gin[: plan.depth] = jnp.where(depth_mask, points[...].astype(F32), 0.0)
+    masked_all = ref["masked_all"]
+    masked_all[me] = gin[:128].astype(BF16)
 
     pl.semaphore_wait(barrier, plan.seq + zs)
 
-    def weights_z(source_z, target_z):
-        piece = gathered.at[2 * source_z + my_x, my_c, my_y]
-        return remote(
-            piece, piece, ref["send_wz"].at[target_z], ref["recv_wz"].at[source_z],
+    def points_copy(source, target):
+        piece = masked_all.at[source]
+        return remote(
+            piece, piece, ref["send_p"].at[target], ref["recv_p"].at[source], {"seq": target}
+        )
+
+    for step in range(1, SEQ):
+
+        @pl.when(me + step < SEQ)
+        def _(step=step):
+            points_copy(me, me + step).start()
+
+    def weights_z(source_z, target_z, w):
+        piece = gathered.at[2 * source_z + my_x, my_c, my_y, w]
+        return remote(
+            piece, piece, ref["send_wz"].at[target_z, w], ref["recv_wz"].at[source_z, w],
             {"dp": 2 * target_z + my_x},
         )
 
-    def weights_plane_out(group, step):
-        piece = gathered.at[2 * group + my_x, my_c, my_y]
+    def weights_plane_out(group, step, w):
+        piece = gathered.at[2 * group + my_x, my_c, my_y, w]
         _, _, device = in_plane(step)
         return remote(
-            piece, piece, ref["send_wp"].at[group, step], ref["recv_wp"].at[group, here], device
-        )
-
-    def weights_plane_in(group, step):
+            piece, piece, ref["send_wp"].at[group, step, w], ref["recv_wp"].at[group, here, w],
+            device,
+        )
+
+    def weights_plane_in(group, step, w):
         x, y, device = in_plane(step)
-        piece = gathered.at[2 * group + x, my_c, y]
-        return remote(
-            piece, piece, ref["send_wp"].at[group, step], ref["recv_wp"].at[group, x * 2 + y],
-            device,
-        )
-
-    def weights_core(share, column):
-        piece = gathered.at[share, column]
-        return remote(piece, piece, ref["send_wc"].at[share], ref["recv_wc"].at[share], sibling)
-
-    def own_group(group):
-        @pl.when(group == my_z)
-        def _():
-            each_other_z(0, zs, lambda z: weights_z(group, z).start())
+        piece = gathered.at[2 * group + x, my_c, y, w]
+        return remote(
+            piece, piece, ref["send_wp"].at[group, step, w],
+            ref["recv_wp"].at[group, x * 2 + y, w], device,
+        )
+
+    def weights_core(share, column, w):
+        piece = gathered.at[share, column, :, w]
+        return remote(
+            piece, piece, ref["send_wc"].at[share, w], ref["recv_wc"].at[share, w], sibling
+        )
+
+    def send_near():
+        for w in waves:
             for step in (2, 3):
-                weights_plane_out(group, step).start()
+                weights_plane_out(my_z, step, w).start()
+        for w in waves:
+            each(0, my_z, lambda z, w=w: weights_z(my_z, z, w).start())
+
+    def send_up():
+        for w in waves:
+            each(0, zs - 1 - my_z, lambda i, w=w: weights_z(my_z, zs - 1 - i, w).start())
 
     def forward_group(group):
-        weights_z(group, my_z).wait_recv()
-        for step in (1, 2, 3):
-            weights_plane_out(group, step).start()
-
-    def spread_group(group):
-        own_group(group)
-
-        @pl.when(group != my_z)
-        def _():
-            forward_group(group)
+        for w in waves:
+            weights_z(group, my_z, w).wait_recv()
+            for step in (1, 2, 3):
+                weights_plane_out(group, step, w).start()
 
     def pass_group(group):
-        @pl.when(group != my_z)
-        def _():
-            weights_plane_in(group, 1).wait_recv()
-            weights_core(2 * group + my_x, my_c).start()
-
-        for step in (2, 3):
-            weights_plane_in(group, step).wait_recv()
-        weights_core(2 * group + 1 - my_x, my_c).start()
+        for w in waves:
+
+            @pl.when(group != my_z)
+            def _(w=w):
+                weights_plane_in(group, 1, w).wait_recv()
+                weights_core(2 * group + my_x, my_c, w).start()
+
+            for step in (2, 3):
+                weights_plane_in(group, step, w).wait_recv()
+            weights_core(2 * group + 1 - my_x, my_c, w).start()
 
     def take_group(group):
-        @pl.when(group != my_z)
-        def _():
-            weights_core(2 * group + my_x, 1 - my_c).wait_recv()
-
-        weights_core(2 * group + 1 - my_x, 1 - my_c).wait_recv()
+        for w in waves:
+
+            @pl.when(group != my_z)
+            def _(w=w):
+                weights_core(2 * group + my_x, 1 - my_c, w).wait_recv()
+
+            weights_core(2 * group + 1 - my_x, 1 - my_c, w).wait_recv()
 
     def unpack(low, high):
         for share in range(2 * low, 2 * high):
             for h in range(2):
-                for r in range(2):
-                    flat[h, pl.ds(share * plan.flat + r * half, half), :] = gathered[
-                        share, h, r
+                for r, w, start in quarters:
+                    flat[h, pl.ds(share * plan.flat + start, quarter), :] = gathered[
+                        share, h, r, w
                     ].astype(F32)
 
     def column_of(turned, j):
@@ -292,20 +316,38 @@
     reach_a, reach_b = plan.reach[0, "mixer"], plan.reach[0, "hidden"]
     reach_c, reach_d = plan.reach[1, "mixer"], plan.reach[1, "hidden"]
 
-    each(0, reach_a, spread_group)
-    each(reach_a, reach_b, own_group)
+    def first_groups(group):
+        @pl.when(group == my_z)
+        def _():
+            send_up()
+
+        @pl.when(group != my_z)
+        def _():
+            forward_group(group)
+
+    send_near()
+    each(0, reach_a, first_groups)
+
+    @pl.when(my_z >= reach_a)
+    def _():
+        send_up()
+
+    @pl.when(my_z < reach_a)
+    def _():
+        each(reach_a, reach_b, forward_group)
+
     qmask[...] = jnp.zeros_like(qmask)
     domask[...] = jnp.zeros_like(domask)
     gnorm[...] = jnp.zeros_like(gnorm)
     gemb[...] = jnp.zeros_like(gemb)
     ones = jnp.ones((16, rows), BF16)
-    depth_mask = lax.broadcasted_iota(jnp.int32, (plan.depth, rows), 0) < counts[0]
-    wide_points = ref["wide_points"]
-    wide_points[...] = jnp.zeros_like(wide_points)
-    wide_points[: plan.depth] = jnp.where(depth_mask, points[...].astype(F32), 0.0)
-    ref["masked_t"][...] = wide_points[...].astype(BF16)
     gbuf[...] = jnp.transpose(cot[...].astype(F32))
     each(0, reach_a, pass_group)
+
+    @pl.when(my_z >= reach_a)
+    def _():
+        each_other_z(reach_a, reach_b, forward_group)
+
     each(0, reach_a, take_group)
     unpack(0, reach_a)
 
@@ -320,7 +362,7 @@
         rit[lanes] = jnp.transpose(block).astype(BF16)
     mixer_weights(0)
 
-    embedded = mm(rit[...], ref["masked_t"][...]) + twice(rbias[...])
+    embedded = mm(rit[...], masked_all[me]) + twice(rbias[...])
     emb[...] = embedded
     hid[0] = embedded
 
@@ -342,8 +384,13 @@
             {"seq": source},
         )
 
-    def merge_copy(app, block):
-        return remote(nrm.at[app, block], merge.at[app], send_g.at[app, 1], recv_m.at[app], sibling)
+    def turn_of(app):
+        return pl.ds(pl.multiple_of(app * rows, rows), rows)
+
+    def merge_copy(app):
+        return remote(
+            vt.at[:, turn_of(app)], merge.at[app], send_g.at[app, 1], recv_m.at[app], sibling
+        )
 
     causal = lax.broadcasted_iota(jnp.int32, (rows, rows), 0) <= lax.broadcasted_iota(
         jnp.int32, (rows, rows), 1
@@ -381,18 +428,39 @@
             att[app, lanes] = out.astype(BF16)
         lse[app] = peak[...] + jnp.log2(total[...])
 
+    def first_normed(block):
+        points_copy(block, me).wait_recv()
+        unit, _ = normalise(mm(rit[...], masked_all[block]) + twice(rbias[...]))
+        nrm[0, block] = (unit * twice(norms[0, 0]) + twice(norms[0, 1])).astype(BF16)
+
     def gather_blocks(app, layer, place):
         project_block(app, layer, place)
+        near, far = place - 2, 1 - (place - 2)
+
+        @pl.when(app == 0)
+        def _():
+            each(0, place, first_normed)
+
         if place % 2 == 1:
-            normed_copy(app, place - 1, me, 0).wait_recv()
+
+            @pl.when(app > 0)
+            def _():
+                normed_copy(app, place - 1, me, 0).wait_recv()
+
             project_block(app, layer, place - 1)
         if place >= 2:
-            near = place - 2
-            far = 1 - near
-            normed_copy(app, near, me, 0).wait_recv()
-            normed_copy(app, near, place + 1 - 2 * (place % 2), 2).start()
+
+            @pl.when(app > 0)
+            def _():
+                normed_copy(app, near, me, 0).wait_recv()
+                normed_copy(app, near, place + 1 - 2 * (place % 2), 2).start()
+
             project_block(app, layer, near)
-            normed_copy(app, far, me, 0).wait_recv()
+
+            @pl.when(app > 0)
+            def _():
+                normed_copy(app, far, me, 0).wait_recv()
+
             project_block(app, layer, far)
 
     def forward(app, carry):
@@ -409,11 +477,11 @@
         normed = (unit * twice(norms[layer, 0]) + twice(norms[layer, 1])).astype(BF16)
         nrm[app, me] = normed
 
-        @pl.when(my_y == 0)
+        @pl.when((my_y == 0) & (app > 0))
         def _():
             normed_copy(app, me, me + 2, 1).start()
 
-        @pl.when(my_c == 0)
+        @pl.when((my_c == 0) & (app > 0))
         def _():
             normed_copy(app, me, me + 1, 0).start()
 
@@ -422,11 +490,6 @@
         for head in range(HEADS):
             lanes = slice(head * head_width, (head + 1) * head_width)
             qmask[head, lanes] = queries[lanes]
-
-        @pl.when(app == 0)
-        def _():
-            each_other_z(reach_a, reach_b, forward_group)
-            each(reach_b, reach_d, own_group)
 
         for place in range(SEQ):
 
@@ -472,12 +535,19 @@
     lax.fori_loop(0, APPS, forward, 0)
     states[...] = jnp.transpose(hid[APPS]).astype(BF16)
 
-    each_other_z(0, zs, lambda z: weights_z(my_z, z).wait_send())
-    each_other_z(0, zs, lambda z: weights_plane_out(z, 1).wait_send())
-    for step in (2, 3):
-        each(0, zs, lambda z, step=step: weights_plane_out(z, step).wait_send())
-    each_other_z(0, zs, lambda z: weights_core(2 * z + my_x, my_c).wait_send())
-    each(0, zs, lambda z: weights_core(2 * z + 1 - my_x, my_c).wait_send())
+    for w in waves:
+        each_other_z(0, zs, lambda z, w=w: weights_z(my_z, z, w).wait_send())
+        each_other_z(0, zs, lambda z, w=w: weights_plane_out(z, 1, w).wait_send())
+        for step in (2, 3):
+            each(0, zs, lambda z, step=step, w=w: weights_plane_out(z, step, w).wait_send())
+        each_other_z(0, zs, lambda z, w=w: weights_core(2 * z + my_x, my_c, w).wait_send())
+        each(0, zs, lambda z, w=w: weights_core(2 * z + 1 - my_x, my_c, w).wait_send())
+    for step in range(1, SEQ):
+
+        @pl.when(me + step < SEQ)
+        def _(step=step):
+            points_copy(me, me + step).wait_send()
+
 
     def normed_sent(app):
         @pl.when(my_c == 0)
@@ -492,7 +562,7 @@
         def _():
             normed_copy(app, my_c, my_y * 2 + 1 - my_c, 2).wait_send()
 
-    each(0, APPS, normed_sent)
+    each(1, APPS, normed_sent)
     flat[:, pl.ds(plan.used, plan.total - plan.used), :] = jnp.zeros(
         (2, plan.total - plan.used, 128), F32
     )
@@ -500,96 +570,104 @@
     from_core, from_plane, from_z = (ref[n] for n in ("from_core", "from_plane", "from_z"))
     last, summed = ref["last"], ref["summed"]
 
-    def grads_core(group):
+    def grads_core(group, w):
         pair = pl.ds(2 * group, 2)
         return remote(
-            gathered.at[pair, 1 - my_c], from_core.at[pair],
-            ref["send_gc"].at[group], ref["recv_gc"].at[group], sibling,
-        )
-
-    def grads_plane(group, step):
+            gathered.at[pair, 1 - my_c, :, w], from_core.at[pair, :, w],
+            ref["send_gc"].at[group, w], ref["recv_gc"].at[group, w], sibling,
+        )
+
+    def grads_plane(group, step, w):
         x, y, device = in_plane(step)
         return remote(
-            gathered.at[2 * group + x, my_c, y], from_plane.at[group, here],
-            ref["send_gp"].at[group, step], ref["recv_gp"].at[group, here], device,
-        )
-
-    def grads_plane_in(group, step):
+            gathered.at[2 * group + x, my_c, y, w], from_plane.at[group, here, w],
+            ref["send_gp"].at[group, step, w], ref["recv_gp"].at[group, here, w], device,
+        )
+
+    def grads_plane_in(group, step, w):
         x, y, device = in_plane(step)
         place = x * 2 + y
         return place, remote(
-            gathered.at[2 * group + my_x, my_c, my_y], from_plane.at[group, place],
-            ref["send_gp"].at[group, step], ref["recv_gp"].at[group, place], device,
-        )
-
-    def grads_z(source_z, target_z):
-        return remote(
-            gathered.at[2 * target_z + my_x, my_c, my_y], from_z.at[source_z],
-            ref["send_gz"].at[target_z], ref["recv_gz"].at[source_z], {"dp": 2 * target_z + my_x},
+            gathered.at[2 * group + my_x, my_c, my_y, w], from_plane.at[group, place, w],
+            ref["send_gp"].at[group, step, w], ref["recv_gp"].at[group, place, w], device,
+        )
+
+    def grads_z(source_z, target_z, w):
+        return remote(
+            gathered.at[2 * target_z + my_x, my_c, my_y, w], from_z.at[source_z, w],
+            ref["send_gz"].at[target_z, w], ref["recv_gz"].at[source_z, w],
+            {"dp": 2 * target_z + my_x},
         )
 
     def round_group(low, high):
         def body(group):
-            for x in range(2):
+            for w in waves:
                 for h in range(2):
-                    for r in range(2):
-                        start = (2 * group + x) * plan.flat + r * half
-                        gathered[2 * group + x, h, r] = flat[h, pl.ds(start, half), :].astype(BF16)
-            grads_core(group).start()
+                    for x in range(2):
+                        for r in range(2):
+                            start = (2 * group + x) * plan.flat + (2 * r + w) * quarter
+                            gathered[2 * group + x, h, r, w] = flat[
+                                h, pl.ds(start, quarter), :
+                            ].astype(BF16)
+                grads_core(group, w).start()
 
         each(low, high, body)
 
     def plane_group(low, high):
         def body(group):
-            grads_core(group).wait()
-            for step in (3, 2, 1, 0):
-                x, y, _ = in_plane(step)
-                share = 2 * group + x
-                gathered[share, my_c, y] = (
-                    gathered[share, my_c, y].astype(F32) + from_core[share, y].astype(F32)
-                ).astype(BF16)
-                if step:
-                    grads_plane(group, step).start()
+            for w in waves:
+                grads_core(group, w).wait()
+                for step in (3, 2, 1, 0):
+                    x, y, _ = in_plane(step)
+                    share = 2 * group + x
+                    gathered[share, my_c, y, w] = (
+                        gathered[share, my_c, y, w].astype(F32) + from_core[share, y, w].astype(F32)
+                    ).astype(BF16)
+                    if step:
+                        grads_plane(group, step, w).start()
 
         each(low, high, body)
 
     def rise_group(low, high):
         def body(group):
-            value = gathered[2 * group + my_x, my_c, my_y].astype(F32)
-            for step in (1, 2, 3):
-                place, arrival = grads_plane_in(group, step)
-                arrival.wait_recv()
-                value = value + from_plane[group, place].astype(F32)
-            gathered[2 * group + my_x, my_c, my_y] = value.astype(BF16)
-
-            @pl.when(group != my_z)
-            def _():
-                grads_z(my_z, group).start()
-
-            @pl.when(group == my_z)
-            def _():
-                last[...] = value
+            for w in waves:
+                value = gathered[2 * group + my_x, my_c, my_y, w].astype(F32)
+                for step in (1, 2, 3):
+                    place, arrival = grads_plane_in(group, step, w)
+                    arrival.wait_recv()
+                    value = value + from_plane[group, place, w].astype(F32)
+                gathered[2 * group + my_x, my_c, my_y, w] = value.astype(BF16)
+
+                @pl.when(group != my_z)
+                def _(w=w):
+                    grads_z(my_z, group, w).start()
+
+                @pl.when(group == my_z)
+                def _(w=w, value=value):
+                    last[w] = value
 
         each(low, high, body)
 
-    def share_seq(source, target):
-        piece = summed.at[lax.rem(source, 2), source // 2]
-        return remote(
-            piece, piece, ref["send_gs"].at[target], ref["recv_gs"].at[source], {"seq": target}
+    def share_sum(kind, w, column, half, device):
+        piece = summed.at[column, half, w]
+        return remote(
+            piece, piece, ref["send_gs"].at[kind, w], ref["recv_gs"].at[kind, w], device
         )
 
     def collect(low, high):
-        def body(z):
-            grads_z(z, my_z).wait_recv()
-            last[...] += from_z[z].astype(F32)
-
         def when_mine(group):
             @pl.when(group == my_z)
             def _():
-                each_other_z(0, zs, body)
-                summed[my_c, my_y] = last[...].astype(BF16)
-                for step in range(1, SEQ):
-                    share_seq(me, lax.rem(me + step, SEQ)).start()
+                for w in waves:
+
+                    def body(z, w=w):
+                        grads_z(z, my_z, w).wait_recv()
+                        last[w] += from_z[z, w].astype(F32)
+
+                    each_other_z(0, zs, body)
+                    summed[my_c, my_y, w] = last[w].astype(BF16)
+                    share_sum(1, w, my_c, my_y, across).start()
+                    share_sum(0, w, my_c, my_y, sibling).start()
 
         each(low, high, when_mine)
 
@@ -598,6 +676,7 @@
 
     group_a = first_group(plan.base(1) + plan.mixer)
     group_b = first_group(plan.base(0) + plan.mixer)
+    group_m = (group_a + group_b + 1) // 2
 
     def accumulate(app, layer, offset, stride, value, again=False):
         start = plan.base(0) + layer * plan.block + offset
@@ -608,48 +687,72 @@
             kept = flat[place]
             flat[place] = part + (kept if again else jnp.where(app < LAYERS, kept, 0.0))
 
-    def attend_back(app, layer, blocks):
-        keys = blocks * rows
-        own = slice(keys - rows, keys)
+    part_q, held = emb, hid.at[APPS]
+
+    def soften_back(app, keys, diagonal):
         for head in range(HEADS):
-            scores = mm(kv[app, :keys, :width], qmask[head]) * exp_scale
+            scores = mm(kv[app, keys, :width], qmask[head]) * exp_scale
             weight = jnp.exp2(scores - lse[app, head : head + 1])
-            weight = mask_last(weight, 0.0)
-            ps[head, :keys] = weight.astype(BF16)
-            grad = mm(kv[app, :keys, width:], domask[head])
-            ds[head, :keys] = (weight * (grad - total[head : head + 1])).astype(BF16)
+            if diagonal:
+                weight = mask_last(weight, 0.0)
+            ps[head, keys] = weight.astype(BF16)
+            grad = mm(kv[app, keys, width:], domask[head])
+            ds[head, keys] = (weight * (grad - total[head : head + 1])).astype(BF16)
+
+    def heads_back(app, keys, own, added):
         for head in range(HEADS):
             lanes = slice(head * head_width, (head + 1) * head_width)
             key_lanes = slice(width + head * head_width, width + (head + 1) * head_width)
             value_lanes = slice(2 * width + head * head_width, 2 * width + (head + 1) * head_width)
-            dqkv[lanes, own] = (mm(kt[app, lanes, :keys], ds[head, :keys]) * score_scale).astype(BF16)
-            dqkv[key_lanes, :keys] = (
-                mm_nt(qsave[app, lanes], ds[head, :keys]) * score_scale
+            dqkv[key_lanes, keys] = (
+                mm_nt(qsave[app, lanes], ds[head, keys]) * score_scale
             ).astype(BF16)
-            dqkv[value_lanes, :keys] = mm_nt(grad_low[lanes], ps[head, :keys]).astype(BF16)
-        place = blocks - 1
-        order = [b for b in (1 - place % 2, place - 2, place - 1) if 0 <= b < place]
-        order = [*dict.fromkeys(order), place]
-        for block in order:
-            places = slice(block * rows, (block + 1) * rows)
-            first = 0 if block == place else width
-            grads = mm_nt(nrm[app, block], dqkv[first:, places])
-            for j in range(first // width, 3):
-                accumulate(
-                    app, layer, 4 + j, 3, grads[:, width * j - first : width * (j + 1) - first],
-                    again=j > 0 and block != order[0],
-                )
-            back = mm(wqkv[layer, :, first:], dqkv[first:, places])
-            if block == place:
-                gin[...] = back
-            elif block == place - 2:
-                held[...] = back
+            dqkv[value_lanes, keys] = mm_nt(grad_low[lanes], ps[head, keys]).astype(BF16)
+            part = mm(kt[app, lanes, keys], ds[head, keys])
+            if own is None:
+                part_q[lanes] = part
             else:
-                nrm[app, block] = back.astype(BF16)
-                if place >= 2 and block == 1 - place % 2:
-                    merge_copy(app, block).start()
-                else:
-                    grad_copy(app, block, block, 0).start()
+                part = part + part_q[lanes] if added else part
+                dqkv[lanes, own] = (part * score_scale).astype(BF16)
+
+    def span_of(low, high):
+        return slice(low * rows, high * rows)
+
+    def normed_back(layer, first, block):
+        return mm(wqkv[layer, :, first:], dqkv[first:, span_of(block, block + 1)])
+
+    def weights_back(app, layer, first, block, again):
+        grads = mm_nt(nrm[app, block], dqkv[first:, span_of(block, block + 1)])
+        for j in range(first // width, 3):
+            accumulate(
+                app, layer, 4 + j, 3, grads[:, width * j - first : width * (j + 1) - first],
+                again=j > 0 and again,
+            )
+
+    def attend_back(app, layer, place):
+        start = place // 2 * 2
+        if start:
+            kept, passed = place % 2, 1 - place % 2
+            soften_back(app, span_of(0, start), False)
+            heads_back(app, span_of(0, start), None, False)
+            vt[:, turn_of(app)] = normed_back(layer, width, passed).astype(BF16)
+            merge_copy(app).start()
+            held[...] = normed_back(layer, width, kept)
+            weights_back(app, layer, width, passed, False)
+            weights_back(app, layer, width, kept, True)
+        soften_back(app, span_of(start, place + 1), True)
+        if start:
+            merge_copy(app).wait_recv()
+            nrm[app, kept] = (held[...] + merge[app].astype(F32)).astype(BF16)
+            grad_copy(app, kept, kept, 2).start()
+        heads_back(app, span_of(start, place + 1), span_of(place, place + 1), bool(start))
+        if place % 2:
+            back = normed_back(layer, width, place - 1).astype(BF16)
+            weights_back(app, layer, width, place - 1, bool(start))
+            nrm[app, place - 1] = back
+            grad_copy(app, place - 1, place - 1, 0).start()
+        gin[...] = normed_back(layer, 0, place)
+        weights_back(app, layer, 0, place, bool(start) or place % 2 == 1)
 
     def flush_norms(layer):
         start = plan.base(0) + layer * plan.block
@@ -704,13 +807,17 @@
 
         @pl.when(app == 0)
         def _():
-            plane_group(group_b, group_a)
+            plane_group(group_m, group_a)
 
         for place in range(SEQ):
 
             @pl.when(me == place)
             def _(place=place):
-                attend_back(app, layer, place + 1)
+                attend_back(app, layer, place)
+
+        @pl.when(app == 0)
+        def _():
+            plane_group(group_b, group_m)
 
         def arrive(source):
             grad_arrival(app, source).wait_recv()
@@ -733,12 +840,6 @@
         first = jnp.where(layer == 0, 1.0, 0.0)
         gemb[...] += first * grad_in
 
-        @pl.when(my_y == 1)
-        def _():
-            merge_copy(app, my_c).wait_recv()
-            nrm[app, my_c] = (held[...] + merge[app].astype(F32)).astype(BF16)
-            grad_copy(app, my_c, my_c, 2).start()
-
         @pl.when(app < LAYERS)
         def _():
             flush_norms(layer)
@@ -747,7 +848,7 @@
 
     lax.fori_loop(0, APPS, backward, 0)
     embed_low = gemb[...].astype(BF16)
-    grad_in_rows = mm_nt(ref["masked_t"][...], embed_low)
+    grad_in_rows = mm_nt(masked_all[me], embed_low)
     grad_bias_rows = mm_nt(ones, embed_low)
     for h in range(2):
         lanes = slice(128 * h, 128 * (h + 1))
@@ -755,25 +856,34 @@
         flat[h, plan.depth : plan.depth + 1] = grad_bias_rows[:1, lanes]
     round_group(0, group_b)
     point_grad[...] = jnp.where(depth_mask, mm(rin[...], embed_low)[: plan.depth], 0.0)
-    rise_group(group_b, group_a)
+    rise_group(group_m, group_a)
     plane_group(0, group_b)
-    collect(group_b, zs)
+    rise_group(group_b, group_m)
     rise_group(0, group_b)
-    collect(0, group_b)
-    for step in range(1, SEQ):
-        share_seq(lax.rem(me + step, SEQ), me).wait_recv()
+    collect(0, zs)
+    for w in waves:
+        share_sum(1, w, my_c, 1 - my_y, across).wait_recv()
+        share_sum(2, w, my_c, 1 - my_y, sibling).start()
+    for w in waves:
+        share_sum(0, w, 1 - my_c, my_y, sibling).wait_recv()
+    for w in waves:
+        share_sum(2, w, 1 - my_c, 1 - my_y, sibling).wait_recv()
     for h in range(2):
-        for r, count in ((0, low_half), (1, high_half)):
-            ref["shared"][pl.ds(2 * r * half + h, count, stride=2), :] = summed[h, r].astype(F32)[
-                :count
-            ]
-    gradients[...] = ref["shared"][...].astype(BF16)
-
-    for step in (1, 2, 3):
-        each(0, zs, lambda z, step=step: grads_plane(z, step).wait_send())
-    each_other_z(0, zs, lambda z: grads_z(my_z, z).wait_send())
-    for step in range(1, SEQ):
-        share_seq(me, lax.rem(me + step, SEQ)).wait_send()
+        for r, w, start in quarters:
+            count = min(quarter, plan.flat - start)
+            if count > 0:
+                flat[0, pl.ds(2 * start + h, count, stride=2), :] = summed[h, r, w].astype(F32)[
+                    :count
+                ]
+    gradients[...] = flat[0, : gradients.shape[0]].astype(BF16)
+
+    for w in waves:
+        for step in (1, 2, 3):
+            each(0, zs, lambda z, step=step, w=w: grads_plane(z, step, w).wait_send())
+        each_other_z(0, zs, lambda z, w=w: grads_z(my_z, z, w).wait_send())
+        share_sum(0, w, my_c, my_y, sibling).wait_send()
+        share_sum(1, w, my_c, my_y, across).wait_send()
+        share_sum(2, w, my_c, 1 - my_y, sibling).wait_send()
 
     def finish(app):
         @pl.when(my_c == 1)
@@ -782,7 +892,7 @@
 
         @pl.when(my_y == 1)
         def _():
-            merge_copy(app, 1 - my_c).wait_send()
+            merge_copy(app).wait_send()
             grad_copy(app, my_c, my_c, 2).wait_send()
 
     each(0, APPS, finish)
@@ -812,7 +922,7 @@
     width = cotangent.shape[2]
     share = weights.shape[0]
     plan = Plan(rows, depth, width, share, lax.axis_size("dp"), lax.axis_size("seq"))
-    hidden, dp_count, zs, half = plan.hidden, plan.dp, plan.zs, plan.half
+    hidden, dp_count, zs, quarter = plan.hidden, plan.dp, plan.zs, plan.quarter
     vmem = pl.BlockSpec(memory_space=pltpu.VMEM)
     smem = pl.BlockSpec(memory_space=pltpu.SMEM)
     shape = jax.ShapeDtypeStruct
@@ -822,7 +932,7 @@
     full = lambda *dims: pltpu.VMEM(dims, F32)
     flags = lambda *dims: pltpu.SemaphoreType.DMA(dims)
     scratch = {
-        "gathered": low(dp_count, 2, 2, half, 128),
+        "gathered": low(dp_count, 2, 2, 2, quarter, 128),
         "flat": full(2, plan.space, 128),
         "rin": low(128, width),
         "rit": low(width, 128),
@@ -837,15 +947,13 @@
         "wup_t": low(LAYERS, hidden, width),
         "wd": low(LAYERS, hidden, width),
         "wd_t": low(LAYERS, width, hidden),
-        "wide_points": full(128, rows),
-        "masked_t": low(128, rows),
+        "masked_all": low(SEQ, 128, rows),
         "gnorm": full(LAYERS, 4, width, 128),
-        "from_core": low(dp_count, 2, half, 128),
-        "from_plane": low(zs, 4, half, 128),
-        "from_z": low(zs, half, 128),
-        "last": full(half, 128),
-        "summed": low(2, 2, half, 128),
-        "shared": full(share // 128, 128),
+        "from_core": low(dp_count, 2, 2, quarter, 128),
+        "from_plane": low(zs, 4, 2, quarter, 128),
+        "from_z": low(zs, 2, quarter, 128),
+        "last": full(2, quarter, 128),
+        "summed": low(2, 2, 2, quarter, 128),
         "hid": full(APPS + 1, width, rows),
         "nrm": low(APPS, SEQ, width, rows),
         "qsave": low(APPS, width, rows),
@@ -871,27 +979,28 @@
         "gbuf": full(width, rows),
         "gemb": full(width, rows),
         "gin": full(width, rows),
-        "held": full(width, rows),
         "merge": low(APPS, width, rows),
         "send_n": flags(APPS, 3),
         "recv_n": flags(APPS, SEQ),
         "send_g": flags(APPS, 3),
         "recv_g": flags(APPS, SEQ),
         "recv_m": flags(APPS),
-        "send_wz": flags(zs),
-        "recv_wz": flags(zs),
-        "send_wp": flags(zs, 4),
-        "recv_wp": flags(zs, 4),
-        "send_wc": flags(dp_count),
-        "recv_wc": flags(dp_count),
-        "send_gc": flags(zs),
-        "recv_gc": flags(zs),
-        "send_gp": flags(zs, 4),
-        "recv_gp": flags(zs, 4),
-        "send_gz": flags(zs),
-        "recv_gz": flags(zs),
-        "send_gs": flags(SEQ),
-        "recv_gs": flags(SEQ),
+        "send_p": flags(SEQ),
+        "recv_p": flags(SEQ),
+        "send_wz": flags(zs, 2),
+        "recv_wz": flags(zs, 2),
+        "send_wp": flags(zs, 4, 2),
+        "recv_wp": flags(zs, 4, 2),
+        "send_wc": flags(dp_count, 2),
+        "recv_wc": flags(dp_count, 2),
+        "send_gc": flags(zs, 2),
+        "recv_gc": flags(zs, 2),
+        "send_gp": flags(zs, 4, 2),
+        "recv_gp": flags(zs, 4, 2),
+        "send_gz": flags(zs, 2),
+        "recv_gz": flags(zs, 2),
+        "send_gs": flags(3, 2),
+        "recv_gs": flags(3, 2),
     }
     names = (
         "points", "counts", "cot", "weights", "states", "point_grad", "gradients", *scratch,

time: 139 us -> 128 us (0.921)
  Pallas kernels: 137 us -> 126 us
    pallas_call x1, Pallas kernels: 133 us -> 122 us  [shards(): pl.pallas_call(functools.partial(whole_kernel, plan, names), out_shape=ou...]
where the time goes in v5:
time: 128 us
  Pallas kernels  126 us (98%)
  between operations  1.45 us (1%)
    pallas_call x1, Pallas kernels, shards(): pl.pallas_call(functools.partial(whole_kernel, plan, names), out_shape=ou...  122 us
    pallas_call x1, Pallas kernels, shards(): pl.pallas_call(update_kernel, grid=(-(-lines[0] // step_rows),), out_shap...  4.44 us

profile of v5, /device:TPU:0, one launch (start us, length us, event | category | flops | bytes accessed | tf_op | source)
XLA Modules:
  0.0 127.6 jit_solution(3762545766238758136)
XLA Ops:
  1.3 121.7 %shard_map.109 = (bf16[256,256]{1,0:T(8,128)(2,1)}, f32[20,256]{1,0:T(8,128)}, bf16[1548,128]{1,0:T(8,128)(2,1)}) custom-call(bf16[20,256]{1,0:T(8,128)(2,1)} %bitcast.18, s32[1]{0:T(128)S(6)} %copy.12.refs_1_, bf16[256,256]{1,0:T(8,128)(2,1)} %bitcast.17, f32[1548,128]{1,0:T(8,128)} %bitcast.13), custom_call_target="tpu_custom_call" | custom-call | tf_op jit(solution)/shard_map/pallas_call | solution.py:1009
  123.0 4.4 %shard_map.110 = (f32[1548,128]{1,0:T(8,128)}, f32[1548,128]{1,0:T(8,128)}, f32[1548,128]{1,0:T(8,128)}, f32[1548,128]{1,0:T(8,128)}, bf16[256,256]{1,0:T(8,128)(2,1)}, /*index=5*/f32[20,1,256]{2,1,0:T(1,128)}) custom-call(bf16[1548,128]{1,0:T(8,128)(2,1)} %get-tuple-element.15.summed, f32[1548,128]{1,0:T(8,128)} %bitcast.14, f32[1548,128]{1,0:T(8,128)} %bitcast.15, ...), custom_call_target="tpu_custom_call" | custom-call | tf_op jit(solution)/shard_map/pallas_call | solution.py:1024

commit v6 on v5

--- a/solution.py
+++ b/solution.py
@@ -1,5 +1,6 @@
 import functools
 import math
+import types
 
 import jax
 import jax.numpy as jnp
@@ -25,12 +26,7 @@
 GELU_A = math.sqrt(2.0 / math.pi)
 GELU_B = 0.044715
 SEQ = 4
-LOCAL = (
-    "gnorm", "hid", "nrm", "qsave", "kv", "kt", "vt", "att", "osave", "lse", "upd", "nrm2", "gp",
-    "act", "emb", "qmask", "domask", "ps", "ds", "dqkv", "grad_low", "peak", "total", "gbuf",
-    "gemb", "gin", "merge", "send_n", "recv_n", "send_g", "recv_g", "recv_m", "gathered",
-    "flat",
-)
+FIRST = 32
 
 
 def mm(left, right):
@@ -86,16 +82,21 @@
             for part, rows_here in (("mixer", self.mixer), ("hidden", self.block))
         }
         self.reach[LAYERS - 1, "hidden"] = self.zs
+        self.late = [(0, self.base(0) + 4)]
+        group, spill = divmod(self.base(1), 2 * self.flat)
+        if group and 0 < spill <= FIRST:
+            self.late.append((group, spill))
+            self.settled = group
+        else:
+            self.settled = min(self.zs, -(-self.base(1) // (2 * self.flat)))
 
     def base(self, layer):
         return self.depth + 1 + layer * self.block
 
 
 def whole_kernel(plan, names, *refs):
-    ref = dict(zip(names, refs, strict=True))
-    (
-        points, counts, cot, weights, states, point_grad, gradients,
-    ) = (ref[name] for name in names[:7])
+    points, counts, cot, weights, states, point_grad, gradients, *scratch = refs
+    ref = types.SimpleNamespace(**dict(zip(names, scratch, strict=True)))
     rows, width, hidden = plan.rows, plan.width, plan.hidden
     dp_count, zs, quarter = plan.dp, plan.zs, plan.quarter
     head_width = width // HEADS
@@ -103,14 +104,24 @@
     score_scale = 1.0 / math.sqrt(head_width)
     quarters = [(r, w, (2 * r + w) * quarter) for r in range(2) for w in range(2)]
     waves = range(2)
-    (
-        gnorm, hid, nrm, qsave, kv, kt, vt, att, osave, lse, upd, nrm2, gp, act, emb, qmask,
-        domask, ps, ds, dqkv, grad_low, peak, total, gbuf, gemb, gin, merge,
-        send_n, recv_n, send_g, recv_g, recv_m, gathered, flat,
-    ) = (ref[n] for n in LOCAL)
-    rin, rit, rbias, norms, bup = (ref[n] for n in ("rin", "rit", "rbias", "norms", "bup"))
-    wqkv, wqkv_t, wo, wo_t = (ref[n] for n in ("wqkv", "wqkv_t", "wo", "wo_t"))
-    wup, wup_t, wd, wd_t = (ref[n] for n in ("wup", "wup_t", "wd", "wd_t"))
+    gnorm, hid, nrm, qsave, kv, kt, vt, att = (
+        ref.gnorm, ref.hid, ref.nrm, ref.qsave, ref.kv, ref.kt, ref.vt, ref.att,
+    )
+    osave, lse, upd, nrm2, gp, act, emb, qmask = (
+        ref.osave, ref.lse, ref.upd, ref.nrm2, ref.gp, ref.act, ref.emb, ref.qmask,
+    )
+    domask, ps, ds, dqkv, grad_low, peak, total, gbuf = (
+        ref.domask, ref.ps, ref.ds, ref.dqkv, ref.grad_low, ref.peak, ref.total, ref.gbuf,
+    )
+    gemb, gin, merge, send_n, recv_n, send_g, recv_g, recv_m = (
+        ref.gemb, ref.gin, ref.merge, ref.send_n, ref.recv_n, ref.send_g, ref.recv_g, ref.recv_m,
+    )
+    gathered, flat = (
+        ref.gathered, ref.flat,
+    )
+    rin, rit, rbias, norms, bup = ref.rin, ref.rit, ref.rbias, ref.norms, ref.bup
+    wqkv, wqkv_t, wo, wo_t = ref.wqkv, ref.wqkv_t, ref.wo, ref.wo_t
+    wup, wup_t, wd, wd_t = ref.wup, ref.wup_t, ref.wd, ref.wd_t
 
     me = lax.axis_index("seq")
     owner = lax.axis_index("dp")
@@ -179,7 +190,7 @@
     depth_mask = lax.broadcasted_iota(jnp.int32, (plan.depth, rows), 0) < counts[0]
     gin[...] = jnp.zeros_like(gin)
     gin[: plan.depth] = jnp.where(depth_mask, points[...].astype(F32), 0.0)
-    masked_all = ref["masked_all"]
+    masked_all = ref.masked_all
     masked_all[me] = gin[:128].astype(BF16)
 
     pl.semaphore_wait(barrier, plan.seq + zs)
@@ -187,7 +198,7 @@
     def points_copy(source, target):
         piece = masked_all.at[source]
         return remote(
-            piece, piece, ref["send_p"].at[target], ref["recv_p"].at[source], {"seq": target}
+            piece, piece, ref.send_p.at[target], ref.recv_p.at[source], {"seq": target}
         )
 
     for step in range(1, SEQ):
@@ -199,7 +210,7 @@
     def weights_z(source_z, target_z, w):
         piece = gathered.at[2 * source_z + my_x, my_c, my_y, w]
         return remote(
-            piece, piece, ref["send_wz"].at[target_z, w], ref["recv_wz"].at[source_z, w],
+            piece, piece, ref.send_wz.at[target_z, w], ref.recv_wz.at[source_z, w],
             {"dp": 2 * target_z + my_x},
         )
 
@@ -207,7 +218,7 @@
         piece = gathered.at[2 * group + my_x, my_c, my_y, w]
         _, _, device = in_plane(step)
         return remote(
-            piece, piece, ref["send_wp"].at[group, step, w], ref["recv_wp"].at[group, here, w],
+            piece, piece, ref.send_wp.at[group, step, w], ref.recv_wp.at[group, here, w],
             device,
         )
 
@@ -215,14 +226,14 @@
         x, y, device = in_plane(step)
         piece = gathered.at[2 * group + x, my_c, y, w]
         return remote(
-            piece, piece, ref["send_wp"].at[group, step, w],
-            ref["recv_wp"].at[group, x * 2 + y, w], device,
+            piece, piece, ref.send_wp.at[group, step, w],
+            ref.recv_wp.at[group, x * 2 + y, w], device,
         )
 
     def weights_core(share, column, w):
         piece = gathered.at[share, column, :, w]
         return remote(
-            piece, piece, ref["send_wc"].at[share, w], ref["recv_wc"].at[share, w], sibling
+            piece, piece, ref.send_wc.at[share, w], ref.recv_wc.at[share, w], sibling
         )
 
     def send_near():
@@ -317,25 +328,15 @@
     reach_c, reach_d = plan.reach[1, "mixer"], plan.reach[1, "hidden"]
 
     def first_groups(group):
-        @pl.when(group == my_z)
-        def _():
-            send_up()
-
         @pl.when(group != my_z)
         def _():
             forward_group(group)
 
     send_near()
+    send_up()
     each(0, reach_a, first_groups)
 
-    @pl.when(my_z >= reach_a)
-    def _():
-        send_up()
-
-    @pl.when(my_z < reach_a)
-    def _():
-        each(reach_a, reach_b, forward_group)
-
+    each_other_z(reach_a, reach_b, forward_group)
     qmask[...] = jnp.zeros_like(qmask)
     domask[...] = jnp.zeros_like(domask)
     gnorm[...] = jnp.zeros_like(gnorm)
@@ -343,10 +344,6 @@
     ones = jnp.ones((16, rows), BF16)
     gbuf[...] = jnp.transpose(cot[...].astype(F32))
     each(0, reach_a, pass_group)
-
-    @pl.when(my_z >= reach_a)
-    def _():
-        each_other_z(reach_a, reach_b, forward_group)
 
     each(0, reach_a, take_group)
     unpack(0, reach_a)
@@ -378,6 +375,11 @@
             {"seq": target},
         )
 
+    def near_copy(app, target):
+        return remote(
+            merge.at[app], nrm.at[app, me], send_g.at[app, 0], recv_g.at[app, me], {"seq": target}
+        )
+
     def grad_arrival(app, source):
         return remote(
             nrm.at[app, source], nrm.at[app, source], send_g.at[app, 0], recv_g.at[app, source],
@@ -411,19 +413,34 @@
             jnp.transpose(block_t.astype(F32)).astype(BF16), wqkv[layer, :, width:]
         ).astype(BF16)
 
-    def attend(app, blocks):
-        keys = blocks * rows
+    far_peak, far_total = ref.far_peak, ref.far_total
+
+    def soften(app, keys, tops, sums, diagonal):
         for head in range(HEADS):
-            scores = mm(kv[app, :keys, :width], qmask[head]) * exp_scale
-            scores = mask_last(scores, -jnp.inf)
+            scores = mm(kv[app, keys, :width], qmask[head]) * exp_scale
+            if diagonal:
+                scores = mask_last(scores, -jnp.inf)
             top = jnp.max(scores, axis=0, keepdims=True)
             weight = jnp.exp2(scores - top)
-            peak[head : head + 1] = top
-            total[head : head + 1] = jnp.sum(weight, axis=0, keepdims=True)
-            ps[head, :keys] = weight.astype(BF16)
+            tops[head : head + 1] = top
+            sums[head : head + 1] = jnp.sum(weight, axis=0, keepdims=True)
+            ps[head, keys] = weight.astype(BF16)
+
+    def mix(head, keys):
+        lanes = slice(head * head_width, (head + 1) * head_width)
+        return lanes, mm(vt[lanes, keys], ps[head, keys])
+
+    def finish_heads(app, keys, far):
         for head in range(HEADS):
-            lanes = slice(head * head_width, (head + 1) * head_width)
-            out = mm(vt[lanes, :keys], ps[head, :keys]) * (1.0 / total[head : head + 1])
+            lanes, out = mix(head, keys)
+            row = slice(head, head + 1)
+            if far:
+                top = jnp.maximum(peak[row], far_peak[row])
+                fade, far_fade = jnp.exp2(peak[row] - top), jnp.exp2(far_peak[row] - top)
+                out = hid[app + 1, lanes] * fade + out * far_fade
+                peak[row] = top
+                total[row] = total[row] * fade + far_total[row] * far_fade
+            out = out * (1.0 / total[row])
             osave[app, lanes] = out
             att[app, lanes] = out.astype(BF16)
         lse[app] = peak[...] + jnp.log2(total[...])
@@ -448,13 +465,22 @@
                 normed_copy(app, place - 1, me, 0).wait_recv()
 
             project_block(app, layer, place - 1)
-        if place >= 2:
-
-            @pl.when(app > 0)
-            def _():
-                normed_copy(app, near, me, 0).wait_recv()
-                normed_copy(app, near, place + 1 - 2 * (place % 2), 2).start()
-
+
+        def pass_near():
+            normed_copy(app, near, me, 0).wait_recv()
+            normed_copy(app, near, place + 1 - 2 * (place % 2), 2).start()
+
+        keys = slice(place // 2 * 2 * rows, (place + 1) * rows)
+        if place < 2:
+            soften(app, keys, peak, total, True)
+            finish_heads(app, keys, False)
+        else:
+            pl.when(app > 1)(pass_near)
+            soften(app, keys, peak, total, True)
+            for head in range(HEADS):
+                lanes, out = mix(head, keys)
+                hid[app + 1, lanes] = out
+            pl.when(app == 1)(pass_near)
             project_block(app, layer, near)
 
             @pl.when(app > 0)
@@ -462,6 +488,9 @@
                 normed_copy(app, far, me, 0).wait_recv()
 
             project_block(app, layer, far)
+            far_keys = slice(0, 2 * rows)
+            soften(app, far_keys, far_peak, far_total, False)
+            finish_heads(app, far_keys, True)
 
     def forward(app, carry):
         layer = lax.rem(app, LAYERS)
@@ -496,7 +525,6 @@
             @pl.when(me == place)
             def _(place=place):
                 gather_blocks(app, layer, place)
-                attend(app, place + 1)
 
         updated = hid[app] + mm(wo_t[layer], att[app])
         upd[app] = updated
@@ -520,12 +548,11 @@
 
         before = mm(wup_t[layer], nrm2[app]) + twice(bup[layer])
         squared = before * before
-        inner = GELU_A * before * (1.0 + GELU_B * squared)
-        turned = jnp.tanh(inner)
+        turned = jnp.tanh(before * (GELU_A + (GELU_A * GELU_B) * squared))
         risen = 0.5 * (1.0 + turned)
         act[app] = (before * risen).astype(BF16)
-        gp[app] = risen + (0.5 * GELU_A) * before * (1.0 - turned * turned) * (
-            1.0 + (3.0 * GELU_B) * squared
+        gp[app] = risen + before * (1.0 - turned * turned) * (
+            0.5 * GELU_A + (1.5 * GELU_A * GELU_B) * squared
         )
         result = upd[app] + mm(wd_t[layer], act[app])
         again = jnp.where((layer == LAYERS - 1) & (app < APPS - 1), 1.0, 0.0)
@@ -567,21 +594,21 @@
         (2, plan.total - plan.used, 128), F32
     )
 
-    from_core, from_plane, from_z = (ref[n] for n in ("from_core", "from_plane", "from_z"))
-    last, summed = ref["last"], ref["summed"]
+    from_core, from_plane, from_z = ref.from_core, ref.from_plane, ref.from_z
+    last, summed = ref.last, ref.summed
 
     def grads_core(group, w):
         pair = pl.ds(2 * group, 2)
         return remote(
             gathered.at[pair, 1 - my_c, :, w], from_core.at[pair, :, w],
-            ref["send_gc"].at[group, w], ref["recv_gc"].at[group, w], sibling,
+            ref.send_gc.at[group, w], ref.recv_gc.at[group, w], sibling,
         )
 
     def grads_plane(group, step, w):
         x, y, device = in_plane(step)
         return remote(
             gathered.at[2 * group + x, my_c, y, w], from_plane.at[group, here, w],
-            ref["send_gp"].at[group, step, w], ref["recv_gp"].at[group, here, w], device,
+            ref.send_gp.at[group, step, w], ref.recv_gp.at[group, here, w], device,
         )
 
     def grads_plane_in(group, step, w):
@@ -589,13 +616,13 @@
         place = x * 2 + y
         return place, remote(
             gathered.at[2 * group + my_x, my_c, my_y, w], from_plane.at[group, place, w],
-            ref["send_gp"].at[group, step, w], ref["recv_gp"].at[group, place, w], device,
+            ref.send_gp.at[group, step, w], ref.recv_gp.at[group, place, w], device,
         )
 
     def grads_z(source_z, target_z, w):
         return remote(
             gathered.at[2 * target_z + my_x, my_c, my_y, w], from_z.at[source_z, w],
-            ref["send_gz"].at[target_z, w], ref["recv_gz"].at[source_z, w],
+            ref.send_gz.at[target_z, w], ref.recv_gz.at[source_z, w],
             {"dp": 2 * target_z + my_x},
         )
 
@@ -648,10 +675,54 @@
 
         each(low, high, body)
 
+    first_low, first_from, first_places, first_rise, first_levels, first_sum = (
+        ref.first_low, ref.first_from, ref.first_places, ref.first_rise, ref.first_levels, ref.first_sum,
+    )
+
+    def first_core():
+        return remote(
+            first_low.at[1 - my_c], first_from, ref.send_f.at[0], ref.recv_fc.at[0], sibling
+        )
+
+    def first_plane(step):
+        _, _, device = in_plane(step)
+        return remote(
+            first_low.at[my_c], first_places.at[here],
+            ref.send_f.at[step], ref.recv_fp.at[here], device,
+        )
+
+    def first_plane_in(step):
+        x, y, device = in_plane(step)
+        place = x * 2 + y
+        return place, remote(
+            first_low.at[my_c], first_places.at[place],
+            ref.send_f.at[step], ref.recv_fp.at[place], device,
+        )
+
+    def first_z(b, source):
+        return remote(
+            first_rise.at[b], first_levels.at[source], ref.send_f.at[5 + b],
+            ref.recv_fz.at[source], {"dp": 2 * plan.late[b][0] + my_x},
+        )
+
+    def first_share(column):
+        piece = first_sum.at[column]
+        return remote(piece, piece, ref.send_f.at[4], ref.recv_fs.at[0], sibling)
+
+    def to_first_x(body):
+        @pl.when(my_x == 0)
+        def _():
+            body(1)
+
+        @pl.when(my_x == 1)
+        def _():
+            body(2)
+            body(3)
+
     def share_sum(kind, w, column, half, device):
         piece = summed.at[column, half, w]
         return remote(
-            piece, piece, ref["send_gs"].at[kind, w], ref["recv_gs"].at[kind, w], device
+            piece, piece, ref.send_gs.at[kind, w], ref.recv_gs.at[kind, w], device
         )
 
     def collect(low, high):
@@ -676,7 +747,7 @@
 
     group_a = first_group(plan.base(1) + plan.mixer)
     group_b = first_group(plan.base(0) + plan.mixer)
-    group_m = (group_a + group_b + 1) // 2
+    group_e = plan.settled
 
     def accumulate(app, layer, offset, stride, value, again=False):
         start = plan.base(0) + layer * plan.block + offset
@@ -747,10 +818,9 @@
             grad_copy(app, kept, kept, 2).start()
         heads_back(app, span_of(start, place + 1), span_of(place, place + 1), bool(start))
         if place % 2:
-            back = normed_back(layer, width, place - 1).astype(BF16)
+            merge[app] = normed_back(layer, width, place - 1).astype(BF16)
+            near_copy(app, place - 1).start()
             weights_back(app, layer, width, place - 1, bool(start))
-            nrm[app, place - 1] = back
-            grad_copy(app, place - 1, place - 1, 0).start()
         gin[...] = normed_back(layer, 0, place)
         weights_back(app, layer, 0, place, bool(start) or place % 2 == 1)
 
@@ -765,6 +835,11 @@
     def backward(order, carry):
         app = APPS - 1 - order
         layer = lax.rem(app, LAYERS)
+
+        @pl.when(app == 0)
+        def _():
+            plane_group(group_e, group_a)
+
         out_low = gbuf[...].astype(BF16)
         accumulate(app, layer, plan.mixer + hidden + parts, 1, mm_nt(act[app], out_low))
         pre_low = (mm(wd[layer], out_low) * gp[app]).astype(BF16)
@@ -780,8 +855,7 @@
 
         @pl.when(app == 0)
         def _():
-            rise_group(group_a, zs)
-            round_group(group_b, group_a)
+            round_group(group_b, group_e)
 
         grad_second = mm(wup[layer], act[app])
         unit, scale = normalise(upd[app])
@@ -807,7 +881,7 @@
 
         @pl.when(app == 0)
         def _():
-            plane_group(group_m, group_a)
+            plane_group(group_b, group_e)
 
         for place in range(SEQ):
 
@@ -817,7 +891,10 @@
 
         @pl.when(app == 0)
         def _():
-            plane_group(group_b, group_m)
+            round_group(0, group_b)
+            rise_group(group_e, group_a)
+            plane_group(0, group_b)
+            rise_group(group_b, group_e)
 
         def arrive(source):
             grad_arrival(app, source).wait_recv()
@@ -844,6 +921,11 @@
         def _():
             flush_norms(layer)
 
+        @pl.when(app == 1)
+        def _():
+            round_group(group_e, group_a)
+            rise_group(group_a, zs)
+
         return carry
 
     lax.fori_loop(0, APPS, backward, 0)
@@ -854,13 +936,40 @@
         lanes = slice(128 * h, 128 * (h + 1))
         flat[h, : plan.depth] = grad_in_rows[: plan.depth, lanes]
         flat[h, plan.depth : plan.depth + 1] = grad_bias_rows[:1, lanes]
-    round_group(0, group_b)
+    for b, (group, _) in enumerate(plan.late):
+        for h in range(2):
+            first_low[h, b] = flat[h, pl.ds(2 * group * plan.flat, FIRST), :].astype(BF16)
+    first_core().start()
     point_grad[...] = jnp.where(depth_mask, mm(rin[...], embed_low)[: plan.depth], 0.0)
-    rise_group(group_m, group_a)
-    plane_group(0, group_b)
-    rise_group(group_b, group_m)
+    first_core().wait()
+    first_low[my_c] = (first_low[my_c].astype(F32) + first_from[...].astype(F32)).astype(BF16)
+    to_first_x(lambda step: first_plane(step).start())
     rise_group(0, group_b)
+
+    @pl.when(my_x == 0)
+    def _():
+        first_places[here] = first_low[my_c]
+        for step in (1, 2, 3):
+            place, arrival = first_plane_in(step)
+            arrival.wait_recv()
+        first_rise[...] = sum(first_places[place].astype(F32) for place in range(4)).astype(BF16)
+
+        for b, (group, _) in enumerate(plan.late):
+
+            @pl.when(my_z != group)
+            def _(b=b):
+                first_z(b, my_z).start()
+
     collect(0, zs)
+    for b, (group, _) in enumerate(plan.late):
+
+        @pl.when(owner == 2 * group)
+        def _(b=b):
+            first_levels[my_z] = first_rise[b]
+            each_other_z(0, zs, lambda z: first_z(b, z).wait_recv())
+            first_sum[my_c] = sum(first_levels[z].astype(F32) for z in range(zs)).astype(BF16)
+            first_share(my_c).start()
+
     for w in waves:
         share_sum(1, w, my_c, 1 - my_y, across).wait_recv()
         share_sum(2, w, my_c, 1 - my_y, sibling).start()
@@ -875,7 +984,27 @@
                 flat[0, pl.ds(2 * start + h, count, stride=2), :] = summed[h, r, w].astype(F32)[
                     :count
                 ]
+    for group, count in plan.late:
+
+        @pl.when(owner == 2 * group)
+        def _(count=count):
+            first_share(1 - my_c).wait_recv()
+            for h in range(2):
+                flat[0, pl.ds(h, count, stride=2), :] = first_sum[h].astype(F32)[:count]
+
     gradients[...] = flat[0, : gradients.shape[0]].astype(BF16)
+
+    to_first_x(lambda step: first_plane(step).wait_send())
+
+    for b, (group, _) in enumerate(plan.late):
+
+        @pl.when((my_x == 0) & (my_z != group))
+        def _(b=b):
+            first_z(b, my_z).wait_send()
+
+        @pl.when(owner == 2 * group)
+        def _():
+            first_share(my_c).wait_send()
 
     for w in waves:
         for step in (1, 2, 3):
@@ -888,7 +1017,7 @@
     def finish(app):
         @pl.when(my_c == 1)
         def _():
-            grad_copy(app, me - 1, me - 1, 0).wait_send()
+            near_copy(app, me - 1).wait_send()
 
         @pl.when(my_y == 1)
         def _():
@@ -931,83 +1060,93 @@
     low = lambda *dims: pltpu.VMEM(dims, BF16)
     full = lambda *dims: pltpu.VMEM(dims, F32)
     flags = lambda *dims: pltpu.SemaphoreType.DMA(dims)
-    scratch = {
-        "gathered": low(dp_count, 2, 2, 2, quarter, 128),
-        "flat": full(2, plan.space, 128),
-        "rin": low(128, width),
-        "rit": low(width, 128),
-        "rbias": full(width, 128),
-        "norms": low(LAYERS, 4, width, 128),
-        "bup": low(LAYERS, hidden, 128),
-        "wqkv": low(LAYERS, width, 3 * width),
-        "wqkv_t": low(LAYERS, 3 * width, width),
-        "wo": low(LAYERS, width, width),
-        "wo_t": low(LAYERS, width, width),
-        "wup": low(LAYERS, width, hidden),
-        "wup_t": low(LAYERS, hidden, width),
-        "wd": low(LAYERS, hidden, width),
-        "wd_t": low(LAYERS, width, hidden),
-        "masked_all": low(SEQ, 128, rows),
-        "gnorm": full(LAYERS, 4, width, 128),
-        "from_core": low(dp_count, 2, 2, quarter, 128),
-        "from_plane": low(zs, 4, 2, quarter, 128),
-        "from_z": low(zs, 2, quarter, 128),
-        "last": full(2, quarter, 128),
-        "summed": low(2, 2, 2, quarter, 128),
-        "hid": full(APPS + 1, width, rows),
-        "nrm": low(APPS, SEQ, width, rows),
-        "qsave": low(APPS, width, rows),
-        "kv": low(APPS, SEQ * rows, 2 * width),
-        "kt": low(APPS, width, SEQ * rows),
-        "vt": low(width, SEQ * rows),
-        "att": low(APPS, width, rows),
-        "osave": full(APPS, width, rows),
-        "lse": full(APPS, HEADS, rows),
-        "upd": full(APPS, width, rows),
-        "nrm2": low(APPS, width, rows),
-        "gp": full(APPS, hidden, rows),
-        "act": low(APPS, hidden, rows),
-        "emb": full(width, rows),
-        "qmask": low(HEADS, width, rows),
-        "domask": low(HEADS, width, rows),
-        "ps": low(HEADS, SEQ * rows, rows),
-        "ds": low(HEADS, SEQ * rows, rows),
-        "dqkv": low(3 * width, SEQ * rows),
-        "grad_low": low(width, rows),
-        "peak": full(HEADS, rows),
-        "total": full(HEADS, rows),
-        "gbuf": full(width, rows),
-        "gemb": full(width, rows),
-        "gin": full(width, rows),
-        "merge": low(APPS, width, rows),
-        "send_n": flags(APPS, 3),
-        "recv_n": flags(APPS, SEQ),
-        "send_g": flags(APPS, 3),
-        "recv_g": flags(APPS, SEQ),
-        "recv_m": flags(APPS),
-        "send_p": flags(SEQ),
-        "recv_p": flags(SEQ),
-        "send_wz": flags(zs, 2),
-        "recv_wz": flags(zs, 2),
-        "send_wp": flags(zs, 4, 2),
-        "recv_wp": flags(zs, 4, 2),
-        "send_wc": flags(dp_count, 2),
-        "recv_wc": flags(dp_count, 2),
-        "send_gc": flags(zs, 2),
-        "recv_gc": flags(zs, 2),
-        "send_gp": flags(zs, 4, 2),
-        "recv_gp": flags(zs, 4, 2),
-        "send_gz": flags(zs, 2),
-        "recv_gz": flags(zs, 2),
-        "send_gs": flags(3, 2),
-        "recv_gs": flags(3, 2),
-    }
-    names = (
-        "points", "counts", "cot", "weights", "states", "point_grad", "gradients", *scratch,
+    scratch = dict(
+        gathered=low(dp_count, 2, 2, 2, quarter, 128),
+        flat=full(2, plan.space, 128),
+        rin=low(128, width),
+        rit=low(width, 128),
+        rbias=full(width, 128),
+        norms=low(LAYERS, 4, width, 128),
+        bup=low(LAYERS, hidden, 128),
+        wqkv=low(LAYERS, width, 3 * width),
+        wqkv_t=low(LAYERS, 3 * width, width),
+        wo=low(LAYERS, width, width),
+        wo_t=low(LAYERS, width, width),
+        wup=low(LAYERS, width, hidden),
+        wup_t=low(LAYERS, hidden, width),
+        wd=low(LAYERS, hidden, width),
+        wd_t=low(LAYERS, width, hidden),
+        masked_all=low(SEQ, 128, rows),
+        gnorm=full(LAYERS, 4, width, 128),
+        from_core=low(dp_count, 2, 2, quarter, 128),
+        from_plane=low(zs, 4, 2, quarter, 128),
+        from_z=low(zs, 2, quarter, 128),
+        last=full(2, quarter, 128),
+        first_low=low(2, len(plan.late), FIRST, 128),
+        first_from=low(len(plan.late), FIRST, 128),
+        first_places=low(4, len(plan.late), FIRST, 128),
+        first_rise=low(len(plan.late), FIRST, 128),
+        first_levels=low(zs, FIRST, 128),
+        first_sum=low(2, FIRST, 128),
+        send_f=flags(5 + len(plan.late)),
+        recv_fc=flags(1),
+        recv_fp=flags(4),
+        recv_fz=flags(zs),
+        recv_fs=flags(1),
+        summed=low(2, 2, 2, quarter, 128),
+        hid=full(APPS + 1, width, rows),
+        nrm=low(APPS, SEQ, width, rows),
+        qsave=low(APPS, width, rows),
+        kv=low(APPS, SEQ * rows, 2 * width),
+        kt=low(APPS, width, SEQ * rows),
+        vt=low(width, SEQ * rows),
+        att=low(APPS, width, rows),
+        osave=full(APPS, width, rows),
+        lse=full(APPS, HEADS, rows),
+        upd=full(APPS, width, rows),
+        nrm2=low(APPS, width, rows),
+        gp=full(APPS, hidden, rows),
+        act=low(APPS, hidden, rows),
+        emb=full(width, rows),
+        qmask=low(HEADS, width, rows),
+        domask=low(HEADS, width, rows),
+        ps=low(HEADS, SEQ * rows, rows),
+        ds=low(HEADS, SEQ * rows, rows),
+        dqkv=low(3 * width, SEQ * rows),
+        grad_low=low(width, rows),
+        peak=full(HEADS, rows),
+        total=full(HEADS, rows),
+        far_peak=full(HEADS, rows),
+        far_total=full(HEADS, rows),
+        gbuf=full(width, rows),
+        gemb=full(width, rows),
+        gin=full(width, rows),
+        merge=low(APPS, width, rows),
+        send_n=flags(APPS, 3),
+        recv_n=flags(APPS, SEQ),
+        send_g=flags(APPS, 3),
+        recv_g=flags(APPS, SEQ),
+        recv_m=flags(APPS),
+        send_p=flags(SEQ),
+        recv_p=flags(SEQ),
+        send_wz=flags(zs, 2),
+        recv_wz=flags(zs, 2),
+        send_wp=flags(zs, 4, 2),
+        recv_wp=flags(zs, 4, 2),
+        send_wc=flags(dp_count, 2),
+        recv_wc=flags(dp_count, 2),
+        send_gc=flags(zs, 2),
+        recv_gc=flags(zs, 2),
+        send_gp=flags(zs, 4, 2),
+        recv_gp=flags(zs, 4, 2),
+        send_gz=flags(zs, 2),
+        recv_gz=flags(zs, 2),
+        send_gs=flags(3, 2),
+        recv_gs=flags(3, 2),
     )
     mine = weights.reshape(lines)
     states, point_grad, summed = pl.pallas_call(
-        functools.partial(whole_kernel, plan, names),
+        functools.partial(whole_kernel, plan, tuple(scratch)),
         out_shape=outs,
         in_specs=[vmem, smem, vmem, vmem],
         out_specs=(vmem,) * len(outs),
@@ -1017,7 +1156,7 @@
         ),
     )(points[0].T, counts, cotangent[0], mine)
     vector = shape(lines, F32)
-    step_rows = min(512, lines[0])
+    step_rows = min(776, lines[0])
     line_block = pl.BlockSpec((step_rows, 128), lambda i: (i, 0))
     states_block = pl.BlockSpec((rows, width), lambda i: (0, 0))
     point_block = pl.BlockSpec((depth, rows), lambda i: (0, 0))

time: 128 us -> 122 us (0.953)
  Pallas kernels: 126 us -> 120 us
    pallas_call x1, Pallas kernels: 122 us -> 116 us  [shards(): pl.pallas_call(functools.partial(whole_kernel, plan, tuple(scratch)), out...]
where the time goes in v6:
time: 122 us; the launch traced here: 121 us
  Pallas kernels  120 us (98%)
  between operations  1.45 us (1%)
    pallas_call x1, Pallas kernels, shards(): pl.pallas_call(functools.partial(whole_kernel, plan, tuple(scratch)), out...  116 us
    pallas_call x1, Pallas kernels, shards(): pl.pallas_call(update_kernel, grid=(-(-lines[0] // step_rows),), out_shap...  3.46 us

profile of v6, /device:TPU:0, one launch (start us, length us, event | category | flops | bytes accessed | tf_op | source)
XLA Modules:
  0.0 121.1 jit_solution(3721005669252922672)
XLA Ops:
  1.3 116.2 %shard_map.109 = (bf16[256,256]{1,0:T(8,128)(2,1)}, f32[20,256]{1,0:T(8,128)}, bf16[1548,128]{1,0:T(8,128)(2,1)}) custom-call(bf16[20,256]{1,0:T(8,128)(2,1)} %bitcast.18, s32[1]{0:T(128)S(6)} %copy.12.refs_1_, bf16[256,256]{1,0:T(8,128)(2,1)} %bitcast.17, f32[1548,128]{1,0:T(8,128)} %bitcast.13), custom_call_target="tpu_custom_call" | custom-call | tf_op jit(solution)/shard_map/pallas_call | solution.py:1148
  117.5 3.5 %shard_map.110 = (f32[1548,128]{1,0:T(8,128)}, f32[1548,128]{1,0:T(8,128)}, f32[1548,128]{1,0:T(8,128)}, f32[1548,128]{1,0:T(8,128)}, bf16[256,256]{1,0:T(8,128)(2,1)}, /*index=5*/f32[20,1,256]{2,1,0:T(1,128)}) custom-call(bf16[1548,128]{1,0:T(8,128)(2,1)} %get-tuple-element.15.summed, f32[1548,128]{1,0:T(8,128)} %bitcast.14, f32[1548,128]{1,0:T(8,128)} %bitcast.15, ...), custom_call_target="tpu_custom_call" | custom-call | tf_op jit(solution)/shard_map/pallas_call | solution.py:1163

commit v7 on v6

--- a/solution.py
+++ b/solution.py
@@ -84,8 +84,8 @@
         self.reach[LAYERS - 1, "hidden"] = self.zs
         self.late = [(0, self.base(0) + 4)]
         group, spill = divmod(self.base(1), 2 * self.flat)
-        if group and 0 < spill <= FIRST:
-            self.late.append((group, spill))
+        if group and 0 < spill <= FIRST - 4:
+            self.late.append((group, spill + 4))
             self.settled = group
         else:
             self.settled = min(self.zs, -(-self.base(1) // (2 * self.flat)))
@@ -836,7 +836,7 @@
         app = APPS - 1 - order
         layer = lax.rem(app, LAYERS)
 
-        @pl.when(app == 0)
+        @pl.when((app == 0) & (my_y == 1))
         def _():
             plane_group(group_e, group_a)
 
@@ -881,6 +881,7 @@
 
         @pl.when(app == 0)
         def _():
+            rise_group(group_a, zs)
             plane_group(group_b, group_e)
 
         for place in range(SEQ):
@@ -895,6 +896,14 @@
             rise_group(group_e, group_a)
             plane_group(0, group_b)
             rise_group(group_b, group_e)
+
+        @pl.when(app == 1)
+        def _():
+            round_group(group_e, group_a)
+
+        @pl.when((app == 1) & (my_y == 0))
+        def _():
+            plane_group(group_e, group_a)
 
         def arrive(source):
             grad_arrival(app, source).wait_recv()
@@ -920,11 +929,6 @@
         @pl.when(app < LAYERS)
         def _():
             flush_norms(layer)
-
-        @pl.when(app == 1)
-        def _():
-            round_group(group_e, group_a)
-            rise_group(group_a, zs)
 
         return carry
 

time: 122 us -> 121 us (level)
  Pallas kernels: 120 us -> 118 us
    pallas_call x1, Pallas kernels: 116 us -> 115 us  [shards(): pl.pallas_call(functools.partial(whole_kernel, plan, tuple(scratch)), out...]
where the time goes in v7:
time: 121 us; the launch traced here: 120 us
  Pallas kernels  118 us (98%)
  between operations  1.45 us (1%)
    pallas_call x1, Pallas kernels, shards(): pl.pallas_call(functools.partial(whole_kernel, plan, tuple(scratch)), out...  115 us
    pallas_call x1, Pallas kernels, shards(): pl.pallas_call(update_kernel, grid=(-(-lines[0] // step_rows),), out_shap...  3.46 us

profile of v7, /device:TPU:0, one launch (start us, length us, event | category | flops | bytes accessed | tf_op | source)
XLA Modules:
  0.0 119.7 jit_solution(12571277194280501366)
XLA Ops:
  1.3 114.8 %shard_map.109 = (bf16[256,256]{1,0:T(8,128)(2,1)}, f32[20,256]{1,0:T(8,128)}, bf16[1548,128]{1,0:T(8,128)(2,1)}) custom-call(bf16[20,256]{1,0:T(8,128)(2,1)} %bitcast.18, s32[1]{0:T(128)S(6)} %copy.12.refs_1_, bf16[256,256]{1,0:T(8,128)(2,1)} %bitcast.17, f32[1548,128]{1,0:T(8,128)} %bitcast.13), custom_call_target="tpu_custom_call" | custom-call | tf_op jit(solution)/shard_map/pallas_call | solution.py:1152
  116.1 3.5 %shard_map.110 = (f32[1548,128]{1,0:T(8,128)}, f32[1548,128]{1,0:T(8,128)}, f32[1548,128]{1,0:T(8,128)}, f32[1548,128]{1,0:T(8,128)}, bf16[256,256]{1,0:T(8,128)(2,1)}, /*index=5*/f32[20,1,256]{2,1,0:T(1,128)}) custom-call(bf16[1548,128]{1,0:T(8,128)(2,1)} %get-tuple-element.15.summed, f32[1548,128]{1,0:T(8,128)} %bitcast.14, f32[1548,128]{1,0:T(8,128)} %bitcast.15, ...), custom_call_target="tpu_custom_call" | custom-call | tf_op jit(solution)/shard_map/pallas_call | solution.py:1167

commit v8 on v7

--- a/solution.py
+++ b/solution.py
@@ -893,8 +893,8 @@
         @pl.when(app == 0)
         def _():
             round_group(0, group_b)
+            plane_group(0, group_b)
             rise_group(group_e, group_a)
-            plane_group(0, group_b)
             rise_group(group_b, group_e)
 
         @pl.when(app == 1)

time: 121 us -> 121 us (level)
  no operation moved by 1% of the time
where the time goes in v8:
time: 121 us; the launch traced here: 120 us
  Pallas kernels  119 us (98%)
  between operations  1.45 us (1%)
    pallas_call x1, Pallas kernels, shards(): pl.pallas_call(functools.partial(whole_kernel, plan, tuple(scratch)), out...  115 us
    pallas_call x1, Pallas kernels, shards(): pl.pallas_call(update_kernel, grid=(-(-lines[0] // step_rows),), out_shap...  3.46 us

profile of v8, /device:TPU:0, one launch (start us, length us, event | category | flops | bytes accessed | tf_op | source)
XLA Modules:
  0.0 120.0 jit_solution(1392302945563881052)
XLA Ops:
  1.3 115.1 %shard_map.109 = (bf16[256,256]{1,0:T(8,128)(2,1)}, f32[20,256]{1,0:T(8,128)}, bf16[1548,128]{1,0:T(8,128)(2,1)}) custom-call(bf16[20,256]{1,0:T(8,128)(2,1)} %bitcast.18, s32[1]{0:T(128)S(6)} %copy.12.refs_1_, bf16[256,256]{1,0:T(8,128)(2,1)} %bitcast.17, f32[1548,128]{1,0:T(8,128)} %bitcast.13), custom_call_target="tpu_custom_call" | custom-call | tf_op jit(solution)/shard_map/pallas_call | solution.py:1152
  116.4 3.5 %shard_map.110 = (f32[1548,128]{1,0:T(8,128)}, f32[1548,128]{1,0:T(8,128)}, f32[1548,128]{1,0:T(8,128)}, f32[1548,128]{1,0:T(8,128)}, bf16[256,256]{1,0:T(8,128)(2,1)}, /*index=5*/f32[20,1,256]{2,1,0:T(1,128)}) custom-call(bf16[1548,128]{1,0:T(8,128)(2,1)} %get-tuple-element.15.summed, f32[1548,128]{1,0:T(8,128)} %bitcast.14, f32[1548,128]{1,0:T(8,128)} %bitcast.15, ...), custom_call_target="tpu_custom_call" | custom-call | tf_op jit(solution)/shard_map/pallas_call | solution.py:1167
